TPU v7x, 128 devices: a whole 4x4x4 slice. The times are simulated.
128 devices in a mesh: rep: 4 (over y_lo, core), sp: 32 (over x, y_hi, z).
Axes of the slice: x: 4, y: 4 (y_hi: 2, y_lo: 2; y = y_hi * 2 + y_lo), z: 4, core: 2. Of those that a mesh axis runs over, the one named last changes fastest.
Arguments:
- field: bfloat16 [4, 2, 36, 256, 1024], P('rep', None, None, 'sp'), may hold values from -6 to 6
- cotangent: bfloat16 [4, 2, 36, 256, 1024], P('rep', None, None, 'sp'), may hold values from -6 to 6
- spec_weight: float32 [2, 36, 36, 288], P(None, None, None, 'sp'), may hold values from -24 to 24
- point_weight: bfloat16 [36, 36], replicated, may hold values from -1 to 1
- kernel_one: bfloat16 [3, 3, 36, 36], replicated, may hold values from -0.3125 to 0.3125
- kernel_two: bfloat16 [3, 3, 36, 36], replicated, may hold values from -0.3125 to 0.3125
Outputs:
- output: bfloat16 [4, 2, 36, 256, 1024], P('rep', None, None, 'sp')
- field_grad: bfloat16 [4, 2, 36, 256, 1024], P('rep', None, None, 'sp')
- spec_grad: float32 [2, 36, 36, 288], P(None, None, None, 'sp')
- point_grad: float32 [36, 36], replicated
- kernel_one_grad: float32 [3, 3, 36, 36], replicated
- kernel_two_grad: float32 [3, 3, 36, 36], replicated
All inputs are finite; a program needn't handle non-finite values.
Results may differ from a plain program's by a relative error of at most 0.014.
Values may be sent and summed in bfloat16 or wider, within the bound.
No kernel may reach another device: no remote copies, remote signals or barrier semaphores. Data moves between devices by JAX's collectives and lax.ppermute only.
A program may use at most 192 MiB of HBM per device.

v0:
```python
import math

import jax
import jax.numpy as jnp
from jax import lax
from jax.sharding import PartitionSpec as P

M = 12


HIGHEST = lax.Precision.HIGHEST
ROOT_HALF = 0.7071067811865476
INV_ROOT_TAU = 0.3989422804014327


def padded_2(cells, sides, width):
    for axis, dim in sides:
        count = lax.axis_size(axis)
        ends = count - 1
        head = lax.slice_in_dim(cells, 0, width, axis=dim)
        tail = lax.slice_in_dim(cells, cells.shape[dim] - width, cells.shape[dim], axis=dim)
        cells = jnp.concatenate(
            [
                lax.ppermute(tail, axis, [(i, (i + 1) % count) for i in range(ends)]),
                cells,
                lax.ppermute(head, axis, [((i + 1) % count, i) for i in range(ends)]),
            ],
            axis=dim,
        )
    return cells


def gelu_value(values):
    return 0.5 * values * (1.0 + jax.scipy.special.erf(values * ROOT_HALF))


def gelu_slope(values):
    return (
        0.5 * (1.0 + jax.scipy.special.erf(values * ROOT_HALF))
        + values * jnp.exp(-0.5 * values * values) * INV_ROOT_TAU
    )


def column_tables(col_count, mode_count):
    column = jnp.arange(col_count, dtype=jnp.int32)[:, None]
    frequency = jnp.arange(mode_count, dtype=jnp.int32)[None, :]
    phase = (column * frequency % col_count).astype(jnp.float32) * (2.0 * math.pi / col_count)
    forward = jnp.concatenate([jnp.cos(phase), -jnp.sin(phase)], axis=1)
    doubled = jnp.where(frequency == 0, 1.0, 2.0).astype(jnp.float32)
    return (forward, jnp.concatenate([doubled, doubled], axis=1))


def row_tables(row_index, row_count, mode_count):
    slots = jnp.arange(2 * mode_count, dtype=jnp.int32)
    frequency = jnp.where(slots < mode_count, slots, row_count - 2 * mode_count + slots)
    phase = (row_index[:, None] * frequency[None, :] % row_count).astype(jnp.float32) * (
        2.0 * math.pi / row_count
    )
    return (jnp.cos(phase), jnp.sin(phase))


def column_forward(values, table_half):
    flat = jnp.dot(
        values.reshape(-1, values.shape[3]), table_half, preferred_element_type=jnp.float32
    )
    return flat.reshape(values.shape[0], values.shape[1], values.shape[2], table_half.shape[1])


def column_inverse(expanded, matrix):
    return jnp.einsum("bork,kn->born", expanded, matrix, precision=HIGHEST)


def contract_rows(operand, matrix):
    return jnp.einsum("bcrk,rj->bcjk", operand, matrix, precision=HIGHEST)


def expand_rows(spectrum, matrix):
    return jnp.einsum("bojk,rj->bork", spectrum, matrix, precision=HIGHEST)


def row_forward(columns, cosine_table, sine_table, mode_count):
    real_part = columns[..., :mode_count]
    imag_part = columns[..., mode_count:]
    spec_real = contract_rows(real_part, cosine_table) + contract_rows(imag_part, sine_table)
    spec_imag = contract_rows(imag_part, cosine_table) - contract_rows(real_part, sine_table)
    stacked = jnp.stack([spec_real, spec_imag])
    return stacked.reshape(2, stacked.shape[1], stacked.shape[2], -1)


def row_inverse(spectrum, cosine_table, sine_table, mode_count):
    grid = spectrum.reshape(2, spectrum.shape[1], spectrum.shape[2], 2 * mode_count, mode_count)
    rows_real = expand_rows(grid[0], cosine_table) - expand_rows(grid[1], sine_table)
    rows_imag = expand_rows(grid[0], sine_table) + expand_rows(grid[1], cosine_table)
    return jnp.concatenate([rows_real, rows_imag], axis=3)


def spectral_mix(spectrum, weight):
    mixed_real = jnp.einsum("bcq,coq->boq", spectrum[0], weight[0], precision=HIGHEST) - jnp.einsum(
        "bcq,coq->boq", spectrum[1], weight[1], precision=HIGHEST
    )
    mixed_imag = jnp.einsum("bcq,coq->boq", spectrum[0], weight[1], precision=HIGHEST) + jnp.einsum(
        "bcq,coq->boq", spectrum[1], weight[0], precision=HIGHEST
    )
    return jnp.stack([mixed_real, mixed_imag])


def spectral_back(cospectrum, weight):
    back_real = jnp.einsum(
        "boq,coq->bcq", cospectrum[0], weight[0], precision=HIGHEST
    ) + jnp.einsum("boq,coq->bcq", cospectrum[1], weight[1], precision=HIGHEST)
    back_imag = jnp.einsum(
        "boq,coq->bcq", cospectrum[1], weight[0], precision=HIGHEST
    ) - jnp.einsum("boq,coq->bcq", cospectrum[0], weight[1], precision=HIGHEST)
    return jnp.stack([back_real, back_imag])


def spectral_grad(spectrum, cospectrum):
    grad_real = jnp.einsum(
        "bcq,boq->coq", spectrum[0], cospectrum[0], precision=HIGHEST
    ) + jnp.einsum("bcq,boq->coq", spectrum[1], cospectrum[1], precision=HIGHEST)
    grad_imag = jnp.einsum(
        "bcq,boq->coq", spectrum[0], cospectrum[1], precision=HIGHEST
    ) - jnp.einsum("bcq,boq->coq", spectrum[1], cospectrum[0], precision=HIGHEST)
    return jnp.stack([grad_real, grad_imag])


def correlate(padded, kernel):
    return lax.conv_general_dilated(
        padded,
        kernel,
        (1, 1),
        ((0, 0), (1, 1)),
        dimension_numbers=("NCHW", "HWIO", "NCHW"),
        preferred_element_type=jnp.float32,
    )


def channel_mix(values, matrix):
    return lax.conv_general_dilated(
        values,
        matrix[None, None],
        (1, 1),
        ((0, 0), (0, 0)),
        dimension_numbers=("NCHW", "HWIO", "NCHW"),
        preferred_element_type=jnp.float32,
    )


def channel_outer(values, upstream):
    result = lax.conv_general_dilated(
        values,
        upstream,
        (1, 1),
        ((0, 0), (0, 0)),
        dimension_numbers=("CNHW", "IOHW", "NCHW"),
        preferred_element_type=jnp.float32,
    )
    return result[:, :, 0, 0]


def transpose_conv(padded, kernel):
    flipped = jnp.transpose(kernel[::-1, ::-1], (0, 1, 3, 2))
    return correlate(padded, flipped)


def kernel_grad(padded, upstream):
    result = lax.conv_general_dilated(
        padded,
        upstream,
        (1, 1),
        ((0, 0), (1, 1)),
        dimension_numbers=("CNHW", "IOHW", "NCHW"),
        preferred_element_type=jnp.float32,
    )
    return jnp.transpose(result, (2, 3, 0, 1))


def local(field, cotangent, spec_weight, point_weight, kernel_one, kernel_two):
    channels, row_count, col_count = (field.shape[2], field.shape[3], field.shape[4])
    inputs = field.reshape(-1, channels, row_count, col_count)
    upstream = cotangent.reshape(-1, channels, row_count, col_count)
    grid_rows = row_count * lax.axis_size("sp")
    first_row = lax.axis_index("sp") * row_count
    forward, doubled = column_tables(col_count, M)
    table_half = forward.astype(jnp.bfloat16)
    inverse_table = jnp.transpose(forward * doubled) / (grid_rows * col_count)
    cosine_table, sine_table = row_tables(
        first_row + jnp.arange(row_count, dtype=jnp.int32), grid_rows, M
    )
    partial_value = row_forward(column_forward(inputs, table_half), cosine_table, sine_table, M)
    spec_own = lax.psum_scatter(partial_value, "sp", scatter_dimension=3, tiled=True)
    mixed_full = lax.all_gather(spectral_mix(spec_own, spec_weight), "sp", axis=3, tiled=True)
    spectral = column_inverse(row_inverse(mixed_full, cosine_table, sine_table, M), inverse_table)
    pointwise = channel_mix(inputs, point_weight)
    padded = padded_2(inputs, (("sp", 2),), 1)
    hidden = correlate(padded, kernel_one)
    middle = gelu_value(hidden).astype(jnp.bfloat16)
    middle_pad = padded_2(middle, (("sp", 2),), 1)
    branch = correlate(middle_pad, kernel_two)
    preact = spectral + pointwise + branch
    output = gelu_value(preact).astype(jnp.bfloat16)
    out_slope = (upstream.astype(jnp.float32) * gelu_slope(preact)).astype(jnp.bfloat16)
    slope_columns = column_forward(out_slope, table_half) * (doubled / (grid_rows * col_count))
    co_partial = row_forward(slope_columns, cosine_table, sine_table, M)
    cospec_own = lax.psum_scatter(co_partial, "sp", scatter_dimension=3, tiled=True)
    own_grad = spectral_grad(spec_own, cospec_own)
    cofield = lax.all_gather(spectral_back(cospec_own, spec_weight), "sp", axis=3, tiled=True)
    back_spec = column_inverse(
        row_inverse(cofield, cosine_table, sine_table, M), jnp.transpose(forward)
    )
    back_point = channel_mix(out_slope, jnp.transpose(point_weight))
    point_delta = channel_outer(inputs, out_slope)
    two_delta = kernel_grad(middle_pad, out_slope)
    slope_pad = padded_2(out_slope, (("sp", 2),), 1)
    pre_slope = (transpose_conv(slope_pad, kernel_two) * gelu_slope(hidden)).astype(jnp.bfloat16)
    pre_pad = padded_2(pre_slope, (("sp", 2),), 1)
    one_delta = kernel_grad(padded, pre_slope)
    back_conv = transpose_conv(pre_pad, kernel_one)
    field_grad = (back_spec + back_point + back_conv).astype(jnp.bfloat16)
    spec_total = lax.psum(own_grad.astype(jnp.bfloat16), "rep").astype(jnp.float32)
    point_total, one_total, two_total = lax.psum((point_delta, one_delta, two_delta), ("rep", "sp"))
    cell_count = lax.axis_size("rep") * inputs.shape[0] * grid_rows * col_count
    grad_scale = 1.0 / math.sqrt(cell_count)
    return (
        output.reshape(field.shape),
        field_grad.reshape(field.shape),
        spec_total,
        point_total * grad_scale,
        one_total * grad_scale,
        two_total * grad_scale,
    )


def solution(mesh):
    in_specs = (
        P("rep", None, None, "sp", None),
        P("rep", None, None, "sp", None),
        P(None, None, None, "sp"),
        P(),
        P(),
        P(),
    )
    out_specs = (
        P("rep", None, None, "sp", None),
        P("rep", None, None, "sp", None),
        P(None, None, None, "sp"),
        P(),
        P(),
        P(),
    )
    return jax.shard_map(local, mesh=mesh, in_specs=in_specs, out_specs=out_specs, check_vma=False)
```

profile of v0, /device:TPU:1, one launch (start us, length us, event | category | flops | bytes accessed | tf_op | source)
XLA Modules:
  0.0 1076.1 jit_solution(13828076538762547051)
XLA Ops:
  30.4 6.7 fusion.112
  42.2 7.0 copy.169
  63.4 6.5 reshape.136
  74.4 7.4 reshape.141
  81.9 6.5 reshape.107
  91.5 9.1 copy.172
  100.6 10.4 multiply_convert_fusion
  130.1 7.3 copy.175
  146.6 10.8 %copy.231 = bf16[8,2,1024,36]{3,1,2,0:T(2,128)(2,1)} copy(bf16[8,2,1024,36]{2,1,3,0:T(2,128)(2,1)} %slice.145) | data formatting | bytes 2359296
  157.5 7.5 copy.210
  165.0 9.3 copy.212
  174.3 7.3 copy.213
  181.6 156.5 %all-reduce.7.cloned.1.call-done = f32[2,2,36,288]{2,1,3,0:T(2,128)} async-done(((f32[2,2,36,288]{2,1,3,0:T(2,128)}), f32[2,2,36,288]{2,1,3,0:T(2,128)}) %all-reduce.7.cloned.1.call-update) | async-done | bytes 165904
  342.0 80.5 %all_gather.6 = f32[2,2,36,288]{2,1,3,0:T(2,128)S(1)} all-gather(f32[2,2,36,9]{2,1,3,0:T(2,128)S(1)} %pad_maximum_fusion.9), channel_id=1, replica_groups=mesh['rep'=4,'sp'=32] {'sp'}, dimensions={3}, use_global_device_ids=true | all-gather | bytes 171072 | tf_op jit(solution)/shard_map/all_gather | solution.py:192
  424.3 11.2 %fusion.280 = bf16[36,10,2,1024]{0,2,3,1:T(2,128)(2,1)S(1)} fusion(bf16[2,36,1,1024]{1,0,3,2:T(2,128)(2,1)} %collective-permute-done.3, bf16[2,36,8,1024]{1,0,3,2:T(2,128)(2,1)} %bitcast.319, bf16[2,36,1,1024]{1,0,3,2:T(2,128)(2,1)} %collective-permute-done.2), kind=kLoop, calls=%fused_computation.299 | loop fusion | flops 1474560 | bytes 2949120 | tf_op jit(solution)/shard_map/concatenate | solution.py:22
  442.3 10.5 broadcast_select_fusion.1
  452.8 9.7 copy.181
  497.6 11.9 %convolution_bitcast_fusion.1 = f32[36,36]{1,0:T(8,128)} fusion(bf16[2,36,8,1024]{1,0,3,2:T(2,128)(2,1)} %copy.207, bf16[2,36,8,1024]{1,0,3,2:T(2,128)(2,1)} %copy.208), kind=kOutput, calls=%fused_computation.97 | convolution fusion | flops 42467328 | bytes 2364480 | tf_op jit(solution)/shard_map/conv_general_dilated | solution.py:150
  509.5 27.1 %fusion.257 = f32[3,3,36,36]{3,2,1,0:T(8,128)} fusion(bf16[2,36,8,1024]{1,0,3,2:T(2,128)(2,1)S(1)} %copy-done.14, bf16[2,36,1,1024]{1,0,3,2:T(2,128)(2,1)} %collective-permute-done.3, bf16[2,36,8,1024]{1,0,3,2:T(2,128)(2,1)S(1)} %bitcast.320, bf16[2,36,1,1024]{1,0,3,2:T(2,128)(2,1)} %collective-permute-done.2), kind=kOutput, calls=%fused_computation.298 | convolution fusion | flops 386380800 | bytes 2700864 | tf_op jit(solution)/shard_map/transpose | solution.py:175
  541.1 7.0 copy.196
  559.9 6.5 reshape.126
  569.5 9.2 copy.199
  578.7 13.2 %fusion.12 = bf16[8,16,129,36]{3,1,2,0:T(8,128)(2,1)} fusion(f32[8,16,129,36]{3,1,2,0:T(8,128)} %get-tuple-element.60, pred[16,129]{0,1:T(8,128)(4,1)S(1)} %copy-done.31, bf16[3,3,36,36]{3,2,1,0:T(8,128)(2,1)S(1)} %copy-done.29, bf16[36,10,2,8,131]{0,3,2,4,1:T(8,128)(2,1)} %copy.199), kind=kOutput, calls=%fused_computation.14 | convolution fusion | flops 392325120 | bytes 5101104 | tf_op jit(solution)/shard_map/conv_general_dilated | solution.py:128
  591.9 7.1 copy.201
  614.2 14.9 %fusion.62 = f32[3,3,36,36]{3,2,1,0:T(8,128)} fusion(bf16[8,16,129,36]{3,1,2,0:T(8,128)(2,1)} %fusion.12, pred[16,129]{0,1:T(8,128)(4,1)S(1)} %copy-done.31, bf16[36,10,16,129,1]{0,2,4,3,1:T(8,128)(2,1)} %bitcast.322, bf16[36,10,16,129,1]{0,2,4,3,1:T(8,128)(2,1)} %copy.213, bf16[36,10,16,129,1]{0,2,4,3,1:T(8,128)(2,1)} %bitcast.321), kind=kOutput, calls=%fused_computation.81 | convolution fusion | flops 390244608 | bytes 5695824 | tf_op jit(solution)/shard_map/transpose | solution.py:175
  630.0 209.2 %all-reduce.9.cloned.1.call-done = f32[2,2,36,288]{2,1,3,0:T(2,128)} async-done(((f32[2,2,36,288]{2,1,3,0:T(2,128)}), f32[2,2,36,288]{2,1,3,0:T(2,128)}) %all-reduce.9.cloned.1.call-update) | async-done | bytes 165904
  843.6 80.6 %all_gather.7 = f32[2,2,36,288]{2,1,3,0:T(2,128)S(1)} all-gather(f32[2,2,36,9]{2,1,3,0:T(2,128)S(1)} %pad_maximum_fusion.10), channel_id=1, replica_groups=mesh['rep'=4,'sp'=32] {'sp'}, dimensions={3}, use_global_device_ids=true | all-gather | bytes 171072 | tf_op jit(solution)/shard_map/all_gather | solution.py:207
  930.8 43.9 %psum.28 = bf16[2,36,36,9]{1,2,3,0:T(8,128)(2,1)S(1)} all-reduce(bf16[2,36,36,9]{1,2,3,0:T(8,128)(2,1)S(1)} %pad_maximum_fusion.5), channel_id=1, replica_groups=mesh['rep'=4,'sp'=32] {'rep'}, use_global_device_ids=true, to_apply=%region_2.3 | all-reduce | flops 23328 | bytes 93312 | tf_op jit(solution)/shard_map/psum | solution.py:220
  975.9 29.9 %all-reduce.11.cloned.1.call-done = (f32[36,36]{1,0:T(8,128)}, f32[3,3,36,36]{3,2,1,0:T(8,128)}, f32[3,3,36,36]{3,2,1,0:T(8,128)}) async-done(((f32[36,36]{1,0:T(8,128)}, f32[3,3,36,36]{3,2,1,0:T(8,128)}, f32[3,3,36,36]{3,2,1,0:T(8,128)}), (f32[36,36]{1,0:T(8,128)}, f32[3,3,36,36]{3,2,1,0:T(8,128)}, f32[3,3,36,36]{3,2,1,0:T(8,128)})) %all-reduce.11.cloned.1.call-update) | async-done | bytes 98512 | tf_op jit(solution)/shard_map/psum | solution.py:221
  1027.9 9.1 copy.204
  1037.0 9.8 broadcast_select_fusion
  1046.8 9.6 copy.205
  (214 shorter events, 207.3 us)
Async XLA Ops:
  7.2 93.4 %copy-start = (bf16[3,3,36,36]{3,2,1,0:T(8,128)(2,1)S(1)}, bf16[3,3,36,36]{3,2,1,0:T(8,128)(2,1)}, u32[]{:S(2)}) copy-start(bf16[3,3,36,36]{3,2,1,0:T(8,128)(2,1)} %param.10) | copy-start | bytes 69988
  7.2 330.9 %all-reduce.7.cloned.1.call-start = ((), (), s32[]{:S(2)}) async-start(), calls=%async_computation | async-start | bytes 1179648
  7.2 481.4 %copy-start.21 = (s32[24]{0:T(128)}, s32[24]{0:T(128)S(1)}, u32[]{:S(2)}) copy-start(s32[24]{0:T(128)S(1)} %compare_select_fusion) | copy-start | bytes 292
  7.5 478.0 %copy-start.16 = (f32[1024,12]{0,1:T(8,128)}, f32[1024,12]{0,1:T(8,128)S(1)}, u32[]{:S(2)}) copy-start(f32[1024,12]{0,1:T(8,128)S(1)} %get-tuple-element.61) | copy-start | bytes 147460
  7.5 478.0 %copy-start.18 = (f32[1024,12]{0,1:T(8,128)}, f32[1024,12]{0,1:T(8,128)S(1)}, u32[]{:S(2)}) copy-start(f32[1024,12]{0,1:T(8,128)S(1)} %get-tuple-element.62) | copy-start | bytes 147460
  7.6 481.0 %copy-start.23 = (s32[8]{0:T(128)}, s32[8]{0:T(128)S(1)}, u32[]{:S(2)}) copy-start(s32[8]{0:T(128)S(1)} %iota_add_fusion) | copy-start | bytes 100
  9.5 11.5 %copy-start.20 = (f32[2,36,36,9]{2,0,3,1:T(2,128)S(1)}, f32[2,36,36,9]{2,0,3,1:T(2,128)}, u32[]{:S(2)}) copy-start(f32[2,36,36,9]{2,0,3,1:T(2,128)} %param.8) | copy-start | bytes 279940
  14.1 825.1 %all-reduce.9.cloned.1.call-start = ((), (), s32[]{:S(2)}) async-start(), calls=%async_computation.1 | async-start | bytes 1179648
  15.3 38.9 %collective-permute-start = (bf16[2,36,1,1024]{3,2,1,0:T(2,128)(2,1)}, bf16[2,36,1,1024]{3,2,1,0:T(2,128)(2,1)S(1)}, u32[]{:S(2)}, u32[]{:S(2)}) collective-permute-start(bf16[2,36,1,1024]{3,2,1,0:T(2,128)(2,1)} %get-tuple-element.47), channel_id=1, source_target_pairs={{0,1},{1,2},{2,3},{3,4},{4,5},{5,6},{6,7},{7,8},{8,9},{9,10},{10,1... | collective-permute-start | bytes 442376 | tf_op jit(solution)/shard_map/ppermute | solution.py:24
  19.7 34.6 %collective-permute-start.1 = (bf16[2,36,1,1024]{3,2,1,0:T(2,128)(2,1)}, bf16[2,36,1,1024]{3,2,1,0:T(2,128)(2,1)}, u32[]{:S(2)}, u32[]{:S(2)}) collective-permute-start(bf16[2,36,1,1024]{3,2,1,0:T(2,128)(2,1)} %get-tuple-element.48), channel_id=1, source_target_pairs={{1,0},{2,1},{3,2},{4,3},{5,4},{6,5},{7,6},{8,7},{9,8},{10,9},{11,1... | collective-permute-start | bytes 442376 | tf_op jit(solution)/shard_map/ppermute | solution.py:26
  21.3 318.7 %copy-start.11 = (f32[1,36,36,9]{2,0,3,1:T(1,128)}, f32[1,36,36,9]{2,0,3,1:T(1,128)S(1)}, u32[]{:S(2)}) copy-start(f32[1,36,36,9]{2,0,3,1:T(1,128)S(1)} %get-tuple-element.53) | copy-start | bytes 139972
  21.3 319.7 %copy-start.9 = (f32[1,36,36,9]{2,0,3,1:T(1,128)}, f32[1,36,36,9]{2,0,3,1:T(1,128)S(1)}, u32[]{:S(2)}) copy-start(f32[1,36,36,9]{2,0,3,1:T(1,128)S(1)} %get-tuple-element.54) | copy-start | bytes 139972
  115.8 308.5 %collective-permute-start.2 = (bf16[2,36,1,1024]{1,0,3,2:T(2,128)(2,1)}, bf16[2,36,1,1024]{1,0,3,2:T(2,128)(2,1)}, u32[]{:S(2)}, u32[]{:S(2)}) collective-permute-start(bf16[2,36,1,1024]{1,0,3,2:T(2,128)(2,1)} %bitcast.34), channel_id=1, source_target_pairs={{0,1},{1,2},{2,3},{3,4},{4,5},{5,6},{6,7},{7,8},{8,9},{9,10},{10,1... | collective-permute-start | bytes 442376 | tf_op jit(solution)/shard_map/ppermute | solution.py:24
  123.3 301.1 %collective-permute-start.3 = (bf16[2,36,1,1024]{1,0,3,2:T(2,128)(2,1)}, bf16[2,36,1,1024]{1,0,3,2:T(2,128)(2,1)}, u32[]{:S(2)}, u32[]{:S(2)}) collective-permute-start(bf16[2,36,1,1024]{1,0,3,2:T(2,128)(2,1)} %bitcast.36), channel_id=1, source_target_pairs={{1,0},{2,1},{3,2},{4,3},{5,4},{6,5},{7,6},{8,7},{9,8},{10,9},{11,1... | collective-permute-start | bytes 442376 | tf_op jit(solution)/shard_map/ppermute | solution.py:26
  165.0 9.3 copy-start.6
  475.6 15.1 %copy-start.2 = (bf16[2,36,8,1024]{3,2,1,0:T(8,128)(2,1)}, bf16[2,36,8,1024]{3,2,1,0:T(8,128)(2,1)S(1)}, u32[]{:S(2)}) copy-start(bf16[2,36,8,1024]{3,2,1,0:T(8,128)(2,1)S(1)} %get-tuple-element.41) | copy-start | bytes 3538948
  482.3 69.9 %collective-permute-start.4 = (bf16[2,36,1,1024]{3,2,1,0:T(2,128)(2,1)}, bf16[2,36,1,1024]{3,2,1,0:T(2,128)(2,1)}, u32[]{:S(2)}, u32[]{:S(2)}) collective-permute-start(bf16[2,36,1,1024]{3,2,1,0:T(2,128)(2,1)} %get-tuple-element.45), channel_id=1, source_target_pairs={{0,1},{1,2},{2,3},{3,4},{4,5},{5,6},{6,7},{7,8},{8,9},{9,10},{10,1... | collective-permute-start | bytes 442376 | tf_op jit(solution)/shard_map/ppermute | solution.py:24
  484.3 67.9 %collective-permute-start.5 = (bf16[2,36,1,1024]{3,2,1,0:T(2,128)(2,1)}, bf16[2,36,1,1024]{3,2,1,0:T(2,128)(2,1)}, u32[]{:S(2)}, u32[]{:S(2)}) collective-permute-start(bf16[2,36,1,1024]{3,2,1,0:T(2,128)(2,1)} %get-tuple-element.46), channel_id=1, source_target_pairs={{1,0},{2,1},{3,2},{4,3},{5,4},{6,5},{7,6},{8,7},{9,8},{10,9},{11,1... | collective-permute-start | bytes 442376 | tf_op jit(solution)/shard_map/ppermute | solution.py:26
  490.6 515.2 %all-reduce.11.cloned.1.call-start = ((), (), s32[]{:S(2)}) async-start(), calls=%async_computation.2 | async-start | bytes 778240 | tf_op jit(solution)/shard_map/psum | solution.py:221
  497.6 12.0 %copy-start.5 = (bf16[8,2,1024,36]{3,1,2,0:T(2,128)(2,1)S(1)}, bf16[8,2,1024,36]{3,1,2,0:T(2,128)(2,1)}, u32[]{:S(2)}) copy-start(bf16[8,2,1024,36]{3,1,2,0:T(2,128)(2,1)} %copy.231) | copy-start | bytes 3538948
  497.6 12.0 %copy-start.14 = (bf16[2,36,8,1024]{1,0,3,2:T(2,128)(2,1)S(1)}, bf16[2,36,8,1024]{1,0,3,2:T(2,128)(2,1)}, u32[]{:S(2)}) copy-start(bf16[2,36,8,1024]{1,0,3,2:T(2,128)(2,1)} %copy.208) | copy-start | bytes 3538948
  509.5 27.1 %copy-start.4 = (bf16[36,8,16,128]{0,2,3,1:T(8,128)(2,1)S(1)}, bf16[36,8,16,128]{0,2,3,1:T(8,128)(2,1)}, u32[]{:S(2)}) copy-start(bf16[36,8,16,128]{0,2,3,1:T(8,128)(2,1)} %copy.195) | copy-start | bytes 3538948
  509.5 27.1 %copy-start.26 = (bf16[36,36]{1,0:T(8,128)(2,1)S(1)}, bf16[36,36]{1,0:T(8,128)(2,1)}, u32[]{:S(2)}) copy-start(bf16[36,36]{1,0:T(8,128)(2,1)} %param.9) | copy-start | bytes 7780
  569.5 9.2 copy-start.29
  569.5 9.2 copy-start.31
  606.9 403.5 %collective-permute-start.6 = (bf16[2,36,1,1024]{3,0,1,2:T(2,128)(2,1)}, bf16[2,36,1,1024]{3,0,1,2:T(2,128)(2,1)S(1)}, u32[]{:S(2)}, u32[]{:S(2)}) collective-permute-start(bf16[2,36,1,1024]{3,0,1,2:T(2,128)(2,1)} %slice_bitcast_fusion.2), channel_id=1, source_target_pairs={{0,1},{1,2},{2,3},{3,4},{4,5},{5,6},{6,7},{7,8},{8,9},{9,10},{10,1... | collective-permute-start | bytes 442376 | tf_op jit(solution)/shard_map/ppermute | solution.py:24
  612.9 397.5 %collective-permute-start.7 = (bf16[2,36,1,1024]{3,0,1,2:T(2,128)(2,1)}, bf16[2,36,1,1024]{3,0,1,2:T(2,128)(2,1)}, u32[]{:S(2)}, u32[]{:S(2)}) collective-permute-start(bf16[2,36,1,1024]{3,0,1,2:T(2,128)(2,1)} %slice_bitcast_fusion.1), channel_id=1, source_target_pairs={{1,0},{2,1},{3,2},{4,3},{5,4},{6,5},{7,6},{8,7},{9,8},{10,9},{11,1... | collective-permute-start | bytes 442376 | tf_op jit(solution)/shard_map/ppermute | solution.py:26
  614.2 14.9 %copy-start.13 = (bf16[8,2,1032,36]{2,1,3,0:T(2,128)(2,1)S(1)}, bf16[8,2,1032,36]{2,1,3,0:T(2,128)(2,1)}, u32[]{:S(2)}) copy-start(bf16[8,2,1032,36]{2,1,3,0:T(2,128)(2,1)} %reshape.159) | copy-start | bytes 3566596
  614.2 225.0 %copy-start.12 = (f32[1,36,36,9]{2,0,3,1:T(1,128)S(1)}, f32[1,36,36,9]{2,0,3,1:T(1,128)}, u32[]{:S(2)}) copy-start(f32[1,36,36,9]{2,0,3,1:T(1,128)} %copy-done.11) | copy-start | bytes 139972
  614.2 227.2 %copy-start.10 = (f32[1,36,36,9]{2,0,3,1:T(1,128)S(1)}, f32[1,36,36,9]{2,0,3,1:T(1,128)}, u32[]{:S(2)}) copy-start(f32[1,36,36,9]{2,0,3,1:T(1,128)} %copy-done.9) | copy-start | bytes 139972
  629.1 295.1 %copy-start.22 = (s32[24]{0:T(128)S(1)}, s32[24]{0:T(128)}, u32[]{:S(2)}) copy-start(s32[24]{0:T(128)} %copy-done.21) | copy-start | bytes 292
  629.1 295.1 %copy-start.24 = (s32[8]{0:T(128)S(1)}, s32[8]{0:T(128)}, u32[]{:S(2)}) copy-start(s32[8]{0:T(128)} %copy-done.23) | copy-start | bytes 100
  (12 other events, 42.9 us)
Sparse Core Ops, SparseCore 0:
  14.2 323.8 all-reduce.6
  490.7 348.4 all-reduce.8
  845.0 160.7 all-reduce.10
where the time goes:
time: 1080 us
  waiting for transfers between devices  396 us (37%)
  local copies, waits for them, and re-layouts  256 us (24%)
  blocking collectives  205 us (19%)
  matrix products  143 us (13%)
  other arithmetic  40.3 us (4%)
  starting transfers between devices  20.5 us (2%)
  between operations  15.6 us (1%)
    unnamed x5, waiting for transfers between devices  366 us
    conv_general_dilated x17, local copies, waits for them, and re-layouts, correlate(): lax.conv_general_dilated(padded, kernel, (1, 1), ((0, 0), (1, 1)), dimens...  81.3 us
    all_gather x1, blocking collectives, local(): lax.all_gather(spectral_back(cospec_own, spec_weight), 'sp', axis=3, tile...  80.6 us
    all_gather x1, blocking collectives, local(): lax.all_gather(spectral_mix(spec_own, spec_weight), 'sp', axis=3, tiled=T...  80.5 us
    concatenate x11, local copies, waits for them, and re-layouts, padded_2(): jnp.concatenate([lax.ppermute(tail, axis, [(i, (i + 1) % count) for i in...  60.8 us
    conv_general_dilated x4, matrix products, correlate(): lax.conv_general_dilated(padded, kernel, (1, 1), ((0, 0), (1, 1)), dimens...  43.9 us
    psum x1, blocking collectives, local(): lax.psum(own_grad.astype(jnp.bfloat16), 'rep').astype(jnp.float32)  43.9 us
    transpose x2, matrix products, kernel_grad(): return jnp.transpose(result, (2, 3, 0, 1))  42 us
  transfers between devices with their start and end apart: 11, of which 3 were waited for; matrix products, arithmetic and copies ran while one was open for 29% of the time, Pallas kernels for 0%

commit v1 on v0

v1 whole, which is shorter than its diff:
```python
import math

import jax
import jax.numpy as jnp
import numpy as np
import ml_dtypes
from jax import lax
from jax.experimental import pallas as pl
from jax.experimental.pallas import tpu as pltpu
from jax.sharding import PartitionSpec as P

M = 12
C = 36
CP = 48
CO = 40
LEV = 2
RL = 8
NC = 1024
NR = 256
SP = 32
QN = 9
GR = 3 * CP

ROOT_HALF = 0.7071067811865476
INV_ROOT_TAU = 0.3989422804014327
BF = jnp.bfloat16
F32 = jnp.float32
HIGHEST = lax.Precision.HIGHEST
VMEM = 56 * 1024 * 1024


def split_np(values):
    high = values.astype(np.float32).astype(ml_dtypes.bfloat16)
    low = (values - high.astype(np.float64)).astype(np.float32).astype(ml_dtypes.bfloat16)
    return high, low


def make_tables():
    n = np.arange(NC)[:, None]
    k = np.arange(M)[None, :]
    t = 2.0 * np.pi * ((n * k) % NC) / NC
    forward = np.concatenate([np.cos(t), -np.sin(t)], axis=1)
    doubled = np.where(np.arange(M) == 0, 1.0, 2.0)
    doubled = np.concatenate([doubled, doubled]) / (NR * NC)
    table = np.zeros((NC, 128), np.float32)
    table[:, :24] = forward
    table = table.astype(ml_dtypes.bfloat16)

    def inverse(matrix):
        high, low = split_np(matrix.T)
        out = np.zeros((128, NC), ml_dtypes.bfloat16)
        out[0:24], out[24:48], out[48:72] = high, low, high
        return out

    rows = np.zeros((SP, 2, 16, 256))
    freq = np.where(np.arange(24) < M, np.arange(24), NR - 24 + np.arange(24))
    phase = np.zeros((SP, SP, 2, 16, 2))
    for owner in range(SP):
        for q in range(QN):
            mode = owner * QN + q
            j, kk = mode // M, mode % M
            for r in range(RL):
                p = 2.0 * np.pi * ((freq[j] * r) % NR) / NR
                rows[owner, 0, q, r * 24 + kk] = np.cos(p)
                rows[owner, 0, q, r * 24 + 12 + kk] = np.sin(p)
                rows[owner, 1, q, r * 24 + kk] = -np.sin(p)
                rows[owner, 1, q, r * 24 + 12 + kk] = np.cos(p)
            for s in range(SP):
                p = 2.0 * np.pi * ((freq[j] * s) % SP) / SP
                phase[s, owner, :, q, 0] = np.cos(p)
                phase[s, owner, :, q, 1] = np.sin(p)
    high, low = split_np(rows.reshape(SP * 32, 256))
    scale = np.zeros((1, 256), np.float32)
    scale[0, :192] = np.tile(doubled, RL)
    return (
        table,
        inverse(forward * doubled[None, :]),
        inverse(forward),
        high,
        low,
        phase.reshape(SP, SP * 32, 2).astype(np.float32),
        scale,
    )


TABLE, INVERSE, BACK, ROW_HIGH, ROW_LOW, PHASE, SCALE = make_tables()


def dot(a, b, precision=None):
    return lax.dot_general(a, b, (((1,), (0,)), ((), ())), precision=precision, preferred_element_type=F32)


def dot_nt(a, b, precision=None):
    return lax.dot_general(a, b, (((1,), (1,)), ((), ())), precision=precision, preferred_element_type=F32)


def dot_tn(a, b, precision=None):
    return lax.dot_general(a, b, (((0,), (0,)), ((), ())), precision=precision, preferred_element_type=F32)


def split(values):
    high = values.astype(BF)
    return high, (values - high.astype(F32)).astype(BF)


def gelu_parts(v):
    cdf = 0.5 * (1.0 + lax.erf(v * ROOT_HALF))
    return v * cdf, cdf + v * jnp.exp(-0.5 * v * v) * INV_ROOT_TAU


def store_taps(taps, i, x):
    col = lax.broadcasted_iota(jnp.int32, (CP, NC), 1)
    taps[i, 0:CP] = jnp.where(col == 0, 0.0, pltpu.roll(x, 1, 1)).astype(BF)
    taps[i, CP : 2 * CP] = x.astype(BF)
    taps[i, 2 * CP : 3 * CP] = jnp.where(col == NC - 1, 0.0, pltpu.roll(x, NC - 1, 1)).astype(BF)


def three(ref, i, width):
    return ref[pl.ds(i, 3)].reshape(3 * width, NC)


def row_transform(cols, phase, high, low):
    c_high, c_low = split(cols)
    out = dot_nt(high, c_high) + dot_nt(high, c_low) + dot_nt(low, c_high)
    out = out.reshape(SP, 2, 16, 128)
    cosine = phase[:, 0:1].reshape(SP, 2, 16, 1)
    sine = phase[:, 1:2].reshape(SP, 2, 16, 1)
    re, im = out[:, 0], out[:, 1]
    c, s = cosine[:, 0], sine[:, 0]
    both = jnp.concatenate([(re * c + im * s)[:, None], (im * c - re * s)[:, None]], axis=1)
    return both.reshape(SP * 32, 128).astype(BF)


def row_expand(modes, phase, high, low):
    m = modes.astype(F32).reshape(SP, 2, 16, 128)
    cosine = phase[:, 0:1].reshape(SP, 2, 16, 1)
    sine = phase[:, 1:2].reshape(SP, 2, 16, 1)
    re, im = m[:, 0], m[:, 1]
    c, s = cosine[:, 0], sine[:, 0]
    both = jnp.concatenate([(re * c - im * s)[:, None], (re * s + im * c)[:, None]], axis=1)
    m_high, m_low = split(both.reshape(SP * 32, 128))
    return dot_tn(m_high, high) + dot_tn(m_high, low) + dot_tn(m_low, high)


def place_rows(rows, left):
    high, low = split(rows)
    high, low = high.astype(F32), low.astype(F32)
    left[...] = jnp.zeros_like(left)
    for lev in range(LEV):
        for r in range(RL):
            at = (lev * RL + r) * CO
            h = high[lev * 64 : lev * 64 + CO, r * 24 : r * 24 + 24]
            w = low[lev * 64 : lev * 64 + CO, r * 24 : r * 24 + 24]
            left[at : at + CO, 0:72] = jnp.concatenate([h, h, w], axis=1)


def kernel_a(field, table, high, low, phase, message, rows, top, bottom, wide, flat, cols):
    flat[...] = dot(field[...], table[...])
    cols[...] = jnp.zeros_like(cols)
    for lev in range(LEV):
        for r in range(RL):
            part = flat[pl.ds(lev * C * RL + r, C, stride=RL), :]
            cols[lev * 64 : lev * 64 + C, r * 24 : r * 24 + 24] = part[:, 0:24]
    message[...] = row_transform(cols[...], phase[...], high[...], low[...])
    for n in range(0, NC, 128):
        wide[n // 128, 0 : LEV * C * RL, :] = field[:, n : n + 128].astype(F32)
        wide[n // 128, LEV * C * RL :, :] = jnp.zeros((12 * RL, 128), F32)
    for lev in range(LEV):
        for r in range(RL):
            for n in range(0, NC, 128):
                x = wide[n // 128, pl.ds(lev * C * RL + r, CP, stride=RL), :].astype(BF)
                rows[lev, r, :, n : n + 128] = x
                if r < 2:
                    top[lev, r, :, n : n + 128] = x
                if r >= RL - 2:
                    bottom[lev, r - RL + 2, :, n : n + 128] = x


def kernel_b(place, rows, above, below, cot, w_one, w_two, middle, slope, pre, cot_rows, taps, taps_two, point, wide):
    index = place[0]
    for r in range(2):
        store_taps(taps, r, above[0, r].astype(F32))
        store_taps(taps, RL + 2 + r, below[0, r].astype(F32))

    def fill(r, carry):
        store_taps(taps, r + 2, rows[0, r].astype(F32))
        return carry

    lax.fori_loop(0, RL, fill, 0)
    for n in range(0, NC, 128):
        wide[n // 128, 0 : C * RL, :] = cot[0, :, n : n + 128].astype(F32)
        wide[n // 128, C * RL :, :] = jnp.zeros((12 * RL, 128), F32)
    for r in range(RL):
        for n in range(0, NC, 128):
            cot_rows[0, r, :, n : n + 128] = wide[n // 128, pl.ds(r, CP, stride=RL), :].astype(BF)

    def first(i, carry):
        d = dot(w_one[...], three(taps, i, GR))
        value, gradient = gelu_parts(d[0:CO])
        outside = ((i == 0) & (index == 0)) | ((i == RL + 1) & (index == SP - 1))
        keep = jnp.where(outside, 0.0, 1.0).astype(F32)
        value = jnp.concatenate([value * keep, jnp.zeros((CP - CO, NC), F32)], axis=0)
        slope[0, i] = gradient * keep
        middle[0, i] = value.astype(BF)
        store_taps(taps_two, i, value)
        point[i] = d[CP : CP + CO]
        return carry

    lax.fori_loop(0, RL + 2, first, 0)

    def second(r, carry):
        pre[0, r] = dot(w_two[...], three(taps_two, r, GR))[0:CO] + point[r + 1]
        return carry

    lax.fori_loop(0, RL, second, 0)


def own_modes(received):
    own = jnp.sum(received.astype(F32), axis=0)
    return own, jnp.concatenate([own[:, 0:64], own[:, 64:128]], axis=0)


def mode_products(stacked, weight):
    row = lax.broadcasted_iota(jnp.int32, (64, 128), 0) % 16
    total = jnp.zeros((64, 128), F32)
    for q in range(QN):
        total = total + jnp.where(row == q, dot(stacked, weight[q], HIGHEST), 0.0)
    return total


def kernel_mix(received, weight, message, kept):
    _, stacked = own_modes(received[...])
    kept[...] = stacked
    total = mode_products(stacked, weight)
    res, ims = [], []
    for lev in range(LEV):
        r, i = total[lev * 32 : lev * 32 + 16], total[lev * 32 + 16 : lev * 32 + 32]
        res.append(r[:, 0:64] - i[:, 64:128])
        ims.append(r[:, 64:128] + i[:, 0:64])
    mixed = jnp.concatenate([jnp.concatenate(res, axis=1), jnp.concatenate(ims, axis=1)], axis=0)
    message[...] = jnp.broadcast_to(mixed.astype(BF)[None], (SP, 32, 128))


def kernel_mix_back(received, weight, kept, message, grad):
    _, stacked = own_modes(received[...])
    total = mode_products(stacked, weight)
    res, ims = [], []
    for lev in range(LEV):
        r, i = total[lev * 32 : lev * 32 + 16], total[lev * 32 + 16 : lev * 32 + 32]
        res.append(r[:, 0:64] + i[:, 64:128])
        ims.append(i[:, 0:64] - r[:, 64:128])
    mixed = jnp.concatenate([jnp.concatenate(res, axis=1), jnp.concatenate(ims, axis=1)], axis=0)
    message[...] = jnp.broadcast_to(mixed.astype(BF)[None], (SP, 32, 128))
    swapped = jnp.concatenate(
        [stacked[16:32], -stacked[0:16], stacked[48:64], -stacked[32:48]], axis=0
    )
    right = jnp.concatenate([stacked, swapped], axis=1)
    row = lax.broadcasted_iota(jnp.int32, (64, 64), 0) % 16
    left = kept[...]
    for q in range(QN):
        grad[q] = dot_tn(jnp.where(row == q, left, 0.0), right, HIGHEST)[0:CP].astype(BF)


def kernel_d(received, phase, high, low, inverse, pre, cot, table, scale, out, slopes, top, bottom, message, left, spec, wide, flat, cols):
    place_rows(row_expand(received[...], phase[...], high[...], low[...]), left)
    spec[...] = dot(left[...].astype(BF), inverse[...])

    def one(t, carry):
        lev, r = t // RL, t % RL
        preact = pre[lev, r] + spec[pl.ds(pl.multiple_of(t * CO, 8), CO), :]
        value, gradient = gelu_parts(preact)
        for n in range(0, NC, 128):
            wide[n // 128, pl.ds(lev * C * RL + r, C, stride=RL), :] = value[0:C, n : n + 128]
        s = jnp.concatenate([gradient, jnp.zeros((CP - CO, NC), F32)], axis=0) * cot[lev, r].astype(F32)
        s = s.astype(BF)
        slopes[lev, r] = s
        return carry

    lax.fori_loop(0, LEV * RL, one, 0)
    for n in range(0, NC, 128):
        out[:, n : n + 128] = wide[n // 128].astype(BF)
    flat[...] = dot(slopes[...].reshape(LEV * RL * CP, NC), table[...])
    cols[...] = jnp.zeros_like(cols)
    for lev in range(LEV):
        top[lev] = slopes[lev, 0:2]
        bottom[lev] = slopes[lev, RL - 2 : RL]
        for r in range(RL):
            at = (lev * RL + r) * CP
            cols[lev * 64 : lev * 64 + CO, r * 24 : r * 24 + 24] = flat[at : at + CO, 0:24]
    message[...] = row_transform(cols[...] * scale[...], phase[...], high[...], low[...])


def kernel_e(place, slopes, above, below, middle, rows, f_above, f_below, slope, w_two, w_one, back, grad_two, grad_one, grad_point, taps, taps_two, field, point):
    index = place[0]
    lev = pl.program_id(0)
    for r in range(2):
        store_taps(taps, r, above[0, r].astype(F32))
        store_taps(taps, RL + 2 + r, below[0, r].astype(F32))
    field[0] = f_above[0, 1]
    field[RL + 1] = f_below[0, 0]

    def fill(r, carry):
        store_taps(taps, r + 2, slopes[0, r].astype(F32))
        field[r + 1] = rows[0, r]
        return carry

    lax.fori_loop(0, RL, fill, 0)

    @pl.when(lev == 0)
    def _():
        grad_two[...] = jnp.zeros_like(grad_two)
        grad_one[...] = jnp.zeros_like(grad_one)
        grad_point[...] = jnp.zeros_like(grad_point)

    def first(i, carry):
        d = dot(w_two[...], three(taps, i, GR))
        outside = ((i == 0) & (index == 0)) | ((i == RL + 1) & (index == SP - 1))
        keep = jnp.where(outside, 0.0, 1.0).astype(F32)
        value = jnp.concatenate([d[0:CO] * (slope[0, i] * keep), jnp.zeros((CP - CO, NC), F32)], axis=0)
        store_taps(taps_two, i, value)
        point[i] = d[CP : CP + CO]
        return carry

    lax.fori_loop(0, RL + 2, first, 0)

    def second(r, carry):
        back[0, r] = dot(w_one[...], three(taps_two, r, GR))[0:CO] + point[r + 1]
        grad_two[...] += dot_nt(three(middle.at[0], r, CP), taps[r + 2])
        grad_one[...] += dot_nt(three(field, r, CP), taps_two[r + 1])
        grad_point[...] += dot_nt(field[r + 1], taps[r + 2, CP : 2 * CP])
        return carry

    lax.fori_loop(0, RL, second, 0)


def kernel_f(received, phase, high, low, inverse, back, out, left, spec, wide):
    place_rows(row_expand(received[...], phase[...], high[...], low[...]), left)
    spec[...] = dot(left[...].astype(BF), inverse[...])

    def one(t, carry):
        lev, r = t // RL, t % RL
        value = back[lev, r] + spec[pl.ds(pl.multiple_of(t * CO, 8), CO), :]
        for n in range(0, NC, 128):
            wide[n // 128, pl.ds(lev * C * RL + r, C, stride=RL), :] = value[0:C, n : n + 128]
        return carry

    lax.fori_loop(0, LEV * RL, one, 0)
    for n in range(0, NC, 128):
        out[:, n : n + 128] = wide[n // 128].astype(BF)


def shape(dims, kind):
    return jax.ShapeDtypeStruct(dims, kind)


def params():
    return pltpu.CompilerParams(vmem_limit_bytes=VMEM)


def cost(us):
    return pl.CostEstimate(flops=int(us * 1e9), bytes_accessed=int(us * 3e6), transcendentals=0)


def level_spec(*dims):
    return pl.BlockSpec((1,) + dims, lambda lev: (lev,) + (0,) * len(dims))


def whole_spec(*dims):
    return pl.BlockSpec(dims, lambda lev: (0,) * len(dims))


def taps_weight(kernel):
    padded = jnp.pad(kernel, ((0, 0), (0, 0), (0, CP - C), (0, CP - C)))
    return jnp.transpose(padded, (3, 0, 1, 2)).reshape(CP, 9 * CP)


def centre_weight(matrix):
    padded = jnp.pad(matrix, ((0, CP - C), (0, CP - C)))
    return jnp.pad(jnp.transpose(padded), ((0, 0), (4 * CP, 4 * CP)))


def mode_weight(weight):
    moved = jnp.transpose(weight, (3, 1, 0, 2))
    return jnp.pad(moved, ((0, 0), (0, 64 - C), (0, 0), (0, 64 - C))).reshape(QN, 64, 128)


def from_above(x):
    return lax.ppermute(x, "sp", [(i, i + 1) for i in range(SP - 1)])


def from_below(x):
    return lax.ppermute(x, "sp", [(i + 1, i) for i in range(SP - 1)])


def exchange(x):
    return lax.all_to_all(x, "sp", 0, 0, tiled=True)


def local(field, cotangent, spec_weight, point_weight, kernel_one, kernel_two):
    index = lax.axis_index("sp")
    place = index.astype(jnp.int32).reshape(1)
    inputs = field.reshape(LEV * C * RL, NC)
    upstream = cotangent.reshape(LEV, C * RL, NC)
    phase = lax.dynamic_index_in_dim(jnp.asarray(PHASE), index, 0, keepdims=False)
    table, high, low = jnp.asarray(TABLE), jnp.asarray(ROW_HIGH), jnp.asarray(ROW_LOW)
    strip = shape((LEV, 2, CP, NC), BF)
    message, rows, top, bottom = pl.pallas_call(
        kernel_a,
        out_shape=[shape((SP * 32, 128), BF), shape((LEV, RL, CP, NC), BF), strip, strip],
        scratch_shapes=[
            pltpu.VMEM((NC // 128, (LEV * C + 12) * RL, 128), F32),
            pltpu.VMEM((LEV * C * RL, 128), F32),
            pltpu.VMEM((128, 256), F32),
        ],
        compiler_params=params(),
        cost_estimate=cost(8),
        name="field_modes",
    )(inputs, table, high, low, phase)
    f_above, f_below = from_above(bottom), from_below(top)
    arrived = exchange(message.reshape(SP, 32, 128))

    w_one = jnp.concatenate([taps_weight(kernel_one), centre_weight(point_weight)], axis=0)
    w_two = taps_weight(kernel_two)
    middle, slope, pre, cot_rows = pl.pallas_call(
        kernel_b,
        grid=(LEV,),
        in_specs=[
            pl.BlockSpec(memory_space=pltpu.SMEM),
            level_spec(RL, CP, NC),
            level_spec(2, CP, NC),
            level_spec(2, CP, NC),
            level_spec(C * RL, NC),
            whole_spec(2 * CP, 9 * CP),
            whole_spec(CP, 9 * CP),
        ],
        out_specs=[
            level_spec(RL + 2, CP, NC),
            level_spec(RL + 2, CO, NC),
            level_spec(RL, CO, NC),
            level_spec(RL, CP, NC),
        ],
        out_shape=[
            shape((LEV, RL + 2, CP, NC), BF),
            shape((LEV, RL + 2, CO, NC), F32),
            shape((LEV, RL, CO, NC), F32),
            shape((LEV, RL, CP, NC), BF),
        ],
        scratch_shapes=[
            pltpu.VMEM((RL + 4, GR, NC), BF),
            pltpu.VMEM((RL + 2, GR, NC), BF),
            pltpu.VMEM((RL + 2, CO, NC), F32),
            pltpu.VMEM((NC // 128, (C + 12) * RL, 128), F32),
        ],
        compiler_params=params(),
        cost_estimate=cost(25),
        name="two_convolutions",
    )(place, rows, f_above, f_below, upstream, w_one, w_two)

    mixed, kept = pl.pallas_call(
        kernel_mix,
        out_shape=[shape((SP, 32, 128), BF), shape((64, 64), F32)],
        compiler_params=params(),
        cost_estimate=cost(3),
        name="mode_mix",
    )(arrived, mode_weight(spec_weight))
    gathered = exchange(mixed).reshape(SP * 32, 128)

    out, slopes, s_top, s_bottom, message = pl.pallas_call(
        kernel_d,
        out_shape=[
            shape((LEV * C * RL, NC), BF),
            shape((LEV, RL, CP, NC), BF),
            strip,
            strip,
            shape((SP * 32, 128), BF),
        ],
        scratch_shapes=[
            pltpu.VMEM((LEV * RL * CO, 128), F32),
            pltpu.VMEM((LEV * RL * CO, NC), F32),
            pltpu.VMEM((NC // 128, LEV * C * RL, 128), F32),
            pltpu.VMEM((LEV * RL * CP, 128), F32),
            pltpu.VMEM((128, 256), F32),
        ],
        compiler_params=params(),
        cost_estimate=cost(15),
        name="output_and_slope",
    )(gathered, phase, high, low, jnp.asarray(INVERSE), pre, cot_rows, table, jnp.asarray(SCALE))
    s_above, s_below = from_above(s_bottom), from_below(s_top)
    arrived = exchange(message.reshape(SP, 32, 128))

    flip_two = jnp.transpose(kernel_two[::-1, ::-1], (0, 1, 3, 2))
    flip_one = jnp.transpose(kernel_one[::-1, ::-1], (0, 1, 3, 2))
    w_two_back = jnp.concatenate(
        [taps_weight(flip_two), centre_weight(jnp.transpose(point_weight))], axis=0
    )
    w_one_back = taps_weight(flip_one)
    back, grad_two, grad_one, grad_point = pl.pallas_call(
        kernel_e,
        grid=(LEV,),
        in_specs=[
            pl.BlockSpec(memory_space=pltpu.SMEM),
            level_spec(RL, CP, NC),
            level_spec(2, CP, NC),
            level_spec(2, CP, NC),
            level_spec(RL + 2, CP, NC),
            level_spec(RL, CP, NC),
            level_spec(2, CP, NC),
            level_spec(2, CP, NC),
            level_spec(RL + 2, CO, NC),
            whole_spec(2 * CP, 9 * CP),
            whole_spec(CP, 9 * CP),
        ],
        out_specs=[
            level_spec(RL, CO, NC),
            whole_spec(GR, GR),
            whole_spec(GR, GR),
            whole_spec(CP, CP),
        ],
        out_shape=[
            shape((LEV, RL, CO, NC), F32),
            shape((GR, GR), F32),
            shape((GR, GR), F32),
            shape((CP, CP), F32),
        ],
        scratch_shapes=[
            pltpu.VMEM((RL + 4, GR, NC), BF),
            pltpu.VMEM((RL + 2, GR, NC), BF),
            pltpu.VMEM((RL + 2, CP, NC), BF),
            pltpu.VMEM((RL + 2, CO, NC), F32),
        ],
        compiler_params=params(),
        cost_estimate=cost(30),
        name="backward_convolutions",
    )(place, slopes, s_above, s_below, middle, rows, f_above, f_below, slope, w_two_back, w_one_back)

    mixed, spec_part = pl.pallas_call(
        kernel_mix_back,
        out_shape=[shape((SP, 32, 128), BF), shape((QN, CP, 128), BF)],
        compiler_params=params(),
        cost_estimate=cost(4),
        name="mode_mix_back",
    )(arrived, mode_weight(jnp.transpose(spec_weight, (0, 2, 1, 3))), kept)
    gathered = exchange(mixed).reshape(SP * 32, 128)
    spec_all = lax.all_gather(spec_part, "rep", axis=0)

    field_grad = pl.pallas_call(
        kernel_f,
        out_shape=shape((LEV * C * RL, NC), BF),
        scratch_shapes=[
            pltpu.VMEM((LEV * RL * CO, 128), F32),
            pltpu.VMEM((LEV * RL * CO, NC), F32),
            pltpu.VMEM((NC // 128, LEV * C * RL, 128), F32),
        ],
        compiler_params=params(),
        cost_estimate=cost(8),
        name="field_gradient",
    )(gathered, phase, high, low, jnp.asarray(BACK), back)

    def wide_rows(x, count):
        return jnp.pad(x, ((0, count - x.shape[0]), (0, 256 - x.shape[1])))

    sums = jnp.concatenate([wide_rows(grad_two, 160), wide_rows(grad_one, 160), wide_rows(grad_point, 192)], axis=0)
    shares = jnp.sum(exchange(sums.reshape(SP, 16, 256)), axis=0)
    shares = jnp.sum(lax.all_gather(shares, "rep", axis=0), axis=0)
    sums = exchange(jnp.broadcast_to(shares[None], (SP, 16, 256))).reshape(SP * 16, 256)
    grad_scale = 1.0 / math.sqrt(NR * NC * LEV * lax.axis_size("rep"))
    sums = sums * grad_scale

    def kernel_shape(x):
        x = x[:GR, :GR].reshape(3, CP, 3, CP)[:, :C, ::-1, :C]
        return jnp.transpose(x, (0, 2, 1, 3))

    spec_sum = jnp.sum(spec_all.astype(F32), axis=0)
    spec_total = jnp.transpose(spec_sum.reshape(QN, CP, 2, 64)[:, :C, :, :C], (2, 1, 3, 0))
    return (
        out.reshape(field.shape),
        field_grad.reshape(field.shape),
        spec_total,
        sums[320 : 320 + C, :C],
        kernel_shape(sums[160:320]),
        kernel_shape(sums[:160]),
    )


def solution(mesh):
    specs = (
        P("rep", None, None, "sp", None),
        P("rep", None, None, "sp", None),
        P(None, None, None, "sp"),
        P(),
        P(),
        P(),
    )
    return jax.shard_map(local, mesh=mesh, in_specs=specs, out_specs=specs, check_vma=False)
```

time: 1080 us -> 185 us (0.17)
  waiting for transfers between devices: 396 us -> 15 us
  local copies, waits for them, and re-layouts: 256 us -> 14.9 us
  blocking collectives: 205 us -> 16.7 us
  matrix products: 143 us -> 0 us
  Pallas kernels: 0 us -> 68.2 us
  starting transfers between devices: 20.5 us -> 64.1 us
  other arithmetic: 40.3 us -> 3.44 us
  between operations: 15.6 us -> 1.02 us
    unnamed x5 -> x0, waiting for transfers between devices: 366 us -> none
    all_gather x2, blocking collectives: 161 us -> 16.7 us  [the longest x1 10.9 us: local(): spec_all = lax.all_gather(spec_part, 'rep', axis=0)]
    conv_general_dilated x25 -> x0, local copies, waits for them, and re-layouts: 116 us -> none  [the longest x17 81.3 us: correlate(): lax.conv_general_dilated(padded, kernel, (1, 1), ((0, 0), (1, 1)), dimens...]
    pallas_call x0 -> x7, Pallas kernels: none -> 68.2 us  [the longest x1 22.1 us: local(): pl.pallas_call(kernel_e, grid=(LEV,), in_specs=[pl.BlockSpec(memory_space...]
    conv_general_dilated x7 -> x0, matrix products: 67.1 us -> none  [the longest x4 43.9 us: correlate(): lax.conv_general_dilated(padded, kernel, (1, 1), ((0, 0), (1, 1)), dimens...]
    concatenate x13 -> x0, local copies, waits for them, and re-layouts: 61.3 us -> none  [the longest x11 60.8 us: padded_2(): jnp.concatenate([lax.ppermute(tail, axis, [(i, (i + 1) % count) for i in...]
    all_to_all x0 -> x6, starting transfers between devices: none -> 53.8 us  [exchange(): return lax.all_to_all(x, 'sp', 0, 0, tiled=True)]
    psum x1 -> x0, blocking collectives: 43.9 us -> none  [local(): lax.psum(own_grad.astype(jnp.bfloat16), 'rep').astype(jnp.float32)]
  transfers between devices with their start and end apart: 11 -> 10, of which waited for: 3 -> 3; matrix products, arithmetic and copies ran while one was open for 29% -> 5% of each run, Pallas kernels for 0% -> 29%
where the time goes in v1:
time: 185 us; the launch traced here: 183 us
  Pallas kernels  68.2 us (37%)
  starting transfers between devices  64.1 us (35%)
  blocking collectives  16.7 us (9%)
  waiting for transfers between devices  15 us (8%)
  local copies, waits for them, and re-layouts  14.9 us (8%)
  other arithmetic  3.44 us (2%)
    all_to_all x6, starting transfers between devices, exchange(): return lax.all_to_all(x, 'sp', 0, 0, tiled=True)  53.8 us
    pallas_call x1, Pallas kernels, local(): pl.pallas_call(kernel_e, grid=(LEV,), in_specs=[pl.BlockSpec(memory_space...  22.1 us
    pallas_call x1, Pallas kernels, local(): pl.pallas_call(kernel_b, grid=(LEV,), in_specs=[pl.BlockSpec(memory_space...  19.4 us
    all_to_all x6, waiting for transfers between devices, exchange(): return lax.all_to_all(x, 'sp', 0, 0, tiled=True)  15 us
    all_gather x1, blocking collectives, local(): spec_all = lax.all_gather(spec_part, 'rep', axis=0)  10.9 us
    pallas_call x1, Pallas kernels, local(): pl.pallas_call(kernel_d, out_shape=[shape((LEV * C * RL, NC), BF), shape(...  9.88 us
    ppermute x2, starting transfers between devices, from_above(): return lax.ppermute(x, 'sp', [(i, i + 1) for i in range(SP - 1)])  7.66 us
    pallas_call x1, Pallas kernels, local(): pl.pallas_call(kernel_f, out_shape=shape((LEV * C * RL, NC), BF), scratch...  6.13 us
  transfers between devices with their start and end apart: 10, of which 3 were waited for; matrix products, arithmetic and copies ran while one was open for 5% of the time, Pallas kernels for 29%

profile of v1, /device:TPU:1, one launch (start us, length us, event | category | flops | bytes accessed | tf_op | source)
XLA Modules:
  0.0 183.3 jit_solution(9654389140297836461)
XLA Ops:
  0.6 1.9 %dynamic-slice_bitcast_fusion.phase = f32[1024,2]{1,0:T(8,128)} fusion(f32[32,1024,2]{2,1,0:T(8,128)} %constant.32.clone, s32[]{:T(128)S(6)} %select_n.4), kind=kLoop, calls=%fused_computation.7 | loop fusion | bytes 16388 | tf_op jit(solution)/shard_map/jit(dynamic_index_in_dim)/squeeze | solution.py:404
  2.6 5.8 %field_modes.1 = (bf16[1024,128]{1,0:T(8,128)(2,1)}, bf16[2,8,48,1024]{3,2,1,0:T(8,128)(2,1)}, bf16[2,2,48,1024]{3,2,1,0:T(8,128)(2,1)}, bf16[2,2,48,1024]{3,2,1,0:T(8,128)(2,1)}) custom-call(bf16[576,1024]{1,0:T(8,128)(2,1)} %bitcast.57, bf16[1024,128]{1,0:T(8,128)(2,1)} %constant.33.clone.table, bf16[1024,256]{1,0:T(8,128)(2,1)} %constant.34.clone.high, ...), custom_call_target="tpu_custom_call" | custom-call | flops 8000000000 | bytes 24000000 | tf_op jit(solution)/shard_map/field_modes/pallas_call | solution.py:407
  8.4 4.5 %collective-permute-start = (bf16[2,2,48,1024]{3,2,1,0:T(8,128)(2,1)}, bf16[2,2,48,1024]{3,2,1,0:T(8,128)(2,1)S(1)}, u32[]{:S(2)}, u32[]{:S(2)}) collective-permute-start(bf16[2,2,48,1024]{3,2,1,0:T(8,128)(2,1)} %get-tuple-element.30), channel_id=1, source_target_pairs={{0,1},{1,2},{2,3},{3,4},{4,5},{5,6},{6,7},{7,8},{8,9},{9,10},{10,1... | collective-permute-start | bytes 1179656 | tf_op jit(solution)/shard_map/ppermute | solution.py:388
  12.9 1.3 collective-permute-start.1
  14.2 11.1 %all-to-all-start = ((bf16[32,32,128]{2,1,0:T(8,128)(2,1)}), bf16[32,32,128]{2,1,0:T(8,128)(2,1)S(1)}, u32[]{:S(2)}, u32[]{:S(2)}) async-start(bf16[32,32,128]{2,1,0:T(8,128)(2,1)} %bitcast.53), calls=%async_computation | async-start | bytes 524288 | tf_op jit(solution)/shard_map/all_to_all | solution.py:396
  26.9 0.8 copy.56.weight
  27.7 0.7 fusion.3.w_one
  28.4 6.4 %all-to-all-done.received = bf16[32,32,128]{2,1,0:T(8,128)(2,1)S(1)} async-done(((bf16[32,32,128]{2,1,0:T(8,128)(2,1)}), bf16[32,32,128]{2,1,0:T(8,128)(2,1)S(1)}, u32[]{:S(2)}, u32[]{:S(2)}) %all-to-all-start) | async-done | bytes 262176 | tf_op jit(solution)/shard_map/all_to_all | solution.py:396
  35.6 2.4 %mode_mix.1 = (bf16[32,32,128]{2,1,0:T(8,128)(2,1)}, f32[64,64]{1,0:T(8,128)}) custom-call(bf16[32,32,128]{2,1,0:T(8,128)(2,1)} %copy-done.6, f32[9,64,128]{2,1,0:T(8,128)} %copy.56.weight), custom_call_target="tpu_custom_call" | custom-call | flops 3000000000 | bytes 9000000 | tf_op jit(solution)/shard_map/mode_mix/pallas_call | solution.py:459
  38.0 7.0 %all-to-all-start.1 = ((bf16[32,32,128]{2,1,0:T(8,128)(2,1)}), bf16[32,32,128]{2,1,0:T(8,128)(2,1)S(1)}, u32[]{:S(2)}, u32[]{:S(2)}) async-start(bf16[32,32,128]{2,1,0:T(8,128)(2,1)} %get-tuple-element.28), calls=%async_computation.1 | async-start | bytes 524288 | tf_op jit(solution)/shard_map/all_to_all | solution.py:396
  45.1 0.7 copy-done.8
  45.9 19.4 %two_convolutions.1 = (bf16[2,10,48,1024]{3,2,1,0:T(8,128)(2,1)}, f32[2,10,40,1024]{3,2,1,0:T(8,128)}, f32[2,8,40,1024]{3,2,1,0:T(8,128)}, bf16[2,8,48,1024]{3,2,1,0:T(8,128)(2,1)}) custom-call(s32[1]{0:T(128)} %bitcast.5.place, bf16[2,8,48,1024]{3,2,1,0:T(8,128)(2,1)} %get-tuple-element.29.rows, bf16[2,2,48,1024]{3,2,1,0:T(8,128)(2,1)} %copy-done.8, ...), custom_call_target="tpu_custom_call" | custom-call | flops 24999999488 | bytes 75000000 | tf_op jit(solution)/shard_map/two_convolutions/pallas_call | solution.py:424
  66.0 9.9 %output_and_slope.1 = (bf16[576,1024]{1,0:T(8,128)(2,1)}, bf16[2,8,48,1024]{3,2,1,0:T(8,128)(2,1)}, bf16[2,2,48,1024]{3,2,1,0:T(8,128)(2,1)}, bf16[2,2,48,1024]{3,2,1,0:T(8,128)(2,1)}, bf16[1024,128]{1,0:T(8,128)(2,1)}) custom-call(bf16[1024,128]{1,0:T(8,128)(2,1)} %bitcast.54, f32[1024,2]{1,0:T(8,128)} %dynamic-slice_bitcast_fusion.phase, ...), custom_call_target="tpu_custom_call" | custom-call | flops 15000000512 | bytes 45000000 | tf_op jit(solution)/shard_map/output_and_slope/pallas_call | solution.py:468
  75.9 3.1 %collective-permute-start.2 = (bf16[2,2,48,1024]{3,2,1,0:T(8,128)(2,1)}, bf16[2,2,48,1024]{3,2,1,0:T(8,128)(2,1)S(1)}, u32[]{:S(2)}, u32[]{:S(2)}) collective-permute-start(bf16[2,2,48,1024]{3,2,1,0:T(8,128)(2,1)} %get-tuple-element.39), channel_id=1, source_target_pairs={{0,1},{1,2},{2,3},{3,4},{4,5},{5,6},{6,7},{7,8},{8,9},{9,10},{10,1... | collective-permute-start | bytes 1179656 | tf_op jit(solution)/shard_map/ppermute | solution.py:388
  79.0 1.3 collective-permute-start.3
  80.6 0.7 reshape.86.w_one
  81.9 1.1 reshape.83.weight
  82.9 0.7 fusion.4.w_two
  83.7 11.3 %all-to-all-start.2 = ((bf16[32,32,128]{2,1,0:T(8,128)(2,1)}), bf16[32,32,128]{2,1,0:T(8,128)(2,1)S(1)}, u32[]{:S(2)}, u32[]{:S(2)}) async-start(bf16[32,32,128]{2,1,0:T(8,128)(2,1)} %bitcast.13), calls=%async_computation.2 | async-start | bytes 524288 | tf_op jit(solution)/shard_map/all_to_all | solution.py:396
  95.8 22.1 %backward_convolutions.1 = (f32[2,8,40,1024]{3,2,1,0:T(8,128)}, f32[144,144]{1,0:T(8,128)}, f32[144,144]{1,0:T(8,128)}, f32[48,48]{1,0:T(8,128)}) custom-call(s32[1]{0:T(128)} %bitcast.5.place, bf16[2,8,48,1024]{3,2,1,0:T(8,128)(2,1)} %get-tuple-element.38.slopes, bf16[2,2,48,1024]{3,2,1,0:T(8,128)(2,1)} %copy-done.10, bf16[2,2,48,1024]{3,2,1,0:T(8,128)(2,1)} %copy-done.11, ...), custom_call_target="tpu_custom_call" | custom-call | flops 30000001024 | bytes 90000000 | tf_op jit(solution)/shard_map/backward_convolutions/pallas_call | solution.py:497
  118.0 1.8 select_maximum_fusion
  119.8 9.4 %all-to-all-start.4 = ((f32[32,16,256]{2,1,0:T(8,128)}), f32[32,16,256]{2,1,0:T(8,128)S(1)}, u32[]{:S(2)}, u32[]{:S(2)}) async-start(f32[32,16,256]{2,1,0:T(8,128)} %bitcast.25), calls=%async_computation.4 | async-start | bytes 1048576 | tf_op jit(solution)/shard_map/all_to_all | solution.py:396
  129.2 2.5 %mode_mix_back.1 = (bf16[32,32,128]{2,1,0:T(8,128)(2,1)}, bf16[9,48,128]{2,1,0:T(8,128)(2,1)}) custom-call(bf16[32,32,128]{2,1,0:T(8,128)(2,1)} %copy-done.3, f32[9,64,128]{2,1,0:T(8,128)} %reshape.83.weight, f32[64,64]{1,0:T(8,128)} %get-tuple-element.36.kept), custom_call_target="tpu_custom_call" | custom-call | flops 4000000000 | bytes 12000000 | tf_op jit(solution)/shard_map/mode_mix_back/pallas_call | solution.py:536
  131.7 10.9 %all-gather = bf16[36,48,128]{2,1,0:T(8,128)(2,1)S(1)} all-gather(bf16[9,48,128]{2,1,0:T(8,128)(2,1)} %get-tuple-element.44), channel_id=2, replica_groups=mesh['rep'=4,'sp'=32] {'rep'}, dimensions={0}, use_global_device_ids=true | all-gather | bytes 552960 | tf_op jit(solution)/shard_map/all_gather | solution.py:544
  143.0 8.8 %all-to-all-start.3 = ((bf16[32,32,128]{2,1,0:T(8,128)(2,1)}), bf16[32,32,128]{2,1,0:T(8,128)(2,1)S(1)}, u32[]{:S(2)}, u32[]{:S(2)}) async-start(bf16[32,32,128]{2,1,0:T(8,128)(2,1)} %get-tuple-element.37), calls=%async_computation.3 | async-start | bytes 524288 | tf_op jit(solution)/shard_map/all_to_all | solution.py:396
  151.8 0.8 copy.53
  152.7 5.8 %all-gather.1 = f32[64,256]{1,0:T(8,128)S(1)} all-gather(f32[16,256]{1,0:T(8,128)S(1)} %reduce_sum.28), channel_id=3, replica_groups=mesh['rep'=4,'sp'=32] {'rep'}, dimensions={0}, use_global_device_ids=true | all-gather | bytes 81920 | tf_op jit(solution)/shard_map/all_gather | solution.py:564
  158.5 3.1 %all-to-all-done.3 = bf16[32,32,128]{2,1,0:T(8,128)(2,1)S(1)} async-done(((bf16[32,32,128]{2,1,0:T(8,128)(2,1)}), bf16[32,32,128]{2,1,0:T(8,128)(2,1)S(1)}, u32[]{:S(2)}, u32[]{:S(2)}) %all-to-all-start.3) | async-done | bytes 262176 | tf_op jit(solution)/shard_map/all_to_all | solution.py:396
  161.6 0.9 broadcast_in_dim.2
  162.4 6.2 %all-to-all-start.5 = ((f32[32,16,256]{2,1,0:T(8,128)}), f32[32,16,256]{2,1,0:T(8,128)S(1)}, u32[]{:S(2)}, u32[]{:S(2)}) async-start(f32[32,16,256]{2,1,0:T(8,128)} %broadcast_in_dim.2), calls=%async_computation.5 | async-start | bytes 1048576 | tf_op jit(solution)/shard_map/all_to_all | solution.py:396
  168.7 6.1 %field_gradient.1 = bf16[576,1024]{1,0:T(8,128)(2,1)} custom-call(bf16[1024,128]{1,0:T(8,128)(2,1)} %bitcast.55, f32[1024,2]{1,0:T(8,128)} %dynamic-slice_bitcast_fusion.phase, bf16[1024,256]{1,0:T(8,128)(2,1)} %constant.34.clone.high, bf16[1024,256]{1,0:T(8,128)(2,1)} %constant.35.clone.low, bf16[128,1024]{1,0:T(8,128)(2,1)} %constant.38.clone.inverse, ...), custom_call_target="tpu_custom_call" | custom-call | flops 8000000000 | bytes 24000000 | tf_op jit(solution)/shard_map/field_gradient/pallas_call | solution.py:546
  174.8 5.4 %all-to-all-done.5 = f32[32,16,256]{2,1,0:T(8,128)S(1)} async-done(((f32[32,16,256]{2,1,0:T(8,128)}), f32[32,16,256]{2,1,0:T(8,128)S(1)}, u32[]{:S(2)}, u32[]{:S(2)}) %all-to-all-start.5) | async-done | bytes 524320 | tf_op jit(solution)/shard_map/all_to_all | solution.py:396
  (64 shorter events, 8.1 us)
Async XLA Ops:
  2.6 22.7 %copy-start.7 = (bf16[36,36]{1,0:T(8,128)(2,1)S(1)}, bf16[36,36]{1,0:T(8,128)(2,1)}, u32[]{:S(2)}) copy-start(bf16[36,36]{1,0:T(8,128)(2,1)} %param.16) | copy-start | bytes 7780
  2.6 22.9 %copy-start.1 = (bf16[3,3,36,36]{3,2,1,0:T(8,128)(2,1)S(1)}, bf16[3,3,36,36]{3,2,1,0:T(8,128)(2,1)}, u32[]{:S(2)}) copy-start(bf16[3,3,36,36]{3,2,1,0:T(8,128)(2,1)} %param.18) | copy-start | bytes 69988
  2.6 22.9 %copy-start.2 = (bf16[3,3,36,36]{3,2,1,0:T(8,128)(2,1)S(1)}, bf16[3,3,36,36]{3,2,1,0:T(8,128)(2,1)}, u32[]{:S(2)}) copy-start(bf16[3,3,36,36]{3,2,1,0:T(8,128)(2,1)} %param.17) | copy-start | bytes 69988
  8.4 18.0 %copy-start = (f32[2,36,36,9]{2,0,3,1:T(2,128)S(1)}, f32[2,36,36,9]{2,0,3,1:T(2,128)}, u32[]{:S(2)}) copy-start(f32[2,36,36,9]{2,0,3,1:T(2,128)} %param.15) | copy-start | bytes 279940
  8.4 36.6 %collective-permute-start = (bf16[2,2,48,1024]{3,2,1,0:T(8,128)(2,1)}, bf16[2,2,48,1024]{3,2,1,0:T(8,128)(2,1)S(1)}, u32[]{:S(2)}, u32[]{:S(2)}) collective-permute-start(bf16[2,2,48,1024]{3,2,1,0:T(8,128)(2,1)} %get-tuple-element.30), channel_id=1, source_target_pairs={{0,1},{1,2},{2,3},{3,4},{4,5},{5,6},{6,7},{7,8},{8,9},{9,10},{10,1... | collective-permute-start | bytes 1179656 | tf_op jit(solution)/shard_map/ppermute | solution.py:388
  12.9 32.1 %collective-permute-start.1 = (bf16[2,2,48,1024]{3,2,1,0:T(8,128)(2,1)}, bf16[2,2,48,1024]{3,2,1,0:T(8,128)(2,1)S(1)}, u32[]{:S(2)}, u32[]{:S(2)}) collective-permute-start(bf16[2,2,48,1024]{3,2,1,0:T(8,128)(2,1)} %get-tuple-element.31), channel_id=1, source_target_pairs={{1,0},{2,1},{3,2},{4,3},{5,4},{6,5},{7,6},{8,7},{9,8},{10,9},{11,1... | collective-permute-start | bytes 1179656 | tf_op jit(solution)/shard_map/ppermute | solution.py:392
  14.2 20.7 %all-to-all-start = ((bf16[32,32,128]{2,1,0:T(8,128)(2,1)}), bf16[32,32,128]{2,1,0:T(8,128)(2,1)S(1)}, u32[]{:S(2)}, u32[]{:S(2)}) async-start(bf16[32,32,128]{2,1,0:T(8,128)(2,1)} %bitcast.53), calls=%async_computation | async-start | bytes 524288 | tf_op jit(solution)/shard_map/all_to_all | solution.py:396
  34.9 0.7 copy-start.6
  38.0 27.3 %all-to-all-start.1 = ((bf16[32,32,128]{2,1,0:T(8,128)(2,1)}), bf16[32,32,128]{2,1,0:T(8,128)(2,1)S(1)}, u32[]{:S(2)}, u32[]{:S(2)}) async-start(bf16[32,32,128]{2,1,0:T(8,128)(2,1)} %get-tuple-element.28), calls=%async_computation.1 | async-start | bytes 524288 | tf_op jit(solution)/shard_map/all_to_all | solution.py:396
  45.0 0.8 copy-start.8
  45.0 0.9 copy-start.9
  65.3 0.7 copy-start.4
  75.9 19.1 %collective-permute-start.2 = (bf16[2,2,48,1024]{3,2,1,0:T(8,128)(2,1)}, bf16[2,2,48,1024]{3,2,1,0:T(8,128)(2,1)S(1)}, u32[]{:S(2)}, u32[]{:S(2)}) collective-permute-start(bf16[2,2,48,1024]{3,2,1,0:T(8,128)(2,1)} %get-tuple-element.39), channel_id=1, source_target_pairs={{0,1},{1,2},{2,3},{3,4},{4,5},{5,6},{6,7},{7,8},{8,9},{9,10},{10,1... | collective-permute-start | bytes 1179656 | tf_op jit(solution)/shard_map/ppermute | solution.py:388
  79.0 15.9 %collective-permute-start.3 = (bf16[2,2,48,1024]{3,2,1,0:T(8,128)(2,1)}, bf16[2,2,48,1024]{3,2,1,0:T(8,128)(2,1)S(1)}, u32[]{:S(2)}, u32[]{:S(2)}) collective-permute-start(bf16[2,2,48,1024]{3,2,1,0:T(8,128)(2,1)} %get-tuple-element.40), channel_id=1, source_target_pairs={{1,0},{2,1},{3,2},{4,3},{5,4},{6,5},{7,6},{8,7},{9,8},{10,9},{11,1... | collective-permute-start | bytes 1179656 | tf_op jit(solution)/shard_map/ppermute | solution.py:392
  83.7 36.1 %all-to-all-start.2 = ((bf16[32,32,128]{2,1,0:T(8,128)(2,1)}), bf16[32,32,128]{2,1,0:T(8,128)(2,1)S(1)}, u32[]{:S(2)}, u32[]{:S(2)}) async-start(bf16[32,32,128]{2,1,0:T(8,128)(2,1)} %bitcast.13), calls=%async_computation.2 | async-start | bytes 524288 | tf_op jit(solution)/shard_map/all_to_all | solution.py:396
  94.9 0.7 copy-start.10
  95.0 0.9 copy-start.11
  119.8 9.4 %copy-start.3 = (bf16[32,32,128]{2,1,0:T(8,128)(2,1)}, bf16[32,32,128]{2,1,0:T(8,128)(2,1)S(1)}, u32[]{:S(2)}) copy-start(bf16[32,32,128]{2,1,0:T(8,128)(2,1)S(1)} %all-to-all-done.2.received) | copy-start | bytes 786436
  119.8 23.2 %all-to-all-start.4 = ((f32[32,16,256]{2,1,0:T(8,128)}), f32[32,16,256]{2,1,0:T(8,128)S(1)}, u32[]{:S(2)}, u32[]{:S(2)}) async-start(f32[32,16,256]{2,1,0:T(8,128)} %bitcast.25), calls=%async_computation.4 | async-start | bytes 1048576 | tf_op jit(solution)/shard_map/all_to_all | solution.py:396
  143.0 18.6 %all-to-all-start.3 = ((bf16[32,32,128]{2,1,0:T(8,128)(2,1)}), bf16[32,32,128]{2,1,0:T(8,128)(2,1)S(1)}, u32[]{:S(2)}, u32[]{:S(2)}) async-start(bf16[32,32,128]{2,1,0:T(8,128)(2,1)} %get-tuple-element.37), calls=%async_computation.3 | async-start | bytes 524288 | tf_op jit(solution)/shard_map/all_to_all | solution.py:396
  161.5 7.1 %copy-start.5 = (bf16[32,32,128]{2,1,0:T(8,128)(2,1)}, bf16[32,32,128]{2,1,0:T(8,128)(2,1)S(1)}, u32[]{:S(2)}) copy-start(bf16[32,32,128]{2,1,0:T(8,128)(2,1)S(1)} %all-to-all-done.3) | copy-start | bytes 786436
  162.4 17.8 %all-to-all-start.5 = ((f32[32,16,256]{2,1,0:T(8,128)}), f32[32,16,256]{2,1,0:T(8,128)S(1)}, u32[]{:S(2)}, u32[]{:S(2)}) async-start(f32[32,16,256]{2,1,0:T(8,128)} %broadcast_in_dim.2), calls=%async_computation.5 | async-start | bytes 1048576 | tf_op jit(solution)/shard_map/all_to_all | solution.py:396

commit v2 on v1

v2 whole, which is shorter than its diff:
```python
import math

import jax
import jax.numpy as jnp
import numpy as np
import ml_dtypes
from jax import lax
from jax.experimental import pallas as pl
from jax.experimental.pallas import tpu as pltpu
from jax.sharding import PartitionSpec as P

M = 12
C = 36
CP = 48
CO = 40
LEV = 2
RL = 8
NC = 1024
NR = 256
SP = 32
QN = 9
GR = 3 * CP

ROOT_HALF = 0.7071067811865476
INV_ROOT_TAU = 0.3989422804014327
BF = jnp.bfloat16
F32 = jnp.float32


def split_np(values):
    high = values.astype(np.float32).astype(ml_dtypes.bfloat16)
    low = (values - high.astype(np.float64)).astype(np.float32).astype(ml_dtypes.bfloat16)
    return high, low


def make_tables():
    n = np.arange(NC)[:, None]
    k = np.arange(M)[None, :]
    t = 2.0 * np.pi * ((n * k) % NC) / NC
    forward = np.concatenate([np.cos(t), -np.sin(t)], axis=1)
    doubled = np.where(np.arange(M) == 0, 1.0, 2.0)
    doubled = np.concatenate([doubled, doubled]) / (NR * NC)
    table = np.zeros((NC, 128), np.float32)
    table[:, :24] = forward
    table = table.astype(ml_dtypes.bfloat16)

    def inverse(matrix):
        high, low = split_np(matrix.T)
        out = np.zeros((128, NC), ml_dtypes.bfloat16)
        out[0:24], out[24:48], out[48:72] = high, low, high
        return out

    rows = np.zeros((SP, 2, 16, 256))
    freq = np.where(np.arange(24) < M, np.arange(24), NR - 24 + np.arange(24))
    mode_row = np.zeros((SP, 2, 16, 32))
    for owner in range(SP):
        for q in range(QN):
            mode = owner * QN + q
            j, kk = mode // M, mode % M
            for r in range(RL):
                p = 2.0 * np.pi * ((freq[j] * r) % NR) / NR
                rows[owner, 0, q, r * 24 + kk] = np.cos(p)
                rows[owner, 0, q, r * 24 + 12 + kk] = np.sin(p)
                rows[owner, 1, q, r * 24 + kk] = -np.sin(p)
                rows[owner, 1, q, r * 24 + 12 + kk] = np.cos(p)
            mode_row[owner, :, q, j] = 1.0
    high, low = split_np(rows.reshape(SP * 32, 256))
    scale = np.zeros((1, 256), np.float32)
    scale[0, :192] = np.tile(doubled, RL)
    return (
        table,
        inverse(forward * doubled[None, :]),
        inverse(forward),
        high,
        low,
        mode_row.reshape(SP * 32, 32).astype(ml_dtypes.bfloat16),
        scale,
    )


TABLE, INVERSE, BACK, ROW_HIGH, ROW_LOW, MODE_ROW, SCALE = make_tables()


def dot(a, b):
    return lax.dot_general(a, b, (((1,), (0,)), ((), ())), preferred_element_type=F32)


def dot_nt(a, b):
    return lax.dot_general(a, b, (((1,), (1,)), ((), ())), preferred_element_type=F32)


def dot_tn(a, b):
    return lax.dot_general(a, b, (((0,), (0,)), ((), ())), preferred_element_type=F32)


def split(values):
    high = values.astype(BF)
    return high, (values - high.astype(F32)).astype(BF)


def gelu_parts(v):
    cdf = 0.5 * (1.0 + lax.erf(v * ROOT_HALF))
    return v * cdf, cdf + v * jnp.exp(-0.5 * v * v) * INV_ROOT_TAU


def store_taps(taps, i, x):
    col = lax.broadcasted_iota(jnp.int32, (CP, NC), 1)
    taps[i, 0:CP] = jnp.where(col == 0, 0.0, pltpu.roll(x, 1, 1)).astype(BF)
    taps[i, CP : 2 * CP] = x.astype(BF)
    taps[i, 2 * CP : 3 * CP] = jnp.where(col == NC - 1, 0.0, pltpu.roll(x, NC - 1, 1)).astype(BF)


def row_transform(cols, high, low):
    c_high, c_low = split(cols)
    return (dot_nt(high, c_high) + dot_nt(high, c_low) + dot_nt(low, c_high)).astype(BF)


def row_expand(modes, high, low):
    return dot_tn(modes, high) + dot_tn(modes, low)


def place_rows(rows, left):
    high, low = split(rows)
    high, low = high.astype(F32), low.astype(F32)
    left[...] = jnp.zeros_like(left)
    for lev in range(LEV):
        for r in range(RL):
            at = (lev * RL + r) * CO
            h = high[lev * 64 : lev * 64 + CO, r * 24 : r * 24 + 24]
            w = low[lev * 64 : lev * 64 + CO, r * 24 : r * 24 + 24]
            left[at : at + CO, 0:72] = jnp.concatenate([h, h, w], axis=1)


def kernel_a(place, field, table, high, low, mode_row, message, own_high, own_low, flat, cols):
    j = lax.broadcasted_iota(jnp.int32, (32, 128), 0)
    turn = ((j + jnp.where(j < M, 0, NR - 24)) * place[0]) % SP
    angle = turn.astype(F32) * (2.0 * math.pi / SP)
    t_high, t_low = split(jnp.concatenate([jnp.cos(angle), jnp.sin(angle)], axis=1))
    phase = (dot(mode_row[...], t_high) + dot(mode_row[...], t_low)).reshape(SP, 2, 16, 256)[:, 0]
    cosine, sine = phase[:, :, 0:128], phase[:, :, 128:256]
    cosine, sine = jnp.concatenate([cosine, cosine], axis=2), jnp.concatenate([sine, sine], axis=2)
    first = (high[...].astype(F32) + low[...].astype(F32)).reshape(SP, 2, 16, 256)
    re, im = first[:, 0], first[:, 1]
    turned = jnp.concatenate([(re * cosine + im * sine)[:, None], (im * cosine - re * sine)[:, None]], axis=1)
    h, w = split(turned.reshape(SP * 32, 256))
    own_high[...], own_low[...] = h, w
    flat[...] = dot(field[...], table[...])
    cols[...] = jnp.zeros_like(cols)
    for lev in range(LEV):
        for r in range(RL):
            part = flat[pl.ds(lev * C * RL + r, C, stride=RL), :]
            cols[lev * 64 : lev * 64 + C, r * 24 : r * 24 + 24] = part[:, 0:24]
    message[...] = row_transform(cols[...], h, w)


def prepare(one, two, point, w_one, w_two, w_two_back, w_one_back, w_point, w_point_back, base, wide):
    def spread(target, rows):
        wide[...] = jnp.zeros_like(wide)
        for t in range(4):
            wide[t * CP : (t + 1) * CP, t * rows : t * rows + base.shape[1]] = base[...]
        target[...] = wide[:, 0 : target.shape[1]].astype(BF)

    for kernel, forward, backward in ((one, w_one, w_one_back), (two, w_two, w_two_back)):
        base[...] = jnp.zeros_like(base)
        for a in range(3):
            for b in range(3):
                at = (a * 3 + b) * CP
                base[0:C, at : at + C] = jnp.transpose(kernel[a, b].astype(F32))
        spread(forward, GR)
        for a in range(3):
            for b in range(3):
                at = ((2 - a) * 3 + 2 - b) * CP
                base[0:C, at : at + C] = kernel[a, b].astype(F32)
        spread(backward, GR)
    for target, matrix in ((w_point, jnp.transpose(point[...].astype(F32))), (w_point_back, point[...].astype(F32))):
        wide[...] = jnp.zeros_like(wide)
        for t in range(4):
            wide[t * CP : t * CP + C, t * CP : t * CP + C] = matrix
        target[...] = wide[:, 0 : 4 * CP].astype(BF)


def kernel_rows(field, cot, one, two, point, after, rows, top, bottom, cot_rows, w_one, w_two, w_two_back, w_one_back, w_point, w_point_back, wide, base, spread):
    prepare(one, two, point, w_one, w_two, w_two_back, w_one_back, w_point, w_point_back, base, spread)
    for source, target in ((field, rows), (cot, cot_rows)):
        for n in range(0, NC, 128):
            wide[n // 128, 0 : LEV * C * RL, :] = source[:, n : n + 128].astype(F32)
            wide[n // 128, LEV * C * RL :, :] = jnp.zeros((12 * RL, 128), F32)
        for lev in range(LEV):
            for r in range(RL):
                for n in range(0, NC, 128):
                    x = wide[n // 128, pl.ds(lev * C * RL + r, CP, stride=RL), :].astype(BF)
                    target[lev, r, :, n : n + 128] = x
                    if target is rows and r < 2:
                        top[lev, r, :, n : n + 128] = x
                    if target is rows and r >= RL - 2:
                        bottom[lev, r - RL + 2, :, n : n + 128] = x


def window(ref, i, count):
    return ref[i : i + count].reshape(count * GR, NC)


def kernel_b(place, rows, above, below, w_one, w_two, w_point, after, mid_taps, slope, pre, taps):
    index = place[0]
    source = [above.at[0, 0], above.at[0, 1]] + [rows.at[0, r] for r in range(RL)] + [below.at[0, 0], below.at[0, 1]]
    for i, x in enumerate(source):
        store_taps(taps, i, x[...].astype(F32))
    rest = jnp.zeros((CP - CO, NC), F32)
    for start, count in ((0, 4), (4, 3), (7, 3)):
        d = dot(w_one[0 : CP * count, 0 : GR * (count + 2)], window(taps, start, count + 2))
        for t in range(count):
            i = start + t
            value, gradient = gelu_parts(d[t * CP : t * CP + CO])
            if i in (0, RL + 1):
                keep = jnp.where(index == (0 if i == 0 else SP - 1), 0.0, 1.0).astype(F32)
                value, gradient = value * keep, gradient * keep
            slope[0, i] = gradient
            store_taps(mid_taps.at[0], i, jnp.concatenate([value, rest], axis=0))
    for r in (0, 4):
        d = dot(w_two[...], window(mid_taps.at[0], r, 6))
        d = d + dot(w_point[...], rows[0, r : r + 4].reshape(4 * CP, NC))
        for t in range(4):
            pre[0, r + t] = d[t * CP : t * CP + CO]


def own_modes(received):
    return jnp.sum(received.astype(F32), axis=0)


def by_channel(own, real, imag):
    rest = jnp.zeros((96, 128), F32)
    real[...] = jnp.transpose(jnp.concatenate([own, rest], axis=0))
    imag[...] = jnp.transpose(jnp.concatenate([own[16:32], own[0:16], rest], axis=0))


def weight_rows(weight, lines):
    lines[...] = jnp.zeros_like(lines)
    lines[:, 0:C] = weight[...]


def mode_line(lines, q, part):
    return lines[pl.ds(2 * q + part, C, stride=2 * QN), :]


def kernel_mix(received, weight, message, kept, real, imag, mixed, lines):
    own = own_modes(received[...])
    kept[...] = own
    by_channel(own, real, imag)
    weight_rows(weight, lines)
    mixed[...] = jnp.zeros_like(mixed)
    for q in range(QN):
        w_re, w_im = mode_line(lines, q, 0), mode_line(lines, q, 1)
        re, im = [], []
        for lev in range(LEV):
            s_re = real[lev * 64 : lev * 64 + C, q : q + 1]
            s_im = imag[lev * 64 : lev * 64 + C, q : q + 1]
            re.append(jnp.sum(w_re * s_re - w_im * s_im, axis=0, keepdims=True))
            im.append(jnp.sum(w_im * s_re + w_re * s_im, axis=0, keepdims=True))
        mixed[q : q + 1] = re[0] + pltpu.roll(re[1], 64, 1)
        mixed[16 + q : 17 + q] = im[0] + pltpu.roll(im[1], 64, 1)
    message[...] = jnp.broadcast_to(mixed[0:32].astype(BF)[None], (SP, 32, 128))


def mix_back(own, lines, mixed):
    other = pltpu.roll(own, 64, 1)
    mixed[...] = jnp.zeros_like(mixed)
    for q in range(QN):
        w_re, w_im = mode_line(lines, q, 0), mode_line(lines, q, 1)
        for lev, z in enumerate((own, other)):
            z_re, z_im = z[q : q + 1], z[16 + q : 17 + q]
            at = lev * 64
            mixed[at : at + C, q : q + 1] = jnp.sum(w_re * z_re + w_im * z_im, axis=1, keepdims=True)
            mixed[at : at + C, 16 + q : 17 + q] = jnp.sum(w_re * z_im - w_im * z_re, axis=1, keepdims=True)
    return jnp.transpose(mixed[...])[0:32].astype(BF)


def kernel_spec_grad(p0, p1, p2, p3, after, grad, s_re, s_im, lines):
    pairs = (p0, p1, p2, p3)
    co = []
    for i, pair in enumerate(pairs):
        by_channel(pair[0:32], s_re.at[i], s_im.at[i])
        co.append((pair[32:64], pltpu.roll(pair[32:64], 64, 1)))
    for q in range(QN):
        res, ims = [], []
        for i in range(4):
            re, im = jnp.zeros((C, 128), F32), jnp.zeros((C, 128), F32)
            for lev in range(LEV):
                at = lev * 64
                a, b = s_re[i, at : at + C, q : q + 1], s_im[i, at : at + C, q : q + 1]
                x, y = co[i][lev][q : q + 1], co[i][lev][16 + q : 17 + q]
                re = re + (a * x + b * y)
                im = im + (a * y - b * x)
            res.append(re)
            ims.append(im)
        lines[pl.ds(2 * q, C, stride=2 * QN), :] = (res[0] + res[1]) + (res[2] + res[3])
        lines[pl.ds(2 * q + 1, C, stride=2 * QN), :] = (ims[0] + ims[1]) + (ims[2] + ims[3])
    grad[...] = lines[:, 0:C]


def kernel_share(gathered, first, second, share):
    share[...] = jnp.sum(gathered[:, 32:48].astype(F32), axis=0)


def kernel_d(received, high, low, inverse, pre, cot, table, scale, values, slopes, top, bottom, message, left, spec, kept, cols):
    lev = pl.program_id(0)

    @pl.when(lev == 0)
    def _():
        place_rows(row_expand(received[...], high[...], low[...]), left)
        spec[...] = dot(left[...].astype(BF), inverse[...]).reshape(LEV * RL, CO, NC)
        cols[...] = jnp.zeros_like(cols)

    rest = jnp.zeros((CP - CO, NC), F32)
    for r in range(RL):
        value, gradient = gelu_parts(pre[0, r] + spec[lev * RL + r])
        values[0, r] = jnp.concatenate([value, rest], axis=0).astype(BF)
        s = jnp.concatenate([gradient, rest], axis=0) * cot[0, r].astype(F32)
        s = s.astype(BF)
        slopes[0, r] = s
        if r < 2:
            top[0, r] = s
        if r >= RL - 2:
            bottom[0, r - RL + 2] = s
    kept[lev] = dot(slopes[0].reshape(RL * CP, NC), table[...])

    @pl.when(lev == LEV - 1)
    def _():
        for at in range(LEV):
            for r in range(RL):
                cols[at * 64 : at * 64 + CO, r * 24 : r * 24 + 24] = kept[at, r * CP : r * CP + CO, 0:24]
        message[...] = row_transform(cols[...] * scale[...], high[...], low[...])


def kernel_out(values, after, out, wide):
    for lev in range(LEV):
        for r in range(RL):
            for n in range(0, NC, 128):
                x = values[lev, r, :, n : n + 128].astype(F32)
                wide[n // 128, pl.ds(lev * C * RL + r, C, stride=RL), :] = x[0:C]
    for n in range(0, NC, 128):
        out[:, n : n + 128] = wide[n // 128].astype(BF)


def kernel_mix_back(received, weight, kept, cofield, pair, mixed, lines):
    own = own_modes(received[...])
    pair[0:32] = kept[...]
    pair[32:64] = own
    weight_rows(weight, lines)
    cofield[...] = mix_back(own, lines, mixed)


def kernel_e_zero(slopes, mid_taps, rows, grad_two):
    none = jnp.zeros((CP, NC), BF)
    left, right = [], []
    for i in range(RL + 2):
        inside = 1 <= i <= RL
        left.append(jnp.concatenate([mid_taps[0, i], rows[0, i - 1] if inside else none], axis=0))
        right.append(jnp.concatenate([slopes[0, r] if 0 <= r < RL else none for r in (i, i - 1, i - 2)], axis=0))
    part = dot_nt(jnp.concatenate(left, axis=1), jnp.concatenate(right, axis=1))

    @pl.when(pl.program_id(0) == 0)
    def _():
        grad_two[...] = part

    @pl.when(pl.program_id(0) > 0)
    def _():
        grad_two[...] += part


def kernel_e(place, slopes, above, below, rows, f_above, f_below, slope, w_two, cofield, grad_two, pre_taps, message, taps, grad_one, sums):
    index = place[0]
    lev = pl.program_id(0)
    source = [above.at[0, 0], above.at[0, 1]] + [slopes.at[0, r] for r in range(RL)] + [below.at[0, 0], below.at[0, 1]]
    for i, x in enumerate(source):
        store_taps(taps, i, x[...].astype(F32))
    rest = jnp.zeros((CP - CO, NC), F32)
    for start, count in ((0, 4), (4, 3), (7, 3)):
        d = dot(w_two[0 : CP * count, 0 : GR * (count + 2)], window(taps, start, count + 2))
        for t in range(count):
            i = start + t
            value = d[t * CP : t * CP + CO] * slope[0, i]
            if i in (0, RL + 1):
                value = value * jnp.where(index == (0 if i == 0 else SP - 1), 0.0, 1.0).astype(F32)
            store_taps(pre_taps.at[0], i, jnp.concatenate([value, rest], axis=0))
    field = [f_above[0, 1]] + [rows[0, r] for r in range(RL)] + [f_below[0, 0]]
    left = jnp.concatenate([jnp.concatenate(field[r : r + 3], axis=0) for r in range(RL)], axis=1)
    right = jnp.concatenate([pre_taps[0, r + 1] for r in range(RL)], axis=1)
    part_one = dot_nt(left, right)

    @pl.when(lev == 0)
    def _():
        grad_one[...] = part_one

    @pl.when(lev == LEV - 1)
    def _():
        sums[...] = jnp.zeros_like(sums)
        two, one = grad_two[...], grad_one[...] + part_one
        for b in range(3):
            sums[b * GR : (b + 1) * GR, 0:CP] = two[0:GR, b * CP : (b + 1) * CP]
            sums[b * GR : (b + 1) * GR, 64 : 64 + CP] = one[:, b * CP : (b + 1) * CP]
        sums[3 * GR : 3 * GR + CP, 0:CP] = two[GR : GR + CP, CP : 2 * CP]
        message[:, 0:32] = jnp.broadcast_to(cofield[...][None], (SP, 32, 128))
        message[:, 32:48] = sums[...].reshape(SP, 16, 128).astype(BF)


def kernel_e_two(pre_taps, slopes, w_one, w_point, after, back):
    for r in (0, 4):
        d = dot(w_one[...], window(pre_taps.at[0], r, 6))
        d = d + dot(w_point[...], slopes[0, r : r + 4].reshape(4 * CP, NC))
        for t in range(4):
            back[0, r + t] = d[t * CP : t * CP + CO]


def kernel_f(received, high, low, inverse, back, out, left, spec, wide):
    modes = received[:, 0:32].reshape(SP * 32, 128)
    place_rows(row_expand(modes, high[...], low[...]), left)
    spec[...] = dot(left[...].astype(BF), inverse[...])
    for lev in range(LEV):
        for r in range(RL):
            at = (lev * RL + r) * CO
            value = back[lev, r] + spec[at : at + CO, :]
            for n in range(0, NC, 128):
                wide[n // 128, pl.ds(lev * C * RL + r, C, stride=RL), :] = value[0:C, n : n + 128]
    for n in range(0, NC, 128):
        out[:, n : n + 128] = wide[n // 128].astype(BF)


def kernel_last(sums, point, one, two):
    scaled = sums[...] * (1.0 / math.sqrt(NR * NC * LEV * 4))
    for a in range(3):
        for b in range(3):
            at = a * GR + b * CP
            two[a, b] = scaled[at : at + C, 0:C]
            at = (2 - b) * GR + a * CP
            one[a, b] = scaled[at : at + C, 64 : 64 + C]
    point[...] = scaled[3 * GR : 3 * GR + C, 0:C]


def shape(dims, kind):
    return jax.ShapeDtypeStruct(dims, kind)


def params(mib):
    return pltpu.CompilerParams(vmem_limit_bytes=56 * 1024 * 1024)


def estimate(us):
    if us is None:
        return None
    return pl.CostEstimate(flops=us * 10**9, bytes_accessed=us * 3 * 10**6, transcendentals=0)


def level_spec(*dims):
    return pl.BlockSpec((1,) + dims, lambda lev: (lev,) + (0,) * len(dims))


def whole_spec(*dims):
    return pl.BlockSpec(dims, lambda lev: (0,) * len(dims))


def from_above(x):
    return lax.ppermute(x, "sp", [(i, i + 1) for i in range(SP - 1)])


def from_below(x):
    return lax.ppermute(x, "sp", [(i + 1, i) for i in range(SP - 1)])


def exchange(x):
    return lax.all_to_all(x, "sp", 0, 0, tiled=True)


def anywhere():
    return pl.BlockSpec(memory_space=pl.ANY)


def plain_call(kernel, operands, after, outs, scratch, mib, name, place=(), cost=None):
    vmem = pl.BlockSpec(memory_space=pltpu.VMEM)
    return pl.pallas_call(
        kernel,
        in_specs=[pl.BlockSpec(memory_space=pltpu.SMEM)] * len(place) + [vmem] * len(operands) + [anywhere()] * len(after),
        out_specs=[vmem] * len(outs),
        out_shape=outs,
        scratch_shapes=scratch,
        compiler_params=params(mib),
        cost_estimate=estimate(cost),
        name=name,
    )(*place, *operands, *after)


def local(field, cotangent, spec_weight, point_weight, kernel_one, kernel_two):
    place = lax.axis_index("sp").astype(jnp.int32).reshape(1)
    inputs = field.reshape(LEV * C * RL, NC)
    upstream = cotangent.reshape(LEV * C * RL, NC)
    table = jnp.asarray(TABLE)
    weight = jnp.transpose(spec_weight, (1, 3, 0, 2)).reshape(C * QN * 2, C)
    strip = shape((LEV, 2, CP, NC), BF)
    grid_rows = shape((LEV, RL, CP, NC), BF)
    natural = shape((LEV * C * RL, NC), BF)
    relayout = pltpu.VMEM((NC // 128, (LEV * C + 12) * RL, 128), F32)
    flat, cols = pltpu.VMEM((LEV * C * RL, 128), F32), pltpu.VMEM((128, 256), F32)
    row_matrix = shape((SP * 32, 256), BF)
    message, high, low = plain_call(
        kernel_a,
        (inputs, table, jnp.asarray(ROW_HIGH), jnp.asarray(ROW_LOW), jnp.asarray(MODE_ROW)),
        (),
        [shape((SP * 32, 128), BF), row_matrix, row_matrix],
        [flat, cols],
        10,
        "field_modes",
        (place,),
    )
    arrived = exchange(message.reshape(SP, 32, 128))
    toeplitz, blocks = shape((4 * CP, 6 * GR), BF), shape((4 * CP, 4 * CP), BF)
    rows, top, bottom, cot_rows, w_one, w_two, w_two_back, w_one_back, w_point, w_point_back = plain_call(
        kernel_rows,
        (inputs, upstream, kernel_one, kernel_two, point_weight),
        (message,),
        [grid_rows, strip, strip, grid_rows] + [toeplitz] * 4 + [blocks] * 2,
        [relayout, pltpu.VMEM((CP, 9 * CP), F32), pltpu.VMEM((4 * CP, 6 * GR), F32)],
        12,
        "row_layout",
    )
    f_above, f_below = from_above(bottom), from_below(top)

    square, lines = pltpu.VMEM((128, 128), F32), pltpu.VMEM((C * QN * 2, 128), F32)
    mixed, kept = plain_call(
        kernel_mix,
        (arrived, weight),
        (),
        [shape((SP, 32, 128), BF), shape((32, 128), F32)],
        [square, square, square, lines],
        6,
        "mode_mix",
    )
    gathered = exchange(mixed).reshape(SP * 32, 128)

    mid_taps, slope, pre = pl.pallas_call(
        kernel_b,
        grid=(LEV,),
        in_specs=[
            pl.BlockSpec(memory_space=pltpu.SMEM),
            level_spec(RL, CP, NC),
            level_spec(2, CP, NC),
            level_spec(2, CP, NC),
            whole_spec(4 * CP, 6 * GR),
            whole_spec(4 * CP, 6 * GR),
            whole_spec(4 * CP, 4 * CP),
            anywhere(),
        ],
        out_specs=[
            level_spec(RL + 2, GR, NC),
            level_spec(RL + 2, CO, NC),
            level_spec(RL, CO, NC),
        ],
        out_shape=[
            shape((LEV, RL + 2, GR, NC), BF),
            shape((LEV, RL + 2, CO, NC), F32),
            shape((LEV, RL, CO, NC), F32),
        ],
        scratch_shapes=[pltpu.VMEM((RL + 4, GR, NC), BF)],
        compiler_params=params(28),
        name="two_convolutions",
    )(place, rows, f_above, f_below, w_one, w_two, w_point, mixed)

    left, spec = pltpu.VMEM((LEV * RL * CO, 128), F32), pltpu.VMEM((LEV * RL * CO, NC), F32)
    values, slopes, s_top, s_bottom, message = pl.pallas_call(
        kernel_d,
        grid=(LEV,),
        in_specs=[
            whole_spec(SP * 32, 128),
            whole_spec(SP * 32, 256),
            whole_spec(SP * 32, 256),
            whole_spec(128, NC),
            level_spec(RL, CO, NC),
            level_spec(RL, CP, NC),
            whole_spec(NC, 128),
            whole_spec(1, 256),
        ],
        out_specs=[level_spec(RL, CP, NC)] * 2 + [level_spec(2, CP, NC)] * 2 + [whole_spec(SP * 32, 128)],
        out_shape=[grid_rows, grid_rows, strip, strip, shape((SP * 32, 128), BF)],
        scratch_shapes=[
            left,
            pltpu.VMEM((LEV * RL, CO, NC), F32),
            pltpu.VMEM((LEV, RL * CP, 128), F32),
            cols,
        ],
        compiler_params=params(22),
        name="output_and_slope",
    )(gathered, high, low, jnp.asarray(INVERSE), pre, cot_rows, table, jnp.asarray(SCALE))
    arrived = exchange(message.reshape(SP, 32, 128))
    s_above, s_below = from_above(s_bottom), from_below(s_top)

    grad_two = pl.pallas_call(
        kernel_e_zero,
        grid=(LEV,),
        in_specs=[level_spec(RL, CP, NC), level_spec(RL + 2, GR, NC), level_spec(RL, CP, NC)],
        out_specs=whole_spec(GR + CP, GR),
        out_shape=shape((GR + CP, GR), F32),
        compiler_params=params(22),
        name="weight_gradients_two",
    )(slopes, mid_taps, rows)
    cofield, pair = plain_call(
        kernel_mix_back,
        (arrived, weight, kept),
        (),
        [shape((32, 128), BF), shape((64, 128), F32)],
        [square, lines],
        6,
        "mode_mix_back",
        cost=15,
    )
    pre_taps, message = pl.pallas_call(
        kernel_e,
        grid=(LEV,),
        in_specs=[
            pl.BlockSpec(memory_space=pltpu.SMEM),
            level_spec(RL, CP, NC),
            level_spec(2, CP, NC),
            level_spec(2, CP, NC),
            level_spec(RL, CP, NC),
            level_spec(2, CP, NC),
            level_spec(2, CP, NC),
            level_spec(RL + 2, CO, NC),
            whole_spec(4 * CP, 6 * GR),
            whole_spec(32, 128),
            whole_spec(GR + CP, GR),
        ],
        out_specs=[level_spec(RL + 2, GR, NC), whole_spec(SP, 48, 128)],
        out_shape=[shape((LEV, RL + 2, GR, NC), BF), shape((SP, 48, 128), BF)],
        scratch_shapes=[
            pltpu.VMEM((RL + 4, GR, NC), BF),
            pltpu.VMEM((GR, GR), F32),
            pltpu.VMEM((SP * 16, 128), F32),
        ],
        compiler_params=params(28),
        name="slope_and_weight_gradients",
    )(place, slopes, s_above, s_below, rows, f_above, f_below, slope, w_two_back, cofield, grad_two)
    gathered = exchange(message)
    others = [lax.ppermute(pair, "rep", [(i, i ^ k) for i in range(4)]) for k in (1, 2, 3)]
    (spec_grad,) = plain_call(
        kernel_spec_grad,
        (pair, *others),
        (message,),
        [shape(weight.shape, F32)],
        [pltpu.VMEM((4, 128, 128), F32)] * 2 + [lines],
        8,
        "spectral_gradient",
    )
    back = pl.pallas_call(
        kernel_e_two,
        grid=(LEV,),
        in_specs=[
            level_spec(RL + 2, GR, NC),
            level_spec(RL, CP, NC),
            whole_spec(4 * CP, 6 * GR),
            whole_spec(4 * CP, 4 * CP),
            anywhere(),
        ],
        out_specs=level_spec(RL, CO, NC),
        out_shape=shape((LEV, RL, CO, NC), F32),
        compiler_params=params(22),
        name="backward_convolution",
    )(pre_taps, slopes, w_one_back, w_point_back, message)

    (shares,) = plain_call(
        kernel_share, (gathered,), (back, spec_grad), [shape((16, 128), F32)], [], 4, "weight_gradient_shares"
    )
    shares = jnp.sum(lax.all_gather(shares, "rep", axis=0), axis=0)
    every = exchange(jnp.broadcast_to(shares[None], (SP, 16, 128)))
    (out,) = plain_call(
        kernel_out,
        (values,),
        (shares,),
        [natural],
        [pltpu.VMEM((NC // 128, LEV * C * RL, 128), F32)],
        10,
        "output_layout",
    )
    (field_grad,) = plain_call(
        kernel_f,
        (gathered, high, low, jnp.asarray(BACK), back),
        (),
        [natural],
        [left, spec, pltpu.VMEM((NC // 128, LEV * C * RL, 128), F32)],
        18,
        "field_gradient",
    )
    kernel_out_shape = shape((3, 3, C, C), F32)
    point_total, one_total, two_total = plain_call(
        kernel_last,
        (every.reshape(SP * 16, 128),),
        (),
        [shape((C, C), F32), kernel_out_shape, kernel_out_shape],
        [],
        4,
        "weight_gradients",
    )
    spec_total = jnp.transpose(spec_grad.reshape(C, QN, 2, C), (2, 0, 3, 1))
    return (
        out.reshape(field.shape),
        field_grad.reshape(field.shape),
        spec_total,
        point_total,
        one_total,
        two_total,
    )


def solution(mesh):
    specs = (
        P("rep", None, None, "sp", None),
        P("rep", None, None, "sp", None),
        P(None, None, None, "sp"),
        P(),
        P(),
        P(),
    )
    return jax.shard_map(local, mesh=mesh, in_specs=specs, out_specs=specs, check_vma=False)
```

time: 185 us -> 153 us (0.83)
  waiting for transfers between devices: 15 us -> 3.86 us
  blocking collectives: 16.7 us -> 5.71 us
  local copies, waits for them, and re-layouts: 14.9 us -> 7.14 us
  other arithmetic: 3.44 us -> 0.01 us
  starting transfers between devices: 64.1 us -> 67.1 us
    pallas_call x5 -> x12, Pallas kernels: 26.7 us -> 48.1 us  [the longest x9 30 us: plain_call(): pl.pallas_call(kernel, in_specs=[pl.BlockSpec(memory_space=pltpu.SMEM)] *...]
    all_to_all x6 -> x5, waiting for transfers between devices: 15 us -> 1.74 us  [exchange(): return lax.all_to_all(x, 'sp', 0, 0, tiled=True)]
    pallas_call x1, Pallas kernels: 22.1 us -> 9.84 us  [local(): pl.pallas_call(kernel_e, grid=(LEV,), in_specs=[pl.BlockSpec(memory_space...]
    all_gather x1 -> x0, blocking collectives: 10.9 us -> none  [local(): spec_all = lax.all_gather(spec_part, 'rep', axis=0)]
    pallas_call x1, Pallas kernels: 19.4 us -> 9.42 us  [local(): pl.pallas_call(kernel_b, grid=(LEV,), in_specs=[pl.BlockSpec(memory_space...]
    ppermute x0 -> x3, starting transfers between devices: none -> 5.86 us  [local(): lax.ppermute(pair, 'rep', [(i, i ^ k) for i in range(4)])]
    reshape x10 -> x0, local copies, waits for them, and re-layouts: 4.5 us -> none  [the longest x3 2.23 us: mode_weight(): jnp.pad(moved, ((0, 0), (0, 64 - C), (0, 0), (0, 64 - C)))]
    concatenate x3 -> x0, other arithmetic: 3.28 us -> none  [the longest x1 1.83 us: local(): jnp.concatenate([wide_rows(grad_two, 160), wide_rows(grad_one, 160), wide...]
  transfers between devices with their start and end apart: 10 -> 12, of which waited for: 3 -> 2; matrix products, arithmetic and copies ran while one was open for 5% -> 0% of each run, Pallas kernels for 29% -> 28%
where the time goes in v2:
time: 153 us; the launch traced here: 152 us
  Pallas kernels  67.4 us (44%)
  starting transfers between devices  67.1 us (44%)
  local copies, waits for them, and re-layouts  7.14 us (5%)
  blocking collectives  5.71 us (4%)
  waiting for transfers between devices  3.86 us (3%)
    all_to_all x5, starting transfers between devices, exchange(): return lax.all_to_all(x, 'sp', 0, 0, tiled=True)  52.2 us
    pallas_call x9, Pallas kernels, plain_call(): pl.pallas_call(kernel, in_specs=[pl.BlockSpec(memory_space=pltpu.SMEM)] *...  30 us
    pallas_call x1, Pallas kernels, local(): pl.pallas_call(kernel_e, grid=(LEV,), in_specs=[pl.BlockSpec(memory_space...  9.84 us
    pallas_call x1, Pallas kernels, local(): pl.pallas_call(kernel_b, grid=(LEV,), in_specs=[pl.BlockSpec(memory_space...  9.42 us
    pallas_call x1, Pallas kernels, local(): pl.pallas_call(kernel_d, grid=(LEV,), in_specs=[whole_spec(SP * 32, 128),...  7.07 us
    unnamed x28, local copies, waits for them, and re-layouts  6.41 us
    ppermute x2, starting transfers between devices, from_above(): return lax.ppermute(x, 'sp', [(i, i + 1) for i in range(SP - 1)])  6.3 us
    ppermute x3, starting transfers between devices, local(): lax.ppermute(pair, 'rep', [(i, i ^ k) for i in range(4)])  5.86 us
  transfers between devices with their start and end apart: 12, of which 2 were waited for; matrix products, arithmetic and copies ran while one was open for 0% of the time, Pallas kernels for 28%

profile of v2, /device:TPU:1, one launch (start us, length us, event | category | flops | bytes accessed | tf_op | source)
XLA Modules:
  0.0 152.1 jit_solution(17174473430278343061)
XLA Ops:
  0.6 4.7 %field_modes.1 = (bf16[1024,128]{1,0:T(8,128)(2,1)}, bf16[1024,256]{1,0:T(8,128)(2,1)}, bf16[1024,256]{1,0:T(8,128)(2,1)}) custom-call(s32[1]{0:T(128)} %bitcast.place, bf16[576,1024]{1,0:T(8,128)(2,1)} %bitcast.16, bf16[1024,128]{1,0:T(8,128)(2,1)} %constant.20.clone.table, bf16[1024,256]{1,0:T(8,128)(2,1)} %constant.21.clone.high, ...), custom_call_target="tpu_custom_call" | custom-call | tf_op jit(solution)/shard_map/field_modes/pallas_call | solution.py:479
  5.3 11.3 %all-to-all-start = ((bf16[32,32,128]{2,1,0:T(8,128)(2,1)}), bf16[32,32,128]{2,1,0:T(8,128)(2,1)S(1)}, u32[]{:S(2)}, u32[]{:S(2)}) async-start(bf16[32,32,128]{2,1,0:T(8,128)(2,1)} %bitcast.23), calls=%async_computation | async-start | bytes 524288 | tf_op jit(solution)/shard_map/all_to_all | solution.py:470
  16.7 6.7 %row_layout.1 = (bf16[2,8,48,1024]{3,2,1,0:T(8,128)(2,1)}, bf16[2,2,48,1024]{3,2,1,0:T(8,128)(2,1)}, bf16[2,2,48,1024]{3,2,1,0:T(8,128)(2,1)}, bf16[2,8,48,1024]...) custom-call(bf16[576,1024]{1,0:T(8,128)(2,1)} %bitcast.17, ...), custom_call_target="tpu_custom_call" | custom-call | tf_op jit(solution)/shard_map/row_layout/pallas_call | solution.py:479
  23.4 3.1 %collective-permute-start = (bf16[2,2,48,1024]{3,2,1,0:T(8,128)(2,1)}, bf16[2,2,48,1024]{3,2,1,0:T(8,128)(2,1)S(1)}, u32[]{:S(2)}, u32[]{:S(2)}) collective-permute-start(bf16[2,2,48,1024]{3,2,1,0:T(8,128)(2,1)} %get-tuple-element.41), channel_id=1, source_target_pairs={{0,1},{1,2},{2,3},{3,4},{4,5},{5,6},{6,7},{7,8},{8,9},{9,10},{10,1... | collective-permute-start | bytes 1179656 | tf_op jit(solution)/shard_map/ppermute | solution.py:462
  26.5 1.3 collective-permute-start.1
  28.6 2.5 %mode_mix.1 = (bf16[32,32,128]{2,1,0:T(8,128)(2,1)}, f32[32,128]{1,0:T(8,128)}) custom-call(bf16[32,32,128]{2,1,0:T(8,128)(2,1)} %copy-done.4, f32[648,36]{1,0:T(8,128)} %bitcast.25), custom_call_target="tpu_custom_call" | custom-call | tf_op jit(solution)/shard_map/mode_mix/pallas_call | solution.py:479
  31.0 11.3 %all-to-all-start.1 = ((bf16[32,32,128]{2,1,0:T(8,128)(2,1)}), bf16[32,32,128]{2,1,0:T(8,128)(2,1)S(1)}, u32[]{:S(2)}, u32[]{:S(2)}) async-start(bf16[32,32,128]{2,1,0:T(8,128)(2,1)} %get-tuple-element.37.after), calls=%async_computation.1 | async-start | bytes 524288 | tf_op jit(solution)/shard_map/all_to_all | solution.py:470
  42.4 0.7 copy-done.1
  43.2 9.4 %two_convolutions.1 = (bf16[2,10,144,1024]{3,2,1,0:T(8,128)(2,1)}, f32[2,10,40,1024]{3,2,1,0:T(8,128)}, f32[2,8,40,1024]{3,2,1,0:T(8,128)}) custom-call(s32[1]{0:T(128)} %bitcast.place, bf16[2,8,48,1024]{3,2,1,0:T(8,128)(2,1)} %get-tuple-element.40.rows, bf16[2,2,48,1024]{3,2,1,0:T(8,128)(2,1)} %copy-done.1, bf16[2,2,48,1024]{3,2,1,0:T(8,128)(2,1)} %copy-done.2, ...), custom_call_target="tpu_custom_call" | custom-call | tf_op jit(solution)/shard_map/two_convolutions/pallas_call | solution.py:538
  53.3 7.1 %output_and_slope.1 = (bf16[2,8,48,1024]{3,2,1,0:T(8,128)(2,1)}, bf16[2,8,48,1024]{3,2,1,0:T(8,128)(2,1)}, bf16[2,2,48,1024]{3,2,1,0:T(8,128)(2,1)}, bf16[2,2,48,1024]{3,2,1,0:T(8,128)(2,1)}, bf16[1024,128]{1,0:T(8,128)(2,1)}) custom-call(bf16[1024,128]{1,0:T(8,128)(2,1)} %bitcast.22, bf16[1024,256]{1,0:T(8,128)(2,1)} %get-tuple-element.38.high, ...), custom_call_target="tpu_custom_call" | custom-call | tf_op jit(solution)/shard_map/output_and_slope/pallas_call | solution.py:567
  60.4 9.2 %all-to-all-start.2 = ((bf16[32,32,128]{2,1,0:T(8,128)(2,1)}), bf16[32,32,128]{2,1,0:T(8,128)(2,1)S(1)}, u32[]{:S(2)}, u32[]{:S(2)}) async-start(bf16[32,32,128]{2,1,0:T(8,128)(2,1)} %bitcast.27), calls=%async_computation.2 | async-start | bytes 524288 | tf_op jit(solution)/shard_map/all_to_all | solution.py:470
  69.6 3.2 %collective-permute-start.2 = (bf16[2,2,48,1024]{3,2,1,0:T(8,128)(2,1)}, bf16[2,2,48,1024]{3,2,1,0:T(8,128)(2,1)S(1)}, u32[]{:S(2)}, u32[]{:S(2)}) collective-permute-start(bf16[2,2,48,1024]{3,2,1,0:T(8,128)(2,1)} %get-tuple-element.50), channel_id=1, source_target_pairs={{0,1},{1,2},{2,3},{3,4},{4,5},{5,6},{6,7},{7,8},{8,9},{9,10},{10,1... | collective-permute-start | bytes 1179656 | tf_op jit(solution)/shard_map/ppermute | solution.py:462
  72.8 1.5 collective-permute-start.3
  74.3 5.4 %weight_gradients_two.1.grad_two = f32[192,144]{1,0:T(8,128)} custom-call(bf16[2,8,48,1024]{3,2,1,0:T(8,128)(2,1)} %get-tuple-element.49.slopes, bf16[2,10,144,1024]{3,2,1,0:T(8,128)(2,1)} %get-tuple-element.57.mid_taps, bf16[2,8,48,1024]{3,2,1,0:T(8,128)(2,1)} %get-tuple-element.40.rows), custom_call_target="tpu_custom_call" | custom-call | tf_op jit(solution)/shard_map/weight_gradients_two/pallas_call | solution.py:594
  80.4 2.1 %mode_mix_back.1 = (bf16[32,128]{1,0:T(8,128)(2,1)}, f32[64,128]{1,0:T(8,128)}) custom-call(bf16[32,32,128]{2,1,0:T(8,128)(2,1)} %copy-done.8, f32[648,36]{1,0:T(8,128)} %bitcast.26, f32[32,128]{1,0:T(8,128)} %get-tuple-element.55.kept), custom_call_target="tpu_custom_call" | custom-call | flops 15000000512 | bytes 45000000 | tf_op jit(solution)/shard_map/mode_mix_back/pallas_call | solution.py:479
  82.5 2.1 %collective-permute-done.3.below = bf16[2,2,48,1024]{3,2,1,0:T(8,128)(2,1)S(1)} collective-permute-done((bf16[2,2,48,1024]{3,2,1,0:T(8,128)(2,1)}, bf16[2,2,48,1024]{3,2,1,0:T(8,128)(2,1)S(1)}, u32[]{:S(2)}, u32[]{:S(2)}) %collective-permute-start.3) | collective-permute-done | bytes 393248 | tf_op jit(solution)/shard_map/ppermute | solution.py:466
  84.6 0.8 copy-done.7
  85.4 9.8 %slope_and_weight_gradients.1 = (bf16[2,10,144,1024]{3,2,1,0:T(8,128)(2,1)}, bf16[32,48,128]{2,1,0:T(8,128)(2,1)}) custom-call(s32[1]{0:T(128)} %bitcast.place, bf16[2,8,48,1024]{3,2,1,0:T(8,128)(2,1)} %get-tuple-element.49.slopes, bf16[2,2,48,1024]{3,2,1,0:T(8,128)(2,1)} %copy-done.6, bf16[2,2,48,1024]{3,2,1,0:T(8,128)(2,1)} %copy-done.7, ...), custom_call_target="tpu_custom_call" | custom-call | tf_op jit(solution)/shard_map/slope_and_weight_gradients/pallas_call | solution.py:613
  95.2 10.8 %all-to-all-start.3 = ((bf16[32,48,128]{2,1,0:T(8,128)(2,1)}), bf16[32,48,128]{2,1,0:T(8,128)(2,1)S(1)}, u32[]{:S(2)}, u32[]{:S(2)}) async-start(bf16[32,48,128]{2,1,0:T(8,128)(2,1)} %get-tuple-element.58.after), calls=%async_computation.3 | async-start | bytes 786432 | tf_op jit(solution)/shard_map/all_to_all | solution.py:470
  106.1 4.8 %collective-permute-start.6 = (f32[64,128]{1,0:T(8,128)S(1)}, f32[64,128]{1,0:T(8,128)S(1)}, u32[]{:S(2)}, u32[]{:S(2)}) collective-permute-start(f32[64,128]{1,0:T(8,128)S(1)} %copy-done.10), channel_id=1, source_target_pairs={{0,96},{32,64},{64,32},{96,0},{1,97},{33,65},{65,33},{97,1},{2,98}... | collective-permute-start | bytes 98312 | tf_op jit(solution)/shard_map/ppermute | solution.py:640
  110.8 1.1 collective-permute-start.5
  111.9 5.7 %backward_convolution.1.first.back = f32[2,8,40,1024]{3,2,1,0:T(8,128)} custom-call(bf16[2,10,144,1024]{3,2,1,0:T(8,128)(2,1)} %get-tuple-element.59.pre_taps, bf16[2,8,48,1024]{3,2,1,0:T(8,128)(2,1)} %get-tuple-element.49.slopes, bf16[192,864]{1,0:T(8,128)(2,1)} %get-tuple-element.60.w_one, bf16[192,192]{1,0:T(8,128)(2,1)} %get-tuple-element.61.w_point, ...), custom_call_target="tpu_custom_call" | custom-call | tf_op jit(solution)/shard_map/backward_convolution/pallas_call | solution.py:650
  118.8 2.6 %spectral_gradient.1.second = f32[648,36]{1,0:T(8,128)} custom-call(f32[64,128]{1,0:T(8,128)} %get-tuple-element.62.p0, f32[64,128]{1,0:T(8,128)} %copy-done.13, f32[64,128]{1,0:T(8,128)} %copy-done.12, f32[64,128]{1,0:T(8,128)} %copy-done.11, bf16[32,48,128]{2,1,0:T(8,128)(2,1)} %get-tuple-element.58.after), custom_call_target="tpu_custom_call" | custom-call | tf_op jit(solution)/shard_map/spectral_gradient/pallas_call | solution.py:479
  121.4 0.8 copy-done
  122.2 1.6 %weight_gradient_shares.1 = f32[16,128]{1,0:T(8,128)} custom-call(bf16[32,48,128]{2,1,0:T(8,128)(2,1)} %copy-done, f32[2,8,40,1024]{3,2,1,0:T(8,128)} %backward_convolution.1.first.back, f32[648,36]{1,0:T(8,128)} %spectral_gradient.1.second), custom_call_target="tpu_custom_call" | custom-call | tf_op jit(solution)/shard_map/weight_gradient_shares/pallas_call | solution.py:479
  123.8 5.7 %all-gather = f32[64,128]{1,0:T(8,128)S(1)} all-gather(f32[16,128]{1,0:T(8,128)} %weight_gradient_shares.1), channel_id=2, replica_groups=mesh['rep'=4,'sp'=32] {'rep'}, dimensions={0}, use_global_device_ids=true | all-gather | bytes 40960 | tf_op jit(solution)/shard_map/all_gather | solution.py:669
  129.6 0.7 broadcast_in_dim.2
  130.3 9.5 %all-to-all-start.4 = ((f32[32,16,128]{2,1,0:T(8,128)}), f32[32,16,128]{2,1,0:T(8,128)S(1)}, u32[]{:S(2)}, u32[]{:S(2)}) async-start(f32[32,16,128]{2,1,0:T(8,128)} %broadcast_in_dim.2), calls=%async_computation.4 | async-start | bytes 524288 | tf_op jit(solution)/shard_map/all_to_all | solution.py:470
  139.8 3.4 %output_layout.1 = bf16[576,1024]{1,0:T(8,128)(2,1)} custom-call(bf16[2,8,48,1024]{3,2,1,0:T(8,128)(2,1)} %get-tuple-element.48.values, f32[16,128]{1,0:T(8,128)} %copy-done.9), custom_call_target="tpu_custom_call" | custom-call | tf_op jit(solution)/shard_map/output_layout/pallas_call | solution.py:479
  143.2 4.7 %field_gradient.1 = bf16[576,1024]{1,0:T(8,128)(2,1)} custom-call(bf16[32,48,128]{2,1,0:T(8,128)(2,1)} %copy-done, bf16[1024,256]{1,0:T(8,128)(2,1)} %get-tuple-element.38.high, bf16[1024,256]{1,0:T(8,128)(2,1)} %get-tuple-element.39.low, bf16[128,1024]{1,0:T(8,128)(2,1)} %constant.26.clone.inverse, f32[2,8,40,1024]{3,2,1,0:T(8,128)} %backward_convolution.1.first.back), custom_call_target="tpu_custom_call" | custom-call | tf_op jit(solution)/shard_map/field_gradient/pallas_call | solution.py:479
  147.9 1.7 %all-to-all-done.4 = f32[32,16,128]{2,1,0:T(8,128)S(1)} async-done(((f32[32,16,128]{2,1,0:T(8,128)}), f32[32,16,128]{2,1,0:T(8,128)S(1)}, u32[]{:S(2)}, u32[]{:S(2)}) %all-to-all-start.4) | async-done | bytes 262176 | tf_op jit(solution)/shard_map/all_to_all | solution.py:470
  150.3 1.8 %weight_gradients.1 = (f32[36,36]{1,0:T(8,128)}, f32[3,3,36,36]{3,2,1,0:T(8,128)}, f32[3,3,36,36]{3,2,1,0:T(8,128)}) custom-call(f32[512,128]{1,0:T(8,128)} %bitcast.24), custom_call_target="tpu_custom_call" | custom-call | tf_op jit(solution)/shard_map/weight_gradients/pallas_call | solution.py:479
  (37 shorter events, 4.2 us)
Async XLA Ops:
  5.3 22.5 %all-to-all-start = ((bf16[32,32,128]{2,1,0:T(8,128)(2,1)}), bf16[32,32,128]{2,1,0:T(8,128)(2,1)S(1)}, u32[]{:S(2)}, u32[]{:S(2)}) async-start(bf16[32,32,128]{2,1,0:T(8,128)(2,1)} %bitcast.23), calls=%async_computation | async-start | bytes 524288 | tf_op jit(solution)/shard_map/all_to_all | solution.py:470
  23.4 18.9 %collective-permute-start = (bf16[2,2,48,1024]{3,2,1,0:T(8,128)(2,1)}, bf16[2,2,48,1024]{3,2,1,0:T(8,128)(2,1)S(1)}, u32[]{:S(2)}, u32[]{:S(2)}) collective-permute-start(bf16[2,2,48,1024]{3,2,1,0:T(8,128)(2,1)} %get-tuple-element.41), channel_id=1, source_target_pairs={{0,1},{1,2},{2,3},{3,4},{4,5},{5,6},{6,7},{7,8},{8,9},{9,10},{10,1... | collective-permute-start | bytes 1179656 | tf_op jit(solution)/shard_map/ppermute | solution.py:462
  26.5 15.8 %collective-permute-start.1 = (bf16[2,2,48,1024]{3,2,1,0:T(8,128)(2,1)}, bf16[2,2,48,1024]{3,2,1,0:T(8,128)(2,1)S(1)}, u32[]{:S(2)}, u32[]{:S(2)}) collective-permute-start(bf16[2,2,48,1024]{3,2,1,0:T(8,128)(2,1)} %get-tuple-element.42), channel_id=1, source_target_pairs={{1,0},{2,1},{3,2},{4,3},{5,4},{6,5},{7,6},{8,7},{9,8},{10,9},{11,1... | collective-permute-start | bytes 1179656 | tf_op jit(solution)/shard_map/ppermute | solution.py:466
  27.9 0.7 copy-start.4
  31.0 21.6 %all-to-all-start.1 = ((bf16[32,32,128]{2,1,0:T(8,128)(2,1)}), bf16[32,32,128]{2,1,0:T(8,128)(2,1)S(1)}, u32[]{:S(2)}, u32[]{:S(2)}) async-start(bf16[32,32,128]{2,1,0:T(8,128)(2,1)} %get-tuple-element.37.after), calls=%async_computation.1 | async-start | bytes 524288 | tf_op jit(solution)/shard_map/all_to_all | solution.py:470
  42.3 0.7 copy-start.1
  42.3 0.9 copy-start.2
  52.6 0.7 copy-start.3
  60.4 19.3 %all-to-all-start.2 = ((bf16[32,32,128]{2,1,0:T(8,128)(2,1)}), bf16[32,32,128]{2,1,0:T(8,128)(2,1)S(1)}, u32[]{:S(2)}, u32[]{:S(2)}) async-start(bf16[32,32,128]{2,1,0:T(8,128)(2,1)} %bitcast.27), calls=%async_computation.2 | async-start | bytes 524288 | tf_op jit(solution)/shard_map/all_to_all | solution.py:470
  69.6 12.8 %collective-permute-start.2 = (bf16[2,2,48,1024]{3,2,1,0:T(8,128)(2,1)}, bf16[2,2,48,1024]{3,2,1,0:T(8,128)(2,1)S(1)}, u32[]{:S(2)}, u32[]{:S(2)}) collective-permute-start(bf16[2,2,48,1024]{3,2,1,0:T(8,128)(2,1)} %get-tuple-element.50), channel_id=1, source_target_pairs={{0,1},{1,2},{2,3},{3,4},{4,5},{5,6},{6,7},{7,8},{8,9},{9,10},{10,1... | collective-permute-start | bytes 1179656 | tf_op jit(solution)/shard_map/ppermute | solution.py:462
  72.8 11.8 %collective-permute-start.3 = (bf16[2,2,48,1024]{3,2,1,0:T(8,128)(2,1)}, bf16[2,2,48,1024]{3,2,1,0:T(8,128)(2,1)S(1)}, u32[]{:S(2)}, u32[]{:S(2)}) collective-permute-start(bf16[2,2,48,1024]{3,2,1,0:T(8,128)(2,1)} %get-tuple-element.51), channel_id=1, source_target_pairs={{1,0},{2,1},{3,2},{4,3},{5,4},{6,5},{7,6},{8,7},{9,8},{10,9},{11,1... | collective-permute-start | bytes 1179656 | tf_op jit(solution)/shard_map/ppermute | solution.py:466
  79.7 0.7 copy-start.8
  82.5 2.1 %copy-start.6 = (bf16[2,2,48,1024]{3,2,1,0:T(8,128)(2,1)}, bf16[2,2,48,1024]{3,2,1,0:T(8,128)(2,1)S(1)}, u32[]{:S(2)}) copy-start(bf16[2,2,48,1024]{3,2,1,0:T(8,128)(2,1)S(1)} %collective-permute-done.2.above) | copy-start | bytes 1179652
  84.6 0.8 copy-start.7
  85.4 20.7 %copy-start.10 = (f32[64,128]{1,0:T(8,128)S(1)}, f32[64,128]{1,0:T(8,128)}, u32[]{:S(2)}) copy-start(f32[64,128]{1,0:T(8,128)} %get-tuple-element.62.p0) | copy-start | bytes 98308
  95.2 26.2 %all-to-all-start.3 = ((bf16[32,48,128]{2,1,0:T(8,128)(2,1)}), bf16[32,48,128]{2,1,0:T(8,128)(2,1)S(1)}, u32[]{:S(2)}, u32[]{:S(2)}) async-start(bf16[32,48,128]{2,1,0:T(8,128)(2,1)} %get-tuple-element.58.after), calls=%async_computation.3 | async-start | bytes 786432 | tf_op jit(solution)/shard_map/all_to_all | solution.py:470
  106.1 11.5 %collective-permute-start.6 = (f32[64,128]{1,0:T(8,128)S(1)}, f32[64,128]{1,0:T(8,128)S(1)}, u32[]{:S(2)}, u32[]{:S(2)}) collective-permute-start(f32[64,128]{1,0:T(8,128)S(1)} %copy-done.10), channel_id=1, source_target_pairs={{0,96},{32,64},{64,32},{96,0},{1,97},{33,65},{65,33},{97,1},{2,98}... | collective-permute-start | bytes 98312 | tf_op jit(solution)/shard_map/ppermute | solution.py:640
  110.8 6.7 %collective-permute-start.5 = (f32[64,128]{1,0:T(8,128)S(1)}, f32[64,128]{1,0:T(8,128)S(1)}, u32[]{:S(2)}, u32[]{:S(2)}) collective-permute-start(f32[64,128]{1,0:T(8,128)S(1)} %copy-done.10), channel_id=1, source_target_pairs={{0,64},{32,96},{64,0},{96,32},{1,65},{33,97},{65,1},{97,33},{2,66}... | collective-permute-start | bytes 98312 | tf_op jit(solution)/shard_map/ppermute | solution.py:640
  111.9 5.7 %collective-permute-start.4 = (f32[64,128]{1,0:T(8,128)S(1)}, f32[64,128]{1,0:T(8,128)S(1)}, u32[]{:S(2)}, u32[]{:S(2)}) collective-permute-start(f32[64,128]{1,0:T(8,128)S(1)} %copy-done.10), channel_id=1, source_target_pairs={{0,32},{32,0},{64,96},{96,64},{1,33},{33,1},{65,97},{97,65},{2,34}... | collective-permute-start | bytes 98312 | tf_op jit(solution)/shard_map/ppermute | solution.py:640
  117.6 0.6 copy-start.11
  117.6 0.6 copy-start.12
  118.2 0.6 copy-start.13
  121.4 0.8 copy-start
  129.6 10.3 %copy-start.9 = (f32[16,128]{1,0:T(8,128)}, f32[16,128]{1,0:T(8,128)S(1)}, u32[]{:S(2)}) copy-start(f32[16,128]{1,0:T(8,128)S(1)} %reduce_sum.9.after) | copy-start | bytes 24580
  130.3 19.3 %all-to-all-start.4 = ((f32[32,16,128]{2,1,0:T(8,128)}), f32[32,16,128]{2,1,0:T(8,128)S(1)}, u32[]{:S(2)}, u32[]{:S(2)}) async-start(f32[32,16,128]{2,1,0:T(8,128)} %broadcast_in_dim.2), calls=%async_computation.4 | async-start | bytes 524288 | tf_op jit(solution)/shard_map/all_to_all | solution.py:470
  149.6 0.7 copy-start.5

commit v3 on v2

--- a/solution.py
+++ b/solution.py
@@ -180,27 +180,29 @@
 
 
 def kernel_rows(field, cot, one, two, point, after, rows, top, bottom, cot_rows, w_one, w_two, w_two_back, w_one_back, w_point, w_point_back, wide, base, spread):
-    prepare(one, two, point, w_one, w_two, w_two_back, w_one_back, w_point, w_point_back, base, spread)
-    for source, target in ((field, rows), (cot, cot_rows)):
+    @pl.when(pl.program_id(0) == 0)
+    def _():
+        prepare(one, two, point, w_one, w_two, w_two_back, w_one_back, w_point, w_point_back, base, spread)
+
+    for k, (source, target) in enumerate(((field, rows), (cot, cot_rows))):
         for n in range(0, NC, 128):
-            wide[n // 128, 0 : LEV * C * RL, :] = source[:, n : n + 128].astype(F32)
-            wide[n // 128, LEV * C * RL :, :] = jnp.zeros((12 * RL, 128), F32)
-        for lev in range(LEV):
-            for r in range(RL):
-                for n in range(0, NC, 128):
-                    x = wide[n // 128, pl.ds(lev * C * RL + r, CP, stride=RL), :].astype(BF)
-                    target[lev, r, :, n : n + 128] = x
-                    if target is rows and r < 2:
-                        top[lev, r, :, n : n + 128] = x
-                    if target is rows and r >= RL - 2:
-                        bottom[lev, r - RL + 2, :, n : n + 128] = x
+            wide[k, n // 128, 0 : C * RL, :] = source[0, :, n : n + 128].astype(F32)
+            wide[k, n // 128, C * RL :, :] = jnp.zeros((12 * RL, 128), F32)
+        for r in range(RL):
+            for n in range(0, NC, 128):
+                x = wide[k, n // 128, pl.ds(r, CP, stride=RL), :].astype(BF)
+                target[0, r, :, n : n + 128] = x
+                if k == 0 and r < 2:
+                    top[0, r, :, n : n + 128] = x
+                if k == 0 and r >= RL - 2:
+                    bottom[0, r - RL + 2, :, n : n + 128] = x
 
 
 def window(ref, i, count):
     return ref[i : i + count].reshape(count * GR, NC)
 
 
-def kernel_b(place, rows, above, below, w_one, w_two, w_point, after, mid_taps, slope, pre, taps):
+def kernel_b(place, rows, above, below, w_one, w_two, w_point, after, middle, slope, pre, taps, mid_taps):
     index = place[0]
     source = [above.at[0, 0], above.at[0, 1]] + [rows.at[0, r] for r in range(RL)] + [below.at[0, 0], below.at[0, 1]]
     for i, x in enumerate(source):
@@ -215,9 +217,11 @@
                 keep = jnp.where(index == (0 if i == 0 else SP - 1), 0.0, 1.0).astype(F32)
                 value, gradient = value * keep, gradient * keep
             slope[0, i] = gradient
-            store_taps(mid_taps.at[0], i, jnp.concatenate([value, rest], axis=0))
+            value = jnp.concatenate([value, rest], axis=0)
+            middle[0, i] = value.astype(BF)
+            store_taps(mid_taps, i, value)
     for r in (0, 4):
-        d = dot(w_two[...], window(mid_taps.at[0], r, 6))
+        d = dot(w_two[...], window(mid_taps, r, 6))
         d = d + dot(w_point[...], rows[0, r : r + 4].reshape(4 * CP, NC))
         for t in range(4):
             pre[0, r + t] = d[t * CP : t * CP + CO]
@@ -297,10 +301,6 @@
     grad[...] = lines[:, 0:C]
 
 
-def kernel_share(gathered, first, second, share):
-    share[...] = jnp.sum(gathered[:, 32:48].astype(F32), axis=0)
-
-
 def kernel_d(received, high, low, inverse, pre, cot, table, scale, values, slopes, top, bottom, message, left, spec, kept, cols):
     lev = pl.program_id(0)
 
@@ -338,24 +338,33 @@
                 x = values[lev, r, :, n : n + 128].astype(F32)
                 wide[n // 128, pl.ds(lev * C * RL + r, C, stride=RL), :] = x[0:C]
     for n in range(0, NC, 128):
-        out[:, n : n + 128] = wide[n // 128].astype(BF)
-
-
-def kernel_mix_back(received, weight, kept, cofield, pair, mixed, lines):
-    own = own_modes(received[...])
-    pair[0:32] = kept[...]
-    pair[32:64] = own
+        for lev in range(LEV):
+            out[lev, :, n : n + 128] = wide[n // 128, lev * C * RL : (lev + 1) * C * RL].astype(BF)
+
+
+def kernel_own(received, kept, first, second, sums):
+    sums[0:32] = kept[...]
+    sums[32:64] = own_modes(received[:, 0:32])
+    sums[64:80] = own_modes(received[:, 32:48])
+
+
+def kernel_mix_back(sums, weight, cofield, mixed, lines):
     weight_rows(weight, lines)
-    cofield[...] = mix_back(own, lines, mixed)
-
-
-def kernel_e_zero(slopes, mid_taps, rows, grad_two):
-    none = jnp.zeros((CP, NC), BF)
+    cofield[...] = mix_back(sums[32:64], lines, mixed)
+
+
+def kernel_send_back(cofield, p0, p1, p2, p3, message):
+    total = (p0[64:80] + p1[64:80]) + (p2[64:80] + p3[64:80])
+    high, low = split(total)
+    message[...] = jnp.broadcast_to(jnp.concatenate([cofield[...], high, low], axis=0)[None], (SP, 64, 128))
+
+
+def kernel_e_zero(slopes, middle, rows, grad_two, taps):
     left, right = [], []
-    for i in range(RL + 2):
-        inside = 1 <= i <= RL
-        left.append(jnp.concatenate([mid_taps[0, i], rows[0, i - 1] if inside else none], axis=0))
-        right.append(jnp.concatenate([slopes[0, r] if 0 <= r < RL else none for r in (i, i - 1, i - 2)], axis=0))
+    for r in range(RL):
+        store_taps(taps, r, slopes[0, r].astype(F32))
+        left.append(jnp.concatenate([middle[0, r], middle[0, r + 1], middle[0, r + 2], rows[0, r]], axis=0))
+        right.append(taps[r])
     part = dot_nt(jnp.concatenate(left, axis=1), jnp.concatenate(right, axis=1))
 
     @pl.when(pl.program_id(0) == 0)
@@ -367,7 +376,7 @@
         grad_two[...] += part
 
 
-def kernel_e(place, slopes, above, below, rows, f_above, f_below, slope, w_two, cofield, grad_two, pre_taps, message, taps, grad_one, sums):
+def kernel_e(place, slopes, above, below, rows, f_above, f_below, slope, w_two, modes, grad_two, pre_slope, message, taps, pre_taps, grad_one, sums):
     index = place[0]
     lev = pl.program_id(0)
     source = [above.at[0, 0], above.at[0, 1]] + [slopes.at[0, r] for r in range(RL)] + [below.at[0, 0], below.at[0, 1]]
@@ -381,10 +390,12 @@
             value = d[t * CP : t * CP + CO] * slope[0, i]
             if i in (0, RL + 1):
                 value = value * jnp.where(index == (0 if i == 0 else SP - 1), 0.0, 1.0).astype(F32)
-            store_taps(pre_taps.at[0], i, jnp.concatenate([value, rest], axis=0))
+            value = jnp.concatenate([value, rest], axis=0)
+            pre_slope[0, i] = value.astype(BF)
+            store_taps(pre_taps, i, value)
     field = [f_above[0, 1]] + [rows[0, r] for r in range(RL)] + [f_below[0, 0]]
     left = jnp.concatenate([jnp.concatenate(field[r : r + 3], axis=0) for r in range(RL)], axis=1)
-    right = jnp.concatenate([pre_taps[0, r + 1] for r in range(RL)], axis=1)
+    right = jnp.concatenate([pre_taps[r + 1] for r in range(RL)], axis=1)
     part_one = dot_nt(left, right)
 
     @pl.when(lev == 0)
@@ -399,41 +410,47 @@
             sums[b * GR : (b + 1) * GR, 0:CP] = two[0:GR, b * CP : (b + 1) * CP]
             sums[b * GR : (b + 1) * GR, 64 : 64 + CP] = one[:, b * CP : (b + 1) * CP]
         sums[3 * GR : 3 * GR + CP, 0:CP] = two[GR : GR + CP, CP : 2 * CP]
-        message[:, 0:32] = jnp.broadcast_to(cofield[...][None], (SP, 32, 128))
+        message[:, 0:32] = modes[...]
         message[:, 32:48] = sums[...].reshape(SP, 16, 128).astype(BF)
 
 
-def kernel_e_two(pre_taps, slopes, w_one, w_point, after, back):
+def kernel_e_two(pre_slope, slopes, w_one, w_point, after, back, taps, wide):
+    for i in range(RL + 2):
+        store_taps(taps, i, pre_slope[0, i].astype(F32))
     for r in (0, 4):
-        d = dot(w_one[...], window(pre_taps.at[0], r, 6))
+        d = dot(w_one[...], window(taps, r, 6))
         d = d + dot(w_point[...], slopes[0, r : r + 4].reshape(4 * CP, NC))
         for t in range(4):
-            back[0, r + t] = d[t * CP : t * CP + CO]
-
-
-def kernel_f(received, high, low, inverse, back, out, left, spec, wide):
-    modes = received[:, 0:32].reshape(SP * 32, 128)
-    place_rows(row_expand(modes, high[...], low[...]), left)
-    spec[...] = dot(left[...].astype(BF), inverse[...])
-    for lev in range(LEV):
-        for r in range(RL):
-            at = (lev * RL + r) * CO
-            value = back[lev, r] + spec[at : at + CO, :]
             for n in range(0, NC, 128):
-                wide[n // 128, pl.ds(lev * C * RL + r, C, stride=RL), :] = value[0:C, n : n + 128]
+                wide[n // 128, pl.ds(r + t, C, stride=RL), :] = d[t * CP : t * CP + C, n : n + 128]
     for n in range(0, NC, 128):
-        out[:, n : n + 128] = wide[n // 128].astype(BF)
-
-
-def kernel_last(sums, point, one, two):
-    scaled = sums[...] * (1.0 / math.sqrt(NR * NC * LEV * 4))
-    for a in range(3):
-        for b in range(3):
-            at = a * GR + b * CP
-            two[a, b] = scaled[at : at + C, 0:C]
-            at = (2 - b) * GR + a * CP
-            one[a, b] = scaled[at : at + C, 64 : 64 + C]
-    point[...] = scaled[3 * GR : 3 * GR + C, 0:C]
+        back[0, :, n : n + 128] = wide[n // 128]
+
+
+def kernel_f(received, high, low, inverse, back, out, point, one, two, left):
+    lev = pl.program_id(0)
+
+    @pl.when(lev == 0)
+    def _():
+        modes = received[:, 0:32].reshape(SP * 32, 128)
+        r_high, r_low = split(row_expand(modes, high[...], low[...]))
+        r_high, r_low = r_high.astype(F32), r_low.astype(F32)
+        rest = jnp.zeros((C, 56), F32)
+        for at in range(LEV):
+            for r in range(RL):
+                h = r_high[at * 64 : at * 64 + C, r * 24 : r * 24 + 24]
+                w = r_low[at * 64 : at * 64 + C, r * 24 : r * 24 + 24]
+                left[at, pl.ds(r, C, stride=RL), :] = jnp.concatenate([h, h, w, rest], axis=1)
+        total = (received[:, 32:48].astype(F32) + received[:, 48:64].astype(F32)).reshape(SP * 16, 128)
+        scaled = total * (1.0 / math.sqrt(NR * NC * LEV * 4))
+        for a in range(3):
+            for b in range(3):
+                at = (2 - b) * GR + a * CP
+                two[a, b] = scaled[at : at + C, 0:C]
+                one[a, b] = scaled[at : at + C, 64 : 64 + C]
+        point[...] = scaled[3 * GR : 3 * GR + C, 0:C]
+
+    out[0] = (back[0] + dot(left[lev].astype(BF), inverse[...])).astype(BF)
 
 
 def shape(dims, kind):
@@ -491,13 +508,11 @@
 def local(field, cotangent, spec_weight, point_weight, kernel_one, kernel_two):
     place = lax.axis_index("sp").astype(jnp.int32).reshape(1)
     inputs = field.reshape(LEV * C * RL, NC)
-    upstream = cotangent.reshape(LEV * C * RL, NC)
     table = jnp.asarray(TABLE)
     weight = jnp.transpose(spec_weight, (1, 3, 0, 2)).reshape(C * QN * 2, C)
     strip = shape((LEV, 2, CP, NC), BF)
     grid_rows = shape((LEV, RL, CP, NC), BF)
-    natural = shape((LEV * C * RL, NC), BF)
-    relayout = pltpu.VMEM((NC // 128, (LEV * C + 12) * RL, 128), F32)
+    natural = shape((LEV, C * RL, NC), BF)
     flat, cols = pltpu.VMEM((LEV * C * RL, 128), F32), pltpu.VMEM((128, 256), F32)
     row_matrix = shape((SP * 32, 256), BF)
     message, high, low = plain_call(
@@ -512,15 +527,29 @@
     )
     arrived = exchange(message.reshape(SP, 32, 128))
     toeplitz, blocks = shape((4 * CP, 6 * GR), BF), shape((4 * CP, 4 * CP), BF)
-    rows, top, bottom, cot_rows, w_one, w_two, w_two_back, w_one_back, w_point, w_point_back = plain_call(
+    weights_out = [toeplitz] * 4 + [blocks] * 2
+    rows, top, bottom, cot_rows, w_one, w_two, w_two_back, w_one_back, w_point, w_point_back = pl.pallas_call(
         kernel_rows,
-        (inputs, upstream, kernel_one, kernel_two, point_weight),
-        (message,),
-        [grid_rows, strip, strip, grid_rows] + [toeplitz] * 4 + [blocks] * 2,
-        [relayout, pltpu.VMEM((CP, 9 * CP), F32), pltpu.VMEM((4 * CP, 6 * GR), F32)],
-        12,
-        "row_layout",
-    )
+        grid=(LEV,),
+        in_specs=[
+            level_spec(C * RL, NC),
+            level_spec(C * RL, NC),
+            whole_spec(3, 3, C, C),
+            whole_spec(3, 3, C, C),
+            whole_spec(C, C),
+            anywhere(),
+        ],
+        out_specs=[level_spec(RL, CP, NC), level_spec(2, CP, NC), level_spec(2, CP, NC), level_spec(RL, CP, NC)]
+        + [whole_spec(*x.shape) for x in weights_out],
+        out_shape=[grid_rows, strip, strip, grid_rows] + weights_out,
+        scratch_shapes=[
+            pltpu.VMEM((2, NC // 128, (C + 12) * RL, 128), F32),
+            pltpu.VMEM((CP, 9 * CP), F32),
+            pltpu.VMEM((4 * CP, 6 * GR), F32),
+        ],
+        compiler_params=params(12),
+        name="row_layout",
+    )(field.reshape(natural.shape), cotangent.reshape(natural.shape), kernel_one, kernel_two, point_weight, message)
     f_above, f_below = from_above(bottom), from_below(top)
 
     square, lines = pltpu.VMEM((128, 128), F32), pltpu.VMEM((C * QN * 2, 128), F32)
@@ -535,7 +564,7 @@
     )
     gathered = exchange(mixed).reshape(SP * 32, 128)
 
-    mid_taps, slope, pre = pl.pallas_call(
+    middle, slope, pre = pl.pallas_call(
         kernel_b,
         grid=(LEV,),
         in_specs=[
@@ -549,16 +578,16 @@
             anywhere(),
         ],
         out_specs=[
-            level_spec(RL + 2, GR, NC),
+            level_spec(RL + 2, CP, NC),
             level_spec(RL + 2, CO, NC),
             level_spec(RL, CO, NC),
         ],
         out_shape=[
-            shape((LEV, RL + 2, GR, NC), BF),
+            shape((LEV, RL + 2, CP, NC), BF),
             shape((LEV, RL + 2, CO, NC), F32),
             shape((LEV, RL, CO, NC), F32),
         ],
-        scratch_shapes=[pltpu.VMEM((RL + 4, GR, NC), BF)],
+        scratch_shapes=[pltpu.VMEM((RL + 4, GR, NC), BF), pltpu.VMEM((RL + 2, GR, NC), BF)],
         compiler_params=params(28),
         name="two_convolutions",
     )(place, rows, f_above, f_below, w_one, w_two, w_point, mixed)
@@ -588,29 +617,19 @@
         compiler_params=params(22),
         name="output_and_slope",
     )(gathered, high, low, jnp.asarray(INVERSE), pre, cot_rows, table, jnp.asarray(SCALE))
-    arrived = exchange(message.reshape(SP, 32, 128))
     s_above, s_below = from_above(s_bottom), from_below(s_top)
 
     grad_two = pl.pallas_call(
         kernel_e_zero,
         grid=(LEV,),
-        in_specs=[level_spec(RL, CP, NC), level_spec(RL + 2, GR, NC), level_spec(RL, CP, NC)],
+        in_specs=[level_spec(RL, CP, NC), level_spec(RL + 2, CP, NC), level_spec(RL, CP, NC)],
+        scratch_shapes=[pltpu.VMEM((RL, GR, NC), BF)],
         out_specs=whole_spec(GR + CP, GR),
         out_shape=shape((GR + CP, GR), F32),
         compiler_params=params(22),
         name="weight_gradients_two",
-    )(slopes, mid_taps, rows)
-    cofield, pair = plain_call(
-        kernel_mix_back,
-        (arrived, weight, kept),
-        (),
-        [shape((32, 128), BF), shape((64, 128), F32)],
-        [square, lines],
-        6,
-        "mode_mix_back",
-        cost=15,
-    )
-    pre_taps, message = pl.pallas_call(
+    )(slopes, middle, rows)
+    pre_slope, message = pl.pallas_call(
         kernel_e,
         grid=(LEV,),
         in_specs=[
@@ -623,79 +642,83 @@
             level_spec(2, CP, NC),
             level_spec(RL + 2, CO, NC),
             whole_spec(4 * CP, 6 * GR),
-            whole_spec(32, 128),
+            whole_spec(SP, 32, 128),
             whole_spec(GR + CP, GR),
         ],
-        out_specs=[level_spec(RL + 2, GR, NC), whole_spec(SP, 48, 128)],
-        out_shape=[shape((LEV, RL + 2, GR, NC), BF), shape((SP, 48, 128), BF)],
+        out_specs=[level_spec(RL + 2, CP, NC), whole_spec(SP, 48, 128)],
+        out_shape=[shape((LEV, RL + 2, CP, NC), BF), shape((SP, 48, 128), BF)],
         scratch_shapes=[
             pltpu.VMEM((RL + 4, GR, NC), BF),
+            pltpu.VMEM((RL + 2, GR, NC), BF),
             pltpu.VMEM((GR, GR), F32),
             pltpu.VMEM((SP * 16, 128), F32),
         ],
         compiler_params=params(28),
         name="slope_and_weight_gradients",
-    )(place, slopes, s_above, s_below, rows, f_above, f_below, slope, w_two_back, cofield, grad_two)
+    )(place, slopes, s_above, s_below, rows, f_above, f_below, slope, w_two_back, message.reshape(SP, 32, 128), grad_two)
+    arrived = exchange(message)
+    back = pl.pallas_call(
+        kernel_e_two,
+        grid=(LEV,),
+        in_specs=[
+            level_spec(RL + 2, CP, NC),
+            level_spec(RL, CP, NC),
+            whole_spec(4 * CP, 6 * GR),
+            whole_spec(4 * CP, 4 * CP),
+            anywhere(),
+        ],
+        out_specs=level_spec(C * RL, NC),
+        out_shape=shape(natural.shape, F32),
+        scratch_shapes=[pltpu.VMEM((RL + 2, GR, NC), BF), pltpu.VMEM((NC // 128, C * RL, 128), F32)],
+        compiler_params=params(22),
+        name="backward_convolution",
+    )(pre_slope, slopes, w_one_back, w_point_back, message)
+    (out,) = plain_call(
+        kernel_out,
+        (values,),
+        (message,),
+        [natural],
+        [pltpu.VMEM((NC // 128, LEV * C * RL, 128), F32)],
+        10,
+        "output_layout",
+    )
+    (sums,) = plain_call(
+        kernel_own, (arrived, kept), (back, out), [shape((80, 128), F32)], [], 4, "own_sums"
+    )
+    others = [lax.ppermute(sums, "rep", [(i, i ^ k) for i in range(4)]) for k in (1, 2, 3)]
+    (cofield,) = plain_call(
+        kernel_mix_back, (sums, weight), (), [shape((32, 128), BF)], [square, lines], 6, "mode_mix_back"
+    )
+    (message,) = plain_call(
+        kernel_send_back, (cofield, sums, *others), (), [shape((SP, 64, 128), BF)], [], 4, "gradient_modes"
+    )
     gathered = exchange(message)
-    others = [lax.ppermute(pair, "rep", [(i, i ^ k) for i in range(4)]) for k in (1, 2, 3)]
     (spec_grad,) = plain_call(
         kernel_spec_grad,
-        (pair, *others),
+        (sums, *others),
         (message,),
         [shape(weight.shape, F32)],
         [pltpu.VMEM((4, 128, 128), F32)] * 2 + [lines],
         8,
         "spectral_gradient",
     )
-    back = pl.pallas_call(
-        kernel_e_two,
+    kernel_out_shape = shape((3, 3, C, C), F32)
+    field_grad, point_total, one_total, two_total = pl.pallas_call(
+        kernel_f,
         grid=(LEV,),
         in_specs=[
-            level_spec(RL + 2, GR, NC),
-            level_spec(RL, CP, NC),
-            whole_spec(4 * CP, 6 * GR),
-            whole_spec(4 * CP, 4 * CP),
-            anywhere(),
-        ],
-        out_specs=level_spec(RL, CO, NC),
-        out_shape=shape((LEV, RL, CO, NC), F32),
-        compiler_params=params(22),
-        name="backward_convolution",
-    )(pre_taps, slopes, w_one_back, w_point_back, message)
-
-    (shares,) = plain_call(
-        kernel_share, (gathered,), (back, spec_grad), [shape((16, 128), F32)], [], 4, "weight_gradient_shares"
-    )
-    shares = jnp.sum(lax.all_gather(shares, "rep", axis=0), axis=0)
-    every = exchange(jnp.broadcast_to(shares[None], (SP, 16, 128)))
-    (out,) = plain_call(
-        kernel_out,
-        (values,),
-        (shares,),
-        [natural],
-        [pltpu.VMEM((NC // 128, LEV * C * RL, 128), F32)],
-        10,
-        "output_layout",
-    )
-    (field_grad,) = plain_call(
-        kernel_f,
-        (gathered, high, low, jnp.asarray(BACK), back),
-        (),
-        [natural],
-        [left, spec, pltpu.VMEM((NC // 128, LEV * C * RL, 128), F32)],
-        18,
-        "field_gradient",
-    )
-    kernel_out_shape = shape((3, 3, C, C), F32)
-    point_total, one_total, two_total = plain_call(
-        kernel_last,
-        (every.reshape(SP * 16, 128),),
-        (),
-        [shape((C, C), F32), kernel_out_shape, kernel_out_shape],
-        [],
-        4,
-        "weight_gradients",
-    )
+            whole_spec(SP, 64, 128),
+            whole_spec(SP * 32, 256),
+            whole_spec(SP * 32, 256),
+            whole_spec(128, NC),
+            level_spec(C * RL, NC),
+        ],
+        out_specs=[level_spec(C * RL, NC), whole_spec(C, C), whole_spec(3, 3, C, C), whole_spec(3, 3, C, C)],
+        out_shape=[natural, shape((C, C), F32), kernel_out_shape, kernel_out_shape],
+        scratch_shapes=[pltpu.VMEM((LEV, C * RL, 128), F32)],
+        compiler_params=params(18),
+        name="field_gradient",
+    )(gathered, high, low, jnp.asarray(BACK), back)
     spec_total = jnp.transpose(spec_grad.reshape(C, QN, 2, C), (2, 0, 3, 1))
     return (
         out.reshape(field.shape),

time: 153 us -> 144 us (0.941)
  waiting for transfers between devices: 3.86 us -> 14.9 us
  starting transfers between devices: 67.1 us -> 58.3 us
  blocking collectives: 5.71 us -> 0 us
  Pallas kernels: 67.4 us -> 62.6 us
    pallas_call x9 -> x7, Pallas kernels: 30 us -> 18.6 us  [plain_call(): pl.pallas_call(kernel, in_specs=[pl.BlockSpec(memory_space=pltpu.SMEM)] *...]
    all_to_all x5 -> x4, starting transfers between devices: 52.2 us -> 43 us  [exchange(): return lax.all_to_all(x, 'sp', 0, 0, tiled=True)]
    pallas_call x1 -> x3, Pallas kernels: 5.66 us -> 14.7 us  [the longest x1 5.57 us: local(): pl.pallas_call(kernel_e_two, grid=(LEV,), in_specs=[level_spec(RL + 2, CP...]
    all_to_all x5 -> x4, waiting for transfers between devices: 1.74 us -> 10.1 us  [exchange(): return lax.all_to_all(x, 'sp', 0, 0, tiled=True)]
    all_gather x1 -> x0, blocking collectives: 5.71 us -> none  [local(): shares = jnp.sum(lax.all_gather(shares, 'rep', axis=0), axis=0)]
    ppermute x2, waiting for transfers between devices: 2.11 us -> 3.75 us  [from_below(): return lax.ppermute(x, 'sp', [(i + 1, i) for i in range(SP - 1)])]
    unnamed x28 -> x22, local copies, waits for them, and re-layouts: 6.41 us -> 5.78 us
  transfers between devices with their start and end apart: 12 -> 11, of which waited for: 2 -> 6; matrix products, arithmetic and copies ran while one was open for 0% -> 0% of each run, Pallas kernels for 28% -> 24%
where the time goes in v3:
time: 144 us; the launch traced here: 142 us
  Pallas kernels  62.6 us (43%)
  starting transfers between devices  58.3 us (40%)
  waiting for transfers between devices  14.9 us (10%)
  local copies, waits for them, and re-layouts  5.78 us (4%)
    all_to_all x4, starting transfers between devices, exchange(): return lax.all_to_all(x, 'sp', 0, 0, tiled=True)  43 us
    pallas_call x7, Pallas kernels, plain_call(): pl.pallas_call(kernel, in_specs=[pl.BlockSpec(memory_space=pltpu.SMEM)] *...  18.6 us
    all_to_all x4, waiting for transfers between devices, exchange(): return lax.all_to_all(x, 'sp', 0, 0, tiled=True)  10.1 us
    pallas_call x1, Pallas kernels, local(): pl.pallas_call(kernel_e, grid=(LEV,), in_specs=[pl.BlockSpec(memory_space...  9.16 us
    pallas_call x1, Pallas kernels, local(): pl.pallas_call(kernel_b, grid=(LEV,), in_specs=[pl.BlockSpec(memory_space...  8.61 us
    pallas_call x1, Pallas kernels, local(): pl.pallas_call(kernel_d, grid=(LEV,), in_specs=[whole_spec(SP * 32, 128),...  7.08 us
    ppermute x3, starting transfers between devices, local(): lax.ppermute(sums, 'rep', [(i, i ^ k) for i in range(4)])  6.27 us
    ppermute x2, starting transfers between devices, from_above(): return lax.ppermute(x, 'sp', [(i, i + 1) for i in range(SP - 1)])  6.24 us
  transfers between devices with their start and end apart: 11, of which 6 were waited for; matrix products, arithmetic and copies ran while one was open for 0% of the time, Pallas kernels for 24%

profile of v3, /device:TPU:1, one launch (start us, length us, event | category | flops | bytes accessed | tf_op | source)
XLA Modules:
  0.0 142.4 jit_solution(14599750065740657178)
XLA Ops:
  0.6 4.7 %field_modes.1 = (bf16[1024,128]{1,0:T(8,128)(2,1)}, bf16[1024,256]{1,0:T(8,128)(2,1)}, bf16[1024,256]{1,0:T(8,128)(2,1)}) custom-call(s32[1]{0:T(128)} %bitcast.place, bf16[576,1024]{1,0:T(8,128)(2,1)} %bitcast.15, bf16[1024,128]{1,0:T(8,128)(2,1)} %constant.18.clone.table, bf16[1024,256]{1,0:T(8,128)(2,1)} %constant.19.clone.high, ...), custom_call_target="tpu_custom_call" | custom-call | tf_op jit(solution)/shard_map/field_modes/pallas_call | solution.py:496
  5.3 11.3 %all-to-all-start = ((bf16[32,32,128]{2,1,0:T(8,128)(2,1)}), bf16[32,32,128]{2,1,0:T(8,128)(2,1)S(1)}, u32[]{:S(2)}, u32[]{:S(2)}) async-start(bf16[32,32,128]{2,1,0:T(8,128)(2,1)} %bitcast.22), calls=%async_computation | async-start | bytes 524288 | tf_op jit(solution)/shard_map/all_to_all | solution.py:487
  16.7 5.4 %row_layout.1 = (bf16[2,8,48,1024]{3,2,1,0:T(8,128)(2,1)}, bf16[2,2,48,1024]{3,2,1,0:T(8,128)(2,1)}, bf16[2,2,48,1024]{3,2,1,0:T(8,128)(2,1)}, bf16[2,8,48,1024]...) custom-call(bf16[2,288,1024]{2,1,0:T(8,128)(2,1)} %bitcast.16, ...), custom_call_target="tpu_custom_call" | custom-call | tf_op jit(solution)/shard_map/row_layout/pallas_call | solution.py:531
  22.1 3.2 %collective-permute-start = (bf16[2,2,48,1024]{3,2,1,0:T(8,128)(2,1)}, bf16[2,2,48,1024]{3,2,1,0:T(8,128)(2,1)S(1)}, u32[]{:S(2)}, u32[]{:S(2)}) collective-permute-start(bf16[2,2,48,1024]{3,2,1,0:T(8,128)(2,1)} %get-tuple-element.40), channel_id=1, source_target_pairs={{0,1},{1,2},{2,3},{3,4},{4,5},{5,6},{6,7},{7,8},{8,9},{9,10},{10,1... | collective-permute-start | bytes 1179656 | tf_op jit(solution)/shard_map/ppermute | solution.py:479
  25.2 1.3 collective-permute-start.1
  27.3 2.5 %mode_mix.1 = (bf16[32,32,128]{2,1,0:T(8,128)(2,1)}, f32[32,128]{1,0:T(8,128)}) custom-call(bf16[32,32,128]{2,1,0:T(8,128)(2,1)} %copy-done.5, f32[648,36]{1,0:T(8,128)} %bitcast.18), custom_call_target="tpu_custom_call" | custom-call | tf_op jit(solution)/shard_map/mode_mix/pallas_call | solution.py:496
  29.7 11.3 %all-to-all-start.1 = ((bf16[32,32,128]{2,1,0:T(8,128)(2,1)}), bf16[32,32,128]{2,1,0:T(8,128)(2,1)S(1)}, u32[]{:S(2)}, u32[]{:S(2)}) async-start(bf16[32,32,128]{2,1,0:T(8,128)(2,1)} %get-tuple-element.36.after), calls=%async_computation.1 | async-start | bytes 524288 | tf_op jit(solution)/shard_map/all_to_all | solution.py:487
  41.1 0.7 copy-done.1
  41.9 8.6 %two_convolutions.1 = (bf16[2,10,48,1024]{3,2,1,0:T(8,128)(2,1)}, f32[2,10,40,1024]{3,2,1,0:T(8,128)}, f32[2,8,40,1024]{3,2,1,0:T(8,128)}) custom-call(s32[1]{0:T(128)} %bitcast.place, bf16[2,8,48,1024]{3,2,1,0:T(8,128)(2,1)} %get-tuple-element.39.rows, bf16[2,2,48,1024]{3,2,1,0:T(8,128)(2,1)} %copy-done.1, bf16[2,2,48,1024]{3,2,1,0:T(8,128)(2,1)} %copy-done.2, ...), custom_call_target="tpu_custom_call" | custom-call | tf_op jit(solution)/shard_map/two_convolutions/pallas_call | solution.py:567
  50.6 0.7 copy-done.4
  51.3 7.1 %output_and_slope.1 = (bf16[2,8,48,1024]{3,2,1,0:T(8,128)(2,1)}, bf16[2,8,48,1024]{3,2,1,0:T(8,128)(2,1)}, bf16[2,2,48,1024]{3,2,1,0:T(8,128)(2,1)}, bf16[2,2,48,1024]{3,2,1,0:T(8,128)(2,1)}, bf16[1024,128]{1,0:T(8,128)(2,1)}) custom-call(bf16[1024,128]{1,0:T(8,128)(2,1)} %bitcast.21, bf16[1024,256]{1,0:T(8,128)(2,1)} %get-tuple-element.37.high, ...), custom_call_target="tpu_custom_call" | custom-call | tf_op jit(solution)/shard_map/output_and_slope/pallas_call | solution.py:596
  58.4 3.1 %collective-permute-start.2 = (bf16[2,2,48,1024]{3,2,1,0:T(8,128)(2,1)}, bf16[2,2,48,1024]{3,2,1,0:T(8,128)(2,1)S(1)}, u32[]{:S(2)}, u32[]{:S(2)}) collective-permute-start(bf16[2,2,48,1024]{3,2,1,0:T(8,128)(2,1)} %get-tuple-element.49), channel_id=1, source_target_pairs={{0,1},{1,2},{2,3},{3,4},{4,5},{5,6},{6,7},{7,8},{8,9},{9,10},{10,1... | collective-permute-start | bytes 1179656 | tf_op jit(solution)/shard_map/ppermute | solution.py:479
  61.5 1.5 %collective-permute-start.3 = (bf16[2,2,48,1024]{3,2,1,0:T(8,128)(2,1)}, bf16[2,2,48,1024]{3,2,1,0:T(8,128)(2,1)S(1)}, u32[]{:S(2)}, u32[]{:S(2)}) collective-permute-start(bf16[2,2,48,1024]{3,2,1,0:T(8,128)(2,1)} %get-tuple-element.50), channel_id=1, source_target_pairs={{1,0},{2,1},{3,2},{4,3},{5,4},{6,5},{7,6},{8,7},{9,8},{10,9},{11,1... | collective-permute-start | bytes 1179656 | tf_op jit(solution)/shard_map/ppermute | solution.py:483
  63.0 4.5 %weight_gradients_two.1.grad_two = f32[192,144]{1,0:T(8,128)} custom-call(bf16[2,8,48,1024]{3,2,1,0:T(8,128)(2,1)} %get-tuple-element.48.slopes, bf16[2,10,48,1024]{3,2,1,0:T(8,128)(2,1)} %get-tuple-element.54.middle, bf16[2,8,48,1024]{3,2,1,0:T(8,128)(2,1)} %get-tuple-element.39.rows), custom_call_target="tpu_custom_call" | custom-call | tf_op jit(solution)/shard_map/weight_gradients_two/pallas_call | solution.py:622
  67.8 3.7 %collective-permute-done.3.below = bf16[2,2,48,1024]{3,2,1,0:T(8,128)(2,1)S(1)} collective-permute-done((bf16[2,2,48,1024]{3,2,1,0:T(8,128)(2,1)}, bf16[2,2,48,1024]{3,2,1,0:T(8,128)(2,1)S(1)}, u32[]{:S(2)}, u32[]{:S(2)}) %collective-permute-start.3) | collective-permute-done | bytes 393248 | tf_op jit(solution)/shard_map/ppermute | solution.py:483
  71.6 0.8 copy-done.7
  72.3 9.2 %slope_and_weight_gradients.1 = (bf16[2,10,48,1024]{3,2,1,0:T(8,128)(2,1)}, bf16[32,48,128]{2,1,0:T(8,128)(2,1)}) custom-call(s32[1]{0:T(128)} %bitcast.place, bf16[2,8,48,1024]{3,2,1,0:T(8,128)(2,1)} %get-tuple-element.48.slopes, bf16[2,2,48,1024]{3,2,1,0:T(8,128)(2,1)} %copy-done.6, bf16[2,2,48,1024]{3,2,1,0:T(8,128)(2,1)} %copy-done.7, ...), custom_call_target="tpu_custom_call" | custom-call | tf_op jit(solution)/shard_map/slope_and_weight_gradients/pallas_call | solution.py:632
  81.5 13.1 %all-to-all-start.2 = ((bf16[32,48,128]{2,1,0:T(8,128)(2,1)}), bf16[32,48,128]{2,1,0:T(8,128)(2,1)S(1)}, u32[]{:S(2)}, u32[]{:S(2)}) async-start(bf16[32,48,128]{2,1,0:T(8,128)(2,1)} %get-tuple-element.55.after), calls=%async_computation.2 | async-start | bytes 786432 | tf_op jit(solution)/shard_map/all_to_all | solution.py:487
  94.6 3.4 %output_layout.1.second = bf16[2,288,1024]{2,1,0:T(8,128)(2,1)} custom-call(bf16[2,8,48,1024]{3,2,1,0:T(8,128)(2,1)} %get-tuple-element.47.values, bf16[32,48,128]{2,1,0:T(8,128)(2,1)} %get-tuple-element.55.after), custom_call_target="tpu_custom_call" | custom-call | tf_op jit(solution)/shard_map/output_layout/pallas_call | solution.py:496
  98.0 5.6 %backward_convolution.1.first.back = f32[2,288,1024]{2,1,0:T(8,128)} custom-call(bf16[2,10,48,1024]{3,2,1,0:T(8,128)(2,1)} %get-tuple-element.57.pre_slope, bf16[2,8,48,1024]{3,2,1,0:T(8,128)(2,1)} %get-tuple-element.48.slopes, bf16[192,864]{1,0:T(8,128)(2,1)} %get-tuple-element.58.w_one, bf16[192,192]{1,0:T(8,128)(2,1)} %get-tuple-element.59.w_point, ...), custom_call_target="tpu_custom_call" | custom-call | tf_op jit(solution)/shard_map/backward_convolution/pallas_call | solution.py:660
  103.6 1.2 all-to-all-done.2.received
  104.8 0.7 copy-done.3
  105.5 1.7 %own_sums.1.sums.p0 = f32[80,128]{1,0:T(8,128)} custom-call(bf16[32,48,128]{2,1,0:T(8,128)(2,1)} %copy-done.3, f32[32,128]{1,0:T(8,128)} %get-tuple-element.56.kept, f32[2,288,1024]{2,1,0:T(8,128)} %backward_convolution.1.first.back, bf16[2,288,1024]{2,1,0:T(8,128)(2,1)} %output_layout.1.second), custom_call_target="tpu_custom_call" | custom-call | tf_op jit(solution)/shard_map/own_sums/pallas_call | solution.py:496
  107.2 5.2 %collective-permute-start.6 = (f32[80,128]{1,0:T(8,128)}, f32[80,128]{1,0:T(8,128)S(1)}, u32[]{:S(2)}, u32[]{:S(2)}) collective-permute-start(f32[80,128]{1,0:T(8,128)} %own_sums.1.sums.p0), channel_id=1, source_target_pairs={{0,96},{32,64},{64,32},{96,0},{1,97},{33,65},{65,33},{97,1},{2,98}... | collective-permute-start | bytes 122888 | tf_op jit(solution)/shard_map/ppermute | solution.py:688
  112.4 1.1 collective-permute-start.5
  113.5 2.0 %mode_mix_back.1.cofield = bf16[32,128]{1,0:T(8,128)(2,1)} custom-call(f32[80,128]{1,0:T(8,128)} %own_sums.1.sums.p0, f32[648,36]{1,0:T(8,128)} %bitcast.19), custom_call_target="tpu_custom_call" | custom-call | tf_op jit(solution)/shard_map/mode_mix_back/pallas_call | solution.py:496
  117.4 1.7 %gradient_modes.1.after = bf16[32,64,128]{2,1,0:T(8,128)(2,1)} custom-call(bf16[32,128]{1,0:T(8,128)(2,1)} %mode_mix_back.1.cofield, f32[80,128]{1,0:T(8,128)} %own_sums.1.sums.p0, f32[80,128]{1,0:T(8,128)} %copy-done.10, f32[80,128]{1,0:T(8,128)} %copy-done.9, f32[80,128]{1,0:T(8,128)} %copy-done.8), custom_call_target="tpu_custom_call" | custom-call | tf_op jit(solution)/shard_map/gradient_modes/pallas_call | solution.py:496
  119.1 7.3 %all-to-all-start.3 = ((bf16[32,64,128]{2,1,0:T(8,128)(2,1)}), bf16[32,64,128]{2,1,0:T(8,128)(2,1)S(1)}, u32[]{:S(2)}, u32[]{:S(2)}) async-start(bf16[32,64,128]{2,1,0:T(8,128)(2,1)} %gradient_modes.1.after), calls=%async_computation.3 | async-start | bytes 1048576 | tf_op jit(solution)/shard_map/all_to_all | solution.py:487
  126.4 2.6 %spectral_gradient.1 = f32[648,36]{1,0:T(8,128)} custom-call(f32[80,128]{1,0:T(8,128)} %own_sums.1.sums.p0, f32[80,128]{1,0:T(8,128)} %copy-done.10, f32[80,128]{1,0:T(8,128)} %copy-done.9, f32[80,128]{1,0:T(8,128)} %copy-done.8, bf16[32,64,128]{2,1,0:T(8,128)(2,1)} %gradient_modes.1.after), custom_call_target="tpu_custom_call" | custom-call | tf_op jit(solution)/shard_map/spectral_gradient/pallas_call | solution.py:496
  129.0 8.8 %all-to-all-done.3.received = bf16[32,64,128]{2,1,0:T(8,128)(2,1)S(1)} async-done(((bf16[32,64,128]{2,1,0:T(8,128)(2,1)}), bf16[32,64,128]{2,1,0:T(8,128)(2,1)S(1)}, u32[]{:S(2)}, u32[]{:S(2)}) %all-to-all-start.3) | async-done | bytes 524320 | tf_op jit(solution)/shard_map/all_to_all | solution.py:487
  137.9 0.8 copy-done
  138.7 3.7 %field_gradient.1 = (bf16[2,288,1024]{2,1,0:T(8,128)(2,1)}, f32[36,36]{1,0:T(8,128)}, f32[3,3,36,36]{3,2,1,0:T(8,128)}, f32[3,3,36,36]{3,2,1,0:T(8,128)}) custom-call(bf16[32,64,128]{2,1,0:T(8,128)(2,1)} %copy-done, bf16[1024,256]{1,0:T(8,128)(2,1)} %get-tuple-element.37.high, bf16[1024,256]{1,0:T(8,128)(2,1)} %get-tuple-element.38.low, ...), custom_call_target="tpu_custom_call" | custom-call | tf_op jit(solution)/shard_map/field_gradient/pallas_call | solution.py:706
  (26 shorter events, 3.1 us)
Async XLA Ops:
  5.3 21.2 %all-to-all-start = ((bf16[32,32,128]{2,1,0:T(8,128)(2,1)}), bf16[32,32,128]{2,1,0:T(8,128)(2,1)S(1)}, u32[]{:S(2)}, u32[]{:S(2)}) async-start(bf16[32,32,128]{2,1,0:T(8,128)(2,1)} %bitcast.22), calls=%async_computation | async-start | bytes 524288 | tf_op jit(solution)/shard_map/all_to_all | solution.py:487
  22.1 18.9 %collective-permute-start = (bf16[2,2,48,1024]{3,2,1,0:T(8,128)(2,1)}, bf16[2,2,48,1024]{3,2,1,0:T(8,128)(2,1)S(1)}, u32[]{:S(2)}, u32[]{:S(2)}) collective-permute-start(bf16[2,2,48,1024]{3,2,1,0:T(8,128)(2,1)} %get-tuple-element.40), channel_id=1, source_target_pairs={{0,1},{1,2},{2,3},{3,4},{4,5},{5,6},{6,7},{7,8},{8,9},{9,10},{10,1... | collective-permute-start | bytes 1179656 | tf_op jit(solution)/shard_map/ppermute | solution.py:479
  25.2 15.8 %collective-permute-start.1 = (bf16[2,2,48,1024]{3,2,1,0:T(8,128)(2,1)}, bf16[2,2,48,1024]{3,2,1,0:T(8,128)(2,1)S(1)}, u32[]{:S(2)}, u32[]{:S(2)}) collective-permute-start(bf16[2,2,48,1024]{3,2,1,0:T(8,128)(2,1)} %get-tuple-element.41), channel_id=1, source_target_pairs={{1,0},{2,1},{3,2},{4,3},{5,4},{6,5},{7,6},{8,7},{9,8},{10,9},{11,1... | collective-permute-start | bytes 1179656 | tf_op jit(solution)/shard_map/ppermute | solution.py:483
  26.6 0.7 copy-start.5
  29.7 20.9 %all-to-all-start.1 = ((bf16[32,32,128]{2,1,0:T(8,128)(2,1)}), bf16[32,32,128]{2,1,0:T(8,128)(2,1)S(1)}, u32[]{:S(2)}, u32[]{:S(2)}) async-start(bf16[32,32,128]{2,1,0:T(8,128)(2,1)} %get-tuple-element.36.after), calls=%async_computation.1 | async-start | bytes 524288 | tf_op jit(solution)/shard_map/all_to_all | solution.py:487
  41.0 0.7 copy-start.1
  41.1 0.9 copy-start.2
  50.6 0.7 copy-start.4
  58.4 9.4 %collective-permute-start.2 = (bf16[2,2,48,1024]{3,2,1,0:T(8,128)(2,1)}, bf16[2,2,48,1024]{3,2,1,0:T(8,128)(2,1)S(1)}, u32[]{:S(2)}, u32[]{:S(2)}) collective-permute-start(bf16[2,2,48,1024]{3,2,1,0:T(8,128)(2,1)} %get-tuple-element.49), channel_id=1, source_target_pairs={{0,1},{1,2},{2,3},{3,4},{4,5},{5,6},{6,7},{7,8},{8,9},{9,10},{10,1... | collective-permute-start | bytes 1179656 | tf_op jit(solution)/shard_map/ppermute | solution.py:479
  61.5 10.1 %collective-permute-start.3 = (bf16[2,2,48,1024]{3,2,1,0:T(8,128)(2,1)}, bf16[2,2,48,1024]{3,2,1,0:T(8,128)(2,1)S(1)}, u32[]{:S(2)}, u32[]{:S(2)}) collective-permute-start(bf16[2,2,48,1024]{3,2,1,0:T(8,128)(2,1)} %get-tuple-element.50), channel_id=1, source_target_pairs={{1,0},{2,1},{3,2},{4,3},{5,4},{6,5},{7,6},{8,7},{9,8},{10,9},{11,1... | collective-permute-start | bytes 1179656 | tf_op jit(solution)/shard_map/ppermute | solution.py:483
  67.8 3.8 %copy-start.6 = (bf16[2,2,48,1024]{3,2,1,0:T(8,128)(2,1)}, bf16[2,2,48,1024]{3,2,1,0:T(8,128)(2,1)S(1)}, u32[]{:S(2)}) copy-start(bf16[2,2,48,1024]{3,2,1,0:T(8,128)(2,1)S(1)} %collective-permute-done.2.above) | copy-start | bytes 1179652
  71.6 0.8 copy-start.7
  81.5 23.3 %all-to-all-start.2 = ((bf16[32,48,128]{2,1,0:T(8,128)(2,1)}), bf16[32,48,128]{2,1,0:T(8,128)(2,1)S(1)}, u32[]{:S(2)}, u32[]{:S(2)}) async-start(bf16[32,48,128]{2,1,0:T(8,128)(2,1)} %get-tuple-element.55.after), calls=%async_computation.2 | async-start | bytes 786432 | tf_op jit(solution)/shard_map/all_to_all | solution.py:487
  104.8 0.7 copy-start.3
  107.2 8.3 %collective-permute-start.6 = (f32[80,128]{1,0:T(8,128)}, f32[80,128]{1,0:T(8,128)S(1)}, u32[]{:S(2)}, u32[]{:S(2)}) collective-permute-start(f32[80,128]{1,0:T(8,128)} %own_sums.1.sums.p0), channel_id=1, source_target_pairs={{0,96},{32,64},{64,32},{96,0},{1,97},{33,65},{65,33},{97,1},{2,98}... | collective-permute-start | bytes 122888 | tf_op jit(solution)/shard_map/ppermute | solution.py:688
  112.4 3.7 %collective-permute-start.5 = (f32[80,128]{1,0:T(8,128)}, f32[80,128]{1,0:T(8,128)S(1)}, u32[]{:S(2)}, u32[]{:S(2)}) collective-permute-start(f32[80,128]{1,0:T(8,128)} %own_sums.1.sums.p0), channel_id=1, source_target_pairs={{0,64},{32,96},{64,0},{96,32},{1,65},{33,97},{65,1},{97,33},{2,66}... | collective-permute-start | bytes 122888 | tf_op jit(solution)/shard_map/ppermute | solution.py:688
  113.5 2.7 %collective-permute-start.4 = (f32[80,128]{1,0:T(8,128)}, f32[80,128]{1,0:T(8,128)S(1)}, u32[]{:S(2)}, u32[]{:S(2)}) collective-permute-start(f32[80,128]{1,0:T(8,128)} %own_sums.1.sums.p0), channel_id=1, source_target_pairs={{0,32},{32,0},{64,96},{96,64},{1,33},{33,1},{65,97},{97,65},{2,34}... | collective-permute-start | bytes 122888 | tf_op jit(solution)/shard_map/ppermute | solution.py:688
  115.5 0.7 copy-start.8
  116.1 0.6 copy-start.9
  116.7 0.6 copy-start.10
  119.1 18.8 %all-to-all-start.3 = ((bf16[32,64,128]{2,1,0:T(8,128)(2,1)}), bf16[32,64,128]{2,1,0:T(8,128)(2,1)S(1)}, u32[]{:S(2)}, u32[]{:S(2)}) async-start(bf16[32,64,128]{2,1,0:T(8,128)(2,1)} %gradient_modes.1.after), calls=%async_computation.3 | async-start | bytes 1048576 | tf_op jit(solution)/shard_map/all_to_all | solution.py:487
  137.9 0.8 copy-start

commit v4 on v3

--- a/solution.py
+++ b/solution.py
@@ -112,11 +112,25 @@
 
 def row_transform(cols, high, low):
     c_high, c_low = split(cols)
-    return (dot_nt(high, c_high) + dot_nt(high, c_low) + dot_nt(low, c_high)).astype(BF)
+    both = dot_nt(high, jnp.concatenate([c_high, c_low], axis=0))
+    return (both[:, 0:128] + both[:, 128:256] + dot_nt(low, c_high)).astype(BF)
 
 
 def row_expand(modes, high, low):
-    return dot_tn(modes, high) + dot_tn(modes, low)
+    both = dot_tn(modes, jnp.concatenate([high, low], axis=1))
+    return both[:, 0:256] + both[:, 256:512]
+
+
+def strip_pair(even, top, bottom):
+    top, bottom = [jnp.concatenate([x[0:CO].astype(F32) for x in rows], axis=0) for rows in (top, bottom)]
+    return jnp.where(even, bottom, top).astype(BF), jnp.where(even, top, bottom).astype(BF)
+
+
+def halo_rows(even, first, second):
+    first, second = first[0].astype(F32), second[0].astype(F32)
+    above, below = jnp.where(even, second, first), jnp.where(even, first, second)
+    rest = jnp.zeros((CP - CO, NC), F32)
+    return [jnp.concatenate([x[i * CO : (i + 1) * CO], rest], axis=0) for x in (above, below) for i in range(2)]
 
 
 def place_rows(rows, left):
@@ -179,7 +193,9 @@
         target[...] = wide[:, 0 : 4 * CP].astype(BF)
 
 
-def kernel_rows(field, cot, one, two, point, after, rows, top, bottom, cot_rows, w_one, w_two, w_two_back, w_one_back, w_point, w_point_back, wide, base, spread):
+def kernel_rows(place, field, cot, one, two, point, after, rows, strip_one, strip_two, cot_rows, w_one, w_two, w_two_back, w_one_back, w_point, w_point_back, wide, base, spread):
+    even = place[0] % 2 == 0
+
     @pl.when(pl.program_id(0) == 0)
     def _():
         prepare(one, two, point, w_one, w_two, w_two_back, w_one_back, w_point, w_point_back, base, spread)
@@ -188,25 +204,24 @@
         for n in range(0, NC, 128):
             wide[k, n // 128, 0 : C * RL, :] = source[0, :, n : n + 128].astype(F32)
             wide[k, n // 128, C * RL :, :] = jnp.zeros((12 * RL, 128), F32)
-        for r in range(RL):
-            for n in range(0, NC, 128):
-                x = wide[k, n // 128, pl.ds(r, CP, stride=RL), :].astype(BF)
-                target[0, r, :, n : n + 128] = x
-                if k == 0 and r < 2:
-                    top[0, r, :, n : n + 128] = x
-                if k == 0 and r >= RL - 2:
-                    bottom[0, r - RL + 2, :, n : n + 128] = x
+        for n in range(0, NC, 128):
+            found = [wide[k, n // 128, pl.ds(r, CP, stride=RL), :] for r in range(RL)]
+            for r in range(RL):
+                target[0, r, :, n : n + 128] = found[r].astype(BF)
+            if k == 0:
+                x, y = strip_pair(even, found[0:2], found[RL - 2 :])
+                strip_one[0, :, n : n + 128], strip_two[0, :, n : n + 128] = x, y
 
 
 def window(ref, i, count):
     return ref[i : i + count].reshape(count * GR, NC)
 
 
-def kernel_b(place, rows, above, below, w_one, w_two, w_point, after, middle, slope, pre, taps, mid_taps):
+def kernel_b(place, rows, first, second, w_one, w_two, w_point, after, middle, slope, pre, taps, mid_taps):
     index = place[0]
-    source = [above.at[0, 0], above.at[0, 1]] + [rows.at[0, r] for r in range(RL)] + [below.at[0, 0], below.at[0, 1]]
-    for i, x in enumerate(source):
-        store_taps(taps, i, x[...].astype(F32))
+    halo = halo_rows(index % 2 == 0, first, second)
+    for i, x in enumerate(halo[0:2] + [rows[0, r].astype(F32) for r in range(RL)] + halo[2:4]):
+        store_taps(taps, i, x)
     rest = jnp.zeros((CP - CO, NC), F32)
     for start, count in ((0, 4), (4, 3), (7, 3)):
         d = dot(w_one[0 : CP * count, 0 : GR * (count + 2)], window(taps, start, count + 2))
@@ -216,7 +231,7 @@
             if i in (0, RL + 1):
                 keep = jnp.where(index == (0 if i == 0 else SP - 1), 0.0, 1.0).astype(F32)
                 value, gradient = value * keep, gradient * keep
-            slope[0, i] = gradient
+            slope[0, i] = jnp.concatenate([gradient, rest], axis=0).astype(BF)
             value = jnp.concatenate([value, rest], axis=0)
             middle[0, i] = value.astype(BF)
             store_taps(mid_taps, i, value)
@@ -301,7 +316,7 @@
     grad[...] = lines[:, 0:C]
 
 
-def kernel_d(received, high, low, inverse, pre, cot, table, scale, values, slopes, top, bottom, message, left, spec, kept, cols):
+def kernel_d(place, received, high, low, inverse, pre, cot, table, scale, values, slopes, strip_one, strip_two, message, left, spec, kept, cols):
     lev = pl.program_id(0)
 
     @pl.when(lev == 0)
@@ -311,16 +326,15 @@
         cols[...] = jnp.zeros_like(cols)
 
     rest = jnp.zeros((CP - CO, NC), F32)
+    edges = {}
     for r in range(RL):
         value, gradient = gelu_parts(pre[0, r] + spec[lev * RL + r])
         values[0, r] = jnp.concatenate([value, rest], axis=0).astype(BF)
         s = jnp.concatenate([gradient, rest], axis=0) * cot[0, r].astype(F32)
-        s = s.astype(BF)
-        slopes[0, r] = s
-        if r < 2:
-            top[0, r] = s
-        if r >= RL - 2:
-            bottom[0, r - RL + 2] = s
+        slopes[0, r] = s.astype(BF)
+        edges[r] = s
+    x, y = strip_pair(place[0] % 2 == 0, [edges[0], edges[1]], [edges[RL - 2], edges[RL - 1]])
+    strip_one[0], strip_two[0] = x, y
     kept[lev] = dot(slopes[0].reshape(RL * CP, NC), table[...])
 
     @pl.when(lev == LEV - 1)
@@ -376,24 +390,26 @@
         grad_two[...] += part
 
 
-def kernel_e(place, slopes, above, below, rows, f_above, f_below, slope, w_two, modes, grad_two, pre_slope, message, taps, pre_taps, grad_one, sums):
+def kernel_e(place, slopes, first, second, rows, f_first, f_second, slope, w_two, modes, grad_two, pre_slope, message, taps, pre_taps, grad_one, sums):
     index = place[0]
     lev = pl.program_id(0)
-    source = [above.at[0, 0], above.at[0, 1]] + [slopes.at[0, r] for r in range(RL)] + [below.at[0, 0], below.at[0, 1]]
-    for i, x in enumerate(source):
-        store_taps(taps, i, x[...].astype(F32))
+    even = index % 2 == 0
+    halo = halo_rows(even, first, second)
+    for i, x in enumerate(halo[0:2] + [slopes[0, r].astype(F32) for r in range(RL)] + halo[2:4]):
+        store_taps(taps, i, x)
     rest = jnp.zeros((CP - CO, NC), F32)
     for start, count in ((0, 4), (4, 3), (7, 3)):
         d = dot(w_two[0 : CP * count, 0 : GR * (count + 2)], window(taps, start, count + 2))
         for t in range(count):
             i = start + t
-            value = d[t * CP : t * CP + CO] * slope[0, i]
+            value = d[t * CP : t * CP + CO] * slope[0, i].astype(F32)[0:CO]
             if i in (0, RL + 1):
                 value = value * jnp.where(index == (0 if i == 0 else SP - 1), 0.0, 1.0).astype(F32)
             value = jnp.concatenate([value, rest], axis=0)
             pre_slope[0, i] = value.astype(BF)
             store_taps(pre_taps, i, value)
-    field = [f_above[0, 1]] + [rows[0, r] for r in range(RL)] + [f_below[0, 0]]
+    halo = halo_rows(even, f_first, f_second)
+    field = [halo[1].astype(BF)] + [rows[0, r] for r in range(RL)] + [halo[2].astype(BF)]
     left = jnp.concatenate([jnp.concatenate(field[r : r + 3], axis=0) for r in range(RL)], axis=1)
     right = jnp.concatenate([pre_taps[r + 1] for r in range(RL)], axis=1)
     part_one = dot_nt(left, right)
@@ -458,7 +474,7 @@
 
 
 def params(mib):
-    return pltpu.CompilerParams(vmem_limit_bytes=56 * 1024 * 1024)
+    return pltpu.CompilerParams(vmem_limit_bytes=mib * 1024 * 1024)
 
 
 def estimate(us):
@@ -475,12 +491,10 @@
     return pl.BlockSpec(dims, lambda lev: (0,) * len(dims))
 
 
-def from_above(x):
-    return lax.ppermute(x, "sp", [(i, i + 1) for i in range(SP - 1)])
-
-
-def from_below(x):
-    return lax.ppermute(x, "sp", [(i + 1, i) for i in range(SP - 1)])
+def partners(first, second):
+    pairs = [(i, i ^ 1) for i in range(SP)]
+    others = [(i, i + 1) for i in range(1, SP - 1, 2)] + [(i + 1, i) for i in range(1, SP - 1, 2)]
+    return lax.ppermute(first, "sp", pairs), lax.ppermute(second, "sp", others)
 
 
 def exchange(x):
@@ -510,7 +524,7 @@
     inputs = field.reshape(LEV * C * RL, NC)
     table = jnp.asarray(TABLE)
     weight = jnp.transpose(spec_weight, (1, 3, 0, 2)).reshape(C * QN * 2, C)
-    strip = shape((LEV, 2, CP, NC), BF)
+    strip = shape((LEV, 2 * CO, NC), BF)
     grid_rows = shape((LEV, RL, CP, NC), BF)
     natural = shape((LEV, C * RL, NC), BF)
     flat, cols = pltpu.VMEM((LEV * C * RL, 128), F32), pltpu.VMEM((128, 256), F32)
@@ -521,17 +535,18 @@
         (),
         [shape((SP * 32, 128), BF), row_matrix, row_matrix],
         [flat, cols],
-        10,
+        56,
         "field_modes",
         (place,),
     )
     arrived = exchange(message.reshape(SP, 32, 128))
     toeplitz, blocks = shape((4 * CP, 6 * GR), BF), shape((4 * CP, 4 * CP), BF)
     weights_out = [toeplitz] * 4 + [blocks] * 2
-    rows, top, bottom, cot_rows, w_one, w_two, w_two_back, w_one_back, w_point, w_point_back = pl.pallas_call(
+    rows, f_first, f_second, cot_rows, w_one, w_two, w_two_back, w_one_back, w_point, w_point_back = pl.pallas_call(
         kernel_rows,
         grid=(LEV,),
         in_specs=[
+            pl.BlockSpec(memory_space=pltpu.SMEM),
             level_spec(C * RL, NC),
             level_spec(C * RL, NC),
             whole_spec(3, 3, C, C),
@@ -539,7 +554,7 @@
             whole_spec(C, C),
             anywhere(),
         ],
-        out_specs=[level_spec(RL, CP, NC), level_spec(2, CP, NC), level_spec(2, CP, NC), level_spec(RL, CP, NC)]
+        out_specs=[level_spec(RL, CP, NC), level_spec(2 * CO, NC), level_spec(2 * CO, NC), level_spec(RL, CP, NC)]
         + [whole_spec(*x.shape) for x in weights_out],
         out_shape=[grid_rows, strip, strip, grid_rows] + weights_out,
         scratch_shapes=[
@@ -547,10 +562,10 @@
             pltpu.VMEM((CP, 9 * CP), F32),
             pltpu.VMEM((4 * CP, 6 * GR), F32),
         ],
-        compiler_params=params(12),
+        compiler_params=params(56),
         name="row_layout",
-    )(field.reshape(natural.shape), cotangent.reshape(natural.shape), kernel_one, kernel_two, point_weight, message)
-    f_above, f_below = from_above(bottom), from_below(top)
+    )(place, field.reshape(natural.shape), cotangent.reshape(natural.shape), kernel_one, kernel_two, point_weight, message)
+    f_first, f_second = partners(f_first, f_second)
 
     square, lines = pltpu.VMEM((128, 128), F32), pltpu.VMEM((C * QN * 2, 128), F32)
     mixed, kept = plain_call(
@@ -559,7 +574,7 @@
         (),
         [shape((SP, 32, 128), BF), shape((32, 128), F32)],
         [square, square, square, lines],
-        6,
+        8,
         "mode_mix",
     )
     gathered = exchange(mixed).reshape(SP * 32, 128)
@@ -570,8 +585,8 @@
         in_specs=[
             pl.BlockSpec(memory_space=pltpu.SMEM),
             level_spec(RL, CP, NC),
-            level_spec(2, CP, NC),
-            level_spec(2, CP, NC),
+            level_spec(2 * CO, NC),
+            level_spec(2 * CO, NC),
             whole_spec(4 * CP, 6 * GR),
             whole_spec(4 * CP, 6 * GR),
             whole_spec(4 * CP, 4 * CP),
@@ -579,24 +594,25 @@
         ],
         out_specs=[
             level_spec(RL + 2, CP, NC),
-            level_spec(RL + 2, CO, NC),
+            level_spec(RL + 2, CP, NC),
             level_spec(RL, CO, NC),
         ],
         out_shape=[
             shape((LEV, RL + 2, CP, NC), BF),
-            shape((LEV, RL + 2, CO, NC), F32),
+            shape((LEV, RL + 2, CP, NC), BF),
             shape((LEV, RL, CO, NC), F32),
         ],
         scratch_shapes=[pltpu.VMEM((RL + 4, GR, NC), BF), pltpu.VMEM((RL + 2, GR, NC), BF)],
-        compiler_params=params(28),
+        compiler_params=params(56),
         name="two_convolutions",
-    )(place, rows, f_above, f_below, w_one, w_two, w_point, mixed)
+    )(place, rows, f_first, f_second, w_one, w_two, w_point, mixed)
 
     left, spec = pltpu.VMEM((LEV * RL * CO, 128), F32), pltpu.VMEM((LEV * RL * CO, NC), F32)
-    values, slopes, s_top, s_bottom, message = pl.pallas_call(
+    values, slopes, s_first, s_second, message = pl.pallas_call(
         kernel_d,
         grid=(LEV,),
         in_specs=[
+            pl.BlockSpec(memory_space=pltpu.SMEM),
             whole_spec(SP * 32, 128),
             whole_spec(SP * 32, 256),
             whole_spec(SP * 32, 256),
@@ -606,7 +622,7 @@
             whole_spec(NC, 128),
             whole_spec(1, 256),
         ],
-        out_specs=[level_spec(RL, CP, NC)] * 2 + [level_spec(2, CP, NC)] * 2 + [whole_spec(SP * 32, 128)],
+        out_specs=[level_spec(RL, CP, NC)] * 2 + [level_spec(2 * CO, NC)] * 2 + [whole_spec(SP * 32, 128)],
         out_shape=[grid_rows, grid_rows, strip, strip, shape((SP * 32, 128), BF)],
         scratch_shapes=[
             left,
@@ -614,10 +630,10 @@
             pltpu.VMEM((LEV, RL * CP, 128), F32),
             cols,
         ],
-        compiler_params=params(22),
+        compiler_params=params(56),
         name="output_and_slope",
-    )(gathered, high, low, jnp.asarray(INVERSE), pre, cot_rows, table, jnp.asarray(SCALE))
-    s_above, s_below = from_above(s_bottom), from_below(s_top)
+    )(place, gathered, high, low, jnp.asarray(INVERSE), pre, cot_rows, table, jnp.asarray(SCALE))
+    s_first, s_second = partners(s_first, s_second)
 
     grad_two = pl.pallas_call(
         kernel_e_zero,
@@ -626,7 +642,7 @@
         scratch_shapes=[pltpu.VMEM((RL, GR, NC), BF)],
         out_specs=whole_spec(GR + CP, GR),
         out_shape=shape((GR + CP, GR), F32),
-        compiler_params=params(22),
+        compiler_params=params(56),
         name="weight_gradients_two",
     )(slopes, middle, rows)
     pre_slope, message = pl.pallas_call(
@@ -635,12 +651,12 @@
         in_specs=[
             pl.BlockSpec(memory_space=pltpu.SMEM),
             level_spec(RL, CP, NC),
-            level_spec(2, CP, NC),
-            level_spec(2, CP, NC),
+            level_spec(2 * CO, NC),
+            level_spec(2 * CO, NC),
             level_spec(RL, CP, NC),
-            level_spec(2, CP, NC),
-            level_spec(2, CP, NC),
-            level_spec(RL + 2, CO, NC),
+            level_spec(2 * CO, NC),
+            level_spec(2 * CO, NC),
+            level_spec(RL + 2, CP, NC),
             whole_spec(4 * CP, 6 * GR),
             whole_spec(SP, 32, 128),
             whole_spec(GR + CP, GR),
@@ -653,9 +669,9 @@
             pltpu.VMEM((GR, GR), F32),
             pltpu.VMEM((SP * 16, 128), F32),
         ],
-        compiler_params=params(28),
+        compiler_params=params(56),
         name="slope_and_weight_gradients",
-    )(place, slopes, s_above, s_below, rows, f_above, f_below, slope, w_two_back, message.reshape(SP, 32, 128), grad_two)
+    )(place, slopes, s_first, s_second, rows, f_first, f_second, slope, w_two_back, message.reshape(SP, 32, 128), grad_two)
     arrived = exchange(message)
     back = pl.pallas_call(
         kernel_e_two,
@@ -670,7 +686,7 @@
         out_specs=level_spec(C * RL, NC),
         out_shape=shape(natural.shape, F32),
         scratch_shapes=[pltpu.VMEM((RL + 2, GR, NC), BF), pltpu.VMEM((NC // 128, C * RL, 128), F32)],
-        compiler_params=params(22),
+        compiler_params=params(56),
         name="backward_convolution",
     )(pre_slope, slopes, w_one_back, w_point_back, message)
     (out,) = plain_call(
@@ -679,18 +695,18 @@
         (message,),
         [natural],
         [pltpu.VMEM((NC // 128, LEV * C * RL, 128), F32)],
-        10,
+        56,
         "output_layout",
     )
     (sums,) = plain_call(
-        kernel_own, (arrived, kept), (back, out), [shape((80, 128), F32)], [], 4, "own_sums"
+        kernel_own, (arrived, kept), (back, out), [shape((80, 128), F32)], [], 56, "own_sums"
     )
     others = [lax.ppermute(sums, "rep", [(i, i ^ k) for i in range(4)]) for k in (1, 2, 3)]
     (cofield,) = plain_call(
-        kernel_mix_back, (sums, weight), (), [shape((32, 128), BF)], [square, lines], 6, "mode_mix_back"
+        kernel_mix_back, (sums, weight), (), [shape((32, 128), BF)], [square, lines], 56, "mode_mix_back"
     )
     (message,) = plain_call(
-        kernel_send_back, (cofield, sums, *others), (), [shape((SP, 64, 128), BF)], [], 4, "gradient_modes"
+        kernel_send_back, (cofield, sums, *others), (), [shape((SP, 64, 128), BF)], [], 56, "gradient_modes"
     )
     gathered = exchange(message)
     (spec_grad,) = plain_call(
@@ -699,7 +715,7 @@
         (message,),
         [shape(weight.shape, F32)],
         [pltpu.VMEM((4, 128, 128), F32)] * 2 + [lines],
-        8,
+        56,
         "spectral_gradient",
     )
     kernel_out_shape = shape((3, 3, C, C), F32)
@@ -716,7 +732,7 @@
         out_specs=[level_spec(C * RL, NC), whole_spec(C, C), whole_spec(3, 3, C, C), whole_spec(3, 3, C, C)],
         out_shape=[natural, shape((C, C), F32), kernel_out_shape, kernel_out_shape],
         scratch_shapes=[pltpu.VMEM((LEV, C * RL, 128), F32)],
-        compiler_params=params(18),
+        compiler_params=params(56),
         name="field_gradient",
     )(gathered, high, low, jnp.asarray(BACK), back)
     spec_total = jnp.transpose(spec_grad.reshape(C, QN, 2, C), (2, 0, 3, 1))

time: 144 us -> 136 us (0.944)
  starting transfers between devices: 58.3 us -> 53.7 us
  Pallas kernels: 62.6 us -> 60.3 us
  waiting for transfers between devices: 14.9 us -> 13.3 us
    ppermute x4, starting transfers between devices: 9.01 us -> 3.89 us  [the longest x2 2.37 us: partners(): lax.ppermute(first, 'sp', pairs)]
    ppermute x4, waiting for transfers between devices: 4.06 us -> 0.01 us  [the longest x2 0.01 us: partners(): lax.ppermute(second, 'sp', others)]
    all_to_all x4, waiting for transfers between devices: 10.1 us -> 12.6 us  [exchange(): return lax.all_to_all(x, 'sp', 0, 0, tiled=True)]
    pallas_call x7, Pallas kernels: 18.6 us -> 16.7 us  [plain_call(): pl.pallas_call(kernel, in_specs=[pl.BlockSpec(memory_space=pltpu.SMEM)] *...]
    unnamed x22 -> x24, local copies, waits for them, and re-layouts: 5.78 us -> 5.72 us
  transfers between devices with their start and end apart: 11 -> 11, of which waited for: 6 -> 5; matrix products, arithmetic and copies ran while one was open for 0% -> 0% of each run, Pallas kernels for 24% -> 25%
where the time goes in v4:
time: 136 us; the launch traced here: 134 us
  Pallas kernels  60.3 us (44%)
  starting transfers between devices  53.7 us (39%)
  waiting for transfers between devices  13.3 us (10%)
  local copies, waits for them, and re-layouts  5.72 us (4%)
    all_to_all x4, starting transfers between devices, exchange(): return lax.all_to_all(x, 'sp', 0, 0, tiled=True)  43.6 us
    pallas_call x7, Pallas kernels, plain_call(): pl.pallas_call(kernel, in_specs=[pl.BlockSpec(memory_space=pltpu.SMEM)] *...  16.7 us
    all_to_all x4, waiting for transfers between devices, exchange(): return lax.all_to_all(x, 'sp', 0, 0, tiled=True)  12.6 us
    pallas_call x1, Pallas kernels, local(): pl.pallas_call(kernel_e, grid=(LEV,), in_specs=[pl.BlockSpec(memory_space...  9 us
    pallas_call x1, Pallas kernels, local(): pl.pallas_call(kernel_b, grid=(LEV,), in_specs=[pl.BlockSpec(memory_space...  8.48 us
    pallas_call x1, Pallas kernels, local(): pl.pallas_call(kernel_d, grid=(LEV,), in_specs=[pl.BlockSpec(memory_space...  6.96 us
    ppermute x3, starting transfers between devices, local(): lax.ppermute(sums, 'rep', [(i, i ^ k) for i in range(4)])  6.27 us
    unnamed x24, local copies, waits for them, and re-layouts  5.72 us
  transfers between devices with their start and end apart: 11, of which 5 were waited for; matrix products, arithmetic and copies ran while one was open for 0% of the time, Pallas kernels for 25%

profile of v4, /device:TPU:1, one launch (start us, length us, event | category | flops | bytes accessed | tf_op | source)
XLA Modules:
  0.0 133.8 jit_solution(12805357990153871662)
XLA Ops:
  0.6 3.8 %field_modes.1 = (bf16[1024,128]{1,0:T(8,128)(2,1)}, bf16[1024,256]{1,0:T(8,128)(2,1)}, bf16[1024,256]{1,0:T(8,128)(2,1)}) custom-call(s32[1]{0:T(128)} %bitcast.place, bf16[576,1024]{1,0:T(8,128)(2,1)} %bitcast.17, bf16[1024,128]{1,0:T(8,128)(2,1)} %constant.18.clone.table, bf16[1024,256]{1,0:T(8,128)(2,1)} %constant.19.clone.high, ...), custom_call_target="tpu_custom_call" | custom-call | tf_op jit(solution)/shard_map/field_modes/pallas_call | solution.py:510
  4.5 11.5 %all-to-all-start = ((bf16[32,32,128]{2,1,0:T(8,128)(2,1)}), bf16[32,32,128]{2,1,0:T(8,128)(2,1)S(1)}, u32[]{:S(2)}, u32[]{:S(2)}) async-start(bf16[32,32,128]{2,1,0:T(8,128)(2,1)} %bitcast.21), calls=%async_computation | async-start | bytes 524288 | tf_op jit(solution)/shard_map/all_to_all | solution.py:501
  16.0 5.4 %row_layout.1 = (bf16[2,8,48,1024]{3,2,1,0:T(8,128)(2,1)}, bf16[2,80,1024]{2,1,0:T(8,128)(2,1)}, bf16[2,80,1024]{2,1,0:T(8,128)(2,1)}, bf16[2,8,48,1024]{3,2,1,0...) custom-call(s32[1]{0:T(128)} %bitcast.place, ...), custom_call_target="tpu_custom_call" | custom-call | tf_op jit(solution)/shard_map/row_layout/pallas_call | solution.py:545
  21.3 1.3 collective-permute-start
  22.6 0.7 collective-permute-start.1
  23.3 2.3 %all-to-all-done.received = bf16[32,32,128]{2,1,0:T(8,128)(2,1)S(1)} async-done(((bf16[32,32,128]{2,1,0:T(8,128)(2,1)}), bf16[32,32,128]{2,1,0:T(8,128)(2,1)S(1)}, u32[]{:S(2)}, u32[]{:S(2)}) %all-to-all-start) | async-done | bytes 262176 | tf_op jit(solution)/shard_map/all_to_all | solution.py:501
  25.6 1.4 %mode_mix.1 = (bf16[32,32,128]{2,1,0:T(8,128)(2,1)}, f32[32,128]{1,0:T(8,128)S(1)}) custom-call(bf16[32,32,128]{2,1,0:T(8,128)(2,1)S(1)} %all-to-all-done.received, f32[648,36]{1,0:T(8,128)S(1)} %bitcast.16), custom_call_target="tpu_custom_call" | custom-call | tf_op jit(solution)/shard_map/mode_mix/pallas_call | solution.py:510
  27.6 8.8 %all-to-all-start.1 = ((bf16[32,32,128]{2,1,0:T(8,128)(2,1)}), bf16[32,32,128]{2,1,0:T(8,128)(2,1)S(1)}, u32[]{:S(2)}, u32[]{:S(2)}) async-start(bf16[32,32,128]{2,1,0:T(8,128)(2,1)} %get-tuple-element.36.after), calls=%async_computation.1 | async-start | bytes 524288 | tf_op jit(solution)/shard_map/all_to_all | solution.py:501
  36.5 0.7 copy-done.4
  37.3 8.5 %two_convolutions.1 = (bf16[2,10,48,1024]{3,2,1,0:T(8,128)(2,1)}, bf16[2,10,48,1024]{3,2,1,0:T(8,128)(2,1)}, f32[2,8,40,1024]{3,2,1,0:T(8,128)}) custom-call(s32[1]{0:T(128)} %bitcast.place, bf16[2,8,48,1024]{3,2,1,0:T(8,128)(2,1)} %get-tuple-element.39.rows, bf16[2,80,1024]{2,1,0:T(8,128)(2,1)} %copy-done.4, bf16[2,80,1024]{2,1,0:T(8,128)(2,1)} %copy-done.5, ...), custom_call_target="tpu_custom_call" | custom-call | tf_op jit(solution)/shard_map/two_convolutions/pallas_call | solution.py:582
  46.0 0.7 copy-done.6
  46.7 7.0 %output_and_slope.1 = (bf16[2,8,48,1024]{3,2,1,0:T(8,128)(2,1)}, bf16[2,8,48,1024]{3,2,1,0:T(8,128)(2,1)}, bf16[2,80,1024]{2,1,0:T(8,128)(2,1)}, bf16[2,80,1024]{2,1,0:T(8,128)(2,1)}, bf16[1024,128]{1,0:T(8,128)(2,1)}) custom-call(s32[1]{0:T(128)} %bitcast.place, bf16[1024,128]{1,0:T(8,128)(2,1)} %bitcast.22, bf16[1024,256]{1,0:T(8,128)(2,1)} %get-tuple-element.37.high, ...), custom_call_target="tpu_custom_call" | custom-call | tf_op jit(solution)/shard_map/output_and_slope/pallas_call | solution.py:611
  53.7 1.1 collective-permute-start.2
  54.7 0.8 collective-permute-start.3
  55.6 4.5 %weight_gradients_two.1.grad_two = f32[192,144]{1,0:T(8,128)} custom-call(bf16[2,8,48,1024]{3,2,1,0:T(8,128)(2,1)} %get-tuple-element.48.slopes, bf16[2,10,48,1024]{3,2,1,0:T(8,128)(2,1)} %get-tuple-element.54.middle, bf16[2,8,48,1024]{3,2,1,0:T(8,128)(2,1)} %get-tuple-element.39.rows), custom_call_target="tpu_custom_call" | custom-call | tf_op jit(solution)/shard_map/weight_gradients_two/pallas_call | solution.py:638
  60.2 0.7 copy-done.7
  61.0 9.0 %slope_and_weight_gradients.1 = (bf16[2,10,48,1024]{3,2,1,0:T(8,128)(2,1)}, bf16[32,48,128]{2,1,0:T(8,128)(2,1)}) custom-call(s32[1]{0:T(128)} %bitcast.place, bf16[2,8,48,1024]{3,2,1,0:T(8,128)(2,1)} %get-tuple-element.48.slopes, bf16[2,80,1024]{2,1,0:T(8,128)(2,1)} %copy-done.7, bf16[2,80,1024]{2,1,0:T(8,128)(2,1)} %copy-done.8, ...), custom_call_target="tpu_custom_call" | custom-call | tf_op jit(solution)/shard_map/slope_and_weight_gradients/pallas_call | solution.py:648
  70.0 16.0 %all-to-all-start.2 = ((bf16[32,48,128]{2,1,0:T(8,128)(2,1)}), bf16[32,48,128]{2,1,0:T(8,128)(2,1)S(1)}, u32[]{:S(2)}, u32[]{:S(2)}) async-start(bf16[32,48,128]{2,1,0:T(8,128)(2,1)} %get-tuple-element.55.after), calls=%async_computation.2 | async-start | bytes 786432 | tf_op jit(solution)/shard_map/all_to_all | solution.py:501
  86.0 3.4 %output_layout.1.second = bf16[2,288,1024]{2,1,0:T(8,128)(2,1)} custom-call(bf16[2,8,48,1024]{3,2,1,0:T(8,128)(2,1)} %get-tuple-element.47.values, bf16[32,48,128]{2,1,0:T(8,128)(2,1)} %get-tuple-element.55.after), custom_call_target="tpu_custom_call" | custom-call | tf_op jit(solution)/shard_map/output_layout/pallas_call | solution.py:510
  89.3 5.6 %backward_convolution.1.first.back = f32[2,288,1024]{2,1,0:T(8,128)} custom-call(bf16[2,10,48,1024]{3,2,1,0:T(8,128)(2,1)} %get-tuple-element.57.pre_slope, bf16[2,8,48,1024]{3,2,1,0:T(8,128)(2,1)} %get-tuple-element.48.slopes, bf16[192,864]{1,0:T(8,128)(2,1)} %get-tuple-element.58.w_one, bf16[192,192]{1,0:T(8,128)(2,1)} %get-tuple-element.59.w_point, ...), custom_call_target="tpu_custom_call" | custom-call | tf_op jit(solution)/shard_map/backward_convolution/pallas_call | solution.py:676
  94.9 1.2 all-to-all-done.2.received
  96.2 0.7 copy-done.3
  96.9 1.7 %own_sums.1.sums.p0 = f32[80,128]{1,0:T(8,128)} custom-call(bf16[32,48,128]{2,1,0:T(8,128)(2,1)} %copy-done.3, f32[32,128]{1,0:T(8,128)} %copy-done.1, f32[2,288,1024]{2,1,0:T(8,128)} %backward_convolution.1.first.back, bf16[2,288,1024]{2,1,0:T(8,128)(2,1)} %output_layout.1.second), custom_call_target="tpu_custom_call" | custom-call | tf_op jit(solution)/shard_map/own_sums/pallas_call | solution.py:510
  98.6 5.2 %collective-permute-start.6 = (f32[80,128]{1,0:T(8,128)}, f32[80,128]{1,0:T(8,128)S(1)}, u32[]{:S(2)}, u32[]{:S(2)}) collective-permute-start(f32[80,128]{1,0:T(8,128)} %own_sums.1.sums.p0), channel_id=1, source_target_pairs={{0,96},{32,64},{64,32},{96,0},{1,97},{33,65},{65,33},{97,1},{2,98}... | collective-permute-start | bytes 122888 | tf_op jit(solution)/shard_map/ppermute | solution.py:704
  103.8 1.1 collective-permute-start.5
  104.9 2.0 %mode_mix_back.1.cofield = bf16[32,128]{1,0:T(8,128)(2,1)} custom-call(f32[80,128]{1,0:T(8,128)} %own_sums.1.sums.p0, f32[648,36]{1,0:T(8,128)} %bitcast.15), custom_call_target="tpu_custom_call" | custom-call | tf_op jit(solution)/shard_map/mode_mix_back/pallas_call | solution.py:510
  108.7 1.7 %gradient_modes.1.after = bf16[32,64,128]{2,1,0:T(8,128)(2,1)} custom-call(bf16[32,128]{1,0:T(8,128)(2,1)} %mode_mix_back.1.cofield, f32[80,128]{1,0:T(8,128)} %own_sums.1.sums.p0, f32[80,128]{1,0:T(8,128)} %copy-done.11, f32[80,128]{1,0:T(8,128)} %copy-done.10, f32[80,128]{1,0:T(8,128)} %copy-done.9), custom_call_target="tpu_custom_call" | custom-call | tf_op jit(solution)/shard_map/gradient_modes/pallas_call | solution.py:510
  110.5 7.3 %all-to-all-start.3 = ((bf16[32,64,128]{2,1,0:T(8,128)(2,1)}), bf16[32,64,128]{2,1,0:T(8,128)(2,1)S(1)}, u32[]{:S(2)}, u32[]{:S(2)}) async-start(bf16[32,64,128]{2,1,0:T(8,128)(2,1)} %gradient_modes.1.after), calls=%async_computation.3 | async-start | bytes 1048576 | tf_op jit(solution)/shard_map/all_to_all | solution.py:501
  117.8 2.6 %spectral_gradient.1 = f32[648,36]{1,0:T(8,128)} custom-call(f32[80,128]{1,0:T(8,128)} %own_sums.1.sums.p0, f32[80,128]{1,0:T(8,128)} %copy-done.11, f32[80,128]{1,0:T(8,128)} %copy-done.10, f32[80,128]{1,0:T(8,128)} %copy-done.9, bf16[32,64,128]{2,1,0:T(8,128)(2,1)} %gradient_modes.1.after), custom_call_target="tpu_custom_call" | custom-call | tf_op jit(solution)/shard_map/spectral_gradient/pallas_call | solution.py:510
  120.4 8.8 %all-to-all-done.3.received = bf16[32,64,128]{2,1,0:T(8,128)(2,1)S(1)} async-done(((bf16[32,64,128]{2,1,0:T(8,128)(2,1)}), bf16[32,64,128]{2,1,0:T(8,128)(2,1)S(1)}, u32[]{:S(2)}, u32[]{:S(2)}) %all-to-all-start.3) | async-done | bytes 524320 | tf_op jit(solution)/shard_map/all_to_all | solution.py:501
  129.3 0.8 copy-done.2
  130.1 3.7 %field_gradient.1 = (bf16[2,288,1024]{2,1,0:T(8,128)(2,1)}, f32[36,36]{1,0:T(8,128)}, f32[3,3,36,36]{3,2,1,0:T(8,128)}, f32[3,3,36,36]{3,2,1,0:T(8,128)}) custom-call(bf16[32,64,128]{2,1,0:T(8,128)(2,1)} %copy-done.2, bf16[1024,256]{1,0:T(8,128)(2,1)} %get-tuple-element.37.high, bf16[1024,256]{1,0:T(8,128)(2,1)} %get-tuple-element.38.low, ...), custom_call_target="tpu_custom_call" | custom-call | tf_op jit(solution)/shard_map/field_gradient/pallas_call | solution.py:722
  (28 shorter events, 3.0 us)
Async XLA Ops:
  4.5 21.1 %copy-start = (f32[2,36,36,9]{2,0,3,1:T(2,128)S(1)}, f32[2,36,36,9]{2,0,3,1:T(2,128)}, u32[]{:S(2)}) copy-start(f32[2,36,36,9]{2,0,3,1:T(2,128)} %param.15) | copy-start | bytes 279940
  4.5 21.1 %all-to-all-start = ((bf16[32,32,128]{2,1,0:T(8,128)(2,1)}), bf16[32,32,128]{2,1,0:T(8,128)(2,1)S(1)}, u32[]{:S(2)}, u32[]{:S(2)}) async-start(bf16[32,32,128]{2,1,0:T(8,128)(2,1)} %bitcast.21), calls=%async_computation | async-start | bytes 524288 | tf_op jit(solution)/shard_map/all_to_all | solution.py:501
  21.3 15.1 %collective-permute-start = (bf16[2,80,1024]{2,1,0:T(8,128)(2,1)}, bf16[2,80,1024]{2,1,0:T(8,128)(2,1)S(1)}, u32[]{:S(2)}, u32[]{:S(2)}) collective-permute-start(bf16[2,80,1024]{2,1,0:T(8,128)(2,1)} %get-tuple-element.40), channel_id=1, source_target_pairs={{0,1},{1,0},{2,3},{3,2},{4,5},{5,4},{6,7},{7,6},{8,9},{9,8},{10,11... | collective-permute-start | bytes 983048 | tf_op jit(solution)/shard_map/ppermute | solution.py:497
  22.6 13.8 %collective-permute-start.1 = (bf16[2,80,1024]{2,1,0:T(8,128)(2,1)}, bf16[2,80,1024]{2,1,0:T(8,128)(2,1)S(1)}, u32[]{:S(2)}, u32[]{:S(2)}) collective-permute-start(bf16[2,80,1024]{2,1,0:T(8,128)(2,1)} %get-tuple-element.41), channel_id=1, source_target_pairs={{1,2},{3,4},{5,6},{7,8},{9,10},{11,12},{13,14},{15,16},{17,18},{19... | collective-permute-start | bytes 983048 | tf_op jit(solution)/shard_map/ppermute | solution.py:497
  27.0 0.6 copy-start.1
  27.6 18.4 %all-to-all-start.1 = ((bf16[32,32,128]{2,1,0:T(8,128)(2,1)}), bf16[32,32,128]{2,1,0:T(8,128)(2,1)S(1)}, u32[]{:S(2)}, u32[]{:S(2)}) async-start(bf16[32,32,128]{2,1,0:T(8,128)(2,1)} %get-tuple-element.36.after), calls=%async_computation.1 | async-start | bytes 524288 | tf_op jit(solution)/shard_map/all_to_all | solution.py:501
  36.4 0.7 copy-start.4
  36.5 0.8 copy-start.5
  46.0 0.7 copy-start.6
  53.7 6.5 %collective-permute-start.2 = (bf16[2,80,1024]{2,1,0:T(8,128)(2,1)}, bf16[2,80,1024]{2,1,0:T(8,128)(2,1)S(1)}, u32[]{:S(2)}, u32[]{:S(2)}) collective-permute-start(bf16[2,80,1024]{2,1,0:T(8,128)(2,1)} %get-tuple-element.49), channel_id=1, source_target_pairs={{0,1},{1,0},{2,3},{3,2},{4,5},{5,4},{6,7},{7,6},{8,9},{9,8},{10,11... | collective-permute-start | bytes 983048 | tf_op jit(solution)/shard_map/ppermute | solution.py:497
  54.7 5.4 %collective-permute-start.3 = (bf16[2,80,1024]{2,1,0:T(8,128)(2,1)}, bf16[2,80,1024]{2,1,0:T(8,128)(2,1)S(1)}, u32[]{:S(2)}, u32[]{:S(2)}) collective-permute-start(bf16[2,80,1024]{2,1,0:T(8,128)(2,1)} %get-tuple-element.50), channel_id=1, source_target_pairs={{1,2},{3,4},{5,6},{7,8},{9,10},{11,12},{13,14},{15,16},{17,18},{19... | collective-permute-start | bytes 983048 | tf_op jit(solution)/shard_map/ppermute | solution.py:497
  60.1 0.7 copy-start.7
  60.1 0.8 copy-start.8
  70.0 26.2 %all-to-all-start.2 = ((bf16[32,48,128]{2,1,0:T(8,128)(2,1)}), bf16[32,48,128]{2,1,0:T(8,128)(2,1)S(1)}, u32[]{:S(2)}, u32[]{:S(2)}) async-start(bf16[32,48,128]{2,1,0:T(8,128)(2,1)} %get-tuple-element.55.after), calls=%async_computation.2 | async-start | bytes 786432 | tf_op jit(solution)/shard_map/all_to_all | solution.py:501
  96.2 0.7 copy-start.3
  98.6 8.3 %collective-permute-start.6 = (f32[80,128]{1,0:T(8,128)}, f32[80,128]{1,0:T(8,128)S(1)}, u32[]{:S(2)}, u32[]{:S(2)}) collective-permute-start(f32[80,128]{1,0:T(8,128)} %own_sums.1.sums.p0), channel_id=1, source_target_pairs={{0,96},{32,64},{64,32},{96,0},{1,97},{33,65},{65,33},{97,1},{2,98}... | collective-permute-start | bytes 122888 | tf_op jit(solution)/shard_map/ppermute | solution.py:704
  103.8 3.7 %collective-permute-start.5 = (f32[80,128]{1,0:T(8,128)}, f32[80,128]{1,0:T(8,128)S(1)}, u32[]{:S(2)}, u32[]{:S(2)}) collective-permute-start(f32[80,128]{1,0:T(8,128)} %own_sums.1.sums.p0), channel_id=1, source_target_pairs={{0,64},{32,96},{64,0},{96,32},{1,65},{33,97},{65,1},{97,33},{2,66}... | collective-permute-start | bytes 122888 | tf_op jit(solution)/shard_map/ppermute | solution.py:704
  104.8 2.7 %collective-permute-start.4 = (f32[80,128]{1,0:T(8,128)}, f32[80,128]{1,0:T(8,128)S(1)}, u32[]{:S(2)}, u32[]{:S(2)}) collective-permute-start(f32[80,128]{1,0:T(8,128)} %own_sums.1.sums.p0), channel_id=1, source_target_pairs={{0,32},{32,0},{64,96},{96,64},{1,33},{33,1},{65,97},{97,65},{2,34}... | collective-permute-start | bytes 122888 | tf_op jit(solution)/shard_map/ppermute | solution.py:704
  106.8 0.7 copy-start.9
  107.5 0.6 copy-start.10
  108.1 0.6 copy-start.11
  110.5 18.8 %all-to-all-start.3 = ((bf16[32,64,128]{2,1,0:T(8,128)(2,1)}), bf16[32,64,128]{2,1,0:T(8,128)(2,1)S(1)}, u32[]{:S(2)}, u32[]{:S(2)}) async-start(bf16[32,64,128]{2,1,0:T(8,128)(2,1)} %gradient_modes.1.after), calls=%async_computation.3 | async-start | bytes 1048576 | tf_op jit(solution)/shard_map/all_to_all | solution.py:501
  129.3 0.8 copy-start.2

commit v5 on v4

--- a/solution.py
+++ b/solution.py
@@ -20,6 +20,7 @@
 SP = 32
 QN = 9
 GR = 3 * CP
+SHARE = 14
 
 ROOT_HALF = 0.7071067811865476
 INV_ROOT_TAU = 0.3989422804014327
@@ -50,35 +51,37 @@
         out[0:24], out[24:48], out[48:72] = high, low, high
         return out
 
-    rows = np.zeros((SP, 2, 16, 256))
+    rows, turned = np.zeros((SP, 32, 256)), np.zeros((SP, 32, 256))
     freq = np.where(np.arange(24) < M, np.arange(24), NR - 24 + np.arange(24))
-    mode_row = np.zeros((SP, 2, 16, 32))
+    mode_row = np.zeros((SP, 32, 32))
     for owner in range(SP):
         for q in range(QN):
             mode = owner * QN + q
             j, kk = mode // M, mode % M
             for r in range(RL):
                 p = 2.0 * np.pi * ((freq[j] * r) % NR) / NR
-                rows[owner, 0, q, r * 24 + kk] = np.cos(p)
-                rows[owner, 0, q, r * 24 + 12 + kk] = np.sin(p)
-                rows[owner, 1, q, r * 24 + kk] = -np.sin(p)
-                rows[owner, 1, q, r * 24 + 12 + kk] = np.cos(p)
-            mode_row[owner, :, q, j] = 1.0
-    high, low = split_np(rows.reshape(SP * 32, 256))
+                for x, line, sign in ((rows, q, 1.0), (turned, QN + q, -1.0)):
+                    x[owner, line, r * 24 + kk] = sign * np.cos(p)
+                    x[owner, line, r * 24 + 12 + kk] = sign * np.sin(p)
+                for x, line in ((rows, QN + q), (turned, q)):
+                    x[owner, line, r * 24 + kk] = -np.sin(p)
+                    x[owner, line, r * 24 + 12 + kk] = np.cos(p)
+            mode_row[owner, q, j] = mode_row[owner, QN + q, j] = 1.0
+    rows, turned = split_np(rows.reshape(SP * 32, 256)), split_np(turned.reshape(SP * 32, 256))
     scale = np.zeros((1, 256), np.float32)
     scale[0, :192] = np.tile(doubled, RL)
     return (
         table,
         inverse(forward * doubled[None, :]),
         inverse(forward),
-        high,
-        low,
+        rows,
+        turned,
         mode_row.reshape(SP * 32, 32).astype(ml_dtypes.bfloat16),
         scale,
     )
 
 
-TABLE, INVERSE, BACK, ROW_HIGH, ROW_LOW, MODE_ROW, SCALE = make_tables()
+TABLE, INVERSE, BACK, ROWS, ROWS_TURNED, MODE_ROW, SCALE = make_tables()
 
 
 def dot(a, b):
@@ -145,18 +148,18 @@
             left[at : at + CO, 0:72] = jnp.concatenate([h, h, w], axis=1)
 
 
-def kernel_a(place, field, table, high, low, mode_row, message, own_high, own_low, flat, cols):
+def kernel_a(place, field, table, high, low, turned_high, turned_low, mode_row, message, own_high, own_low, flat, cols):
     j = lax.broadcasted_iota(jnp.int32, (32, 128), 0)
     turn = ((j + jnp.where(j < M, 0, NR - 24)) * place[0]) % SP
     angle = turn.astype(F32) * (2.0 * math.pi / SP)
     t_high, t_low = split(jnp.concatenate([jnp.cos(angle), jnp.sin(angle)], axis=1))
-    phase = (dot(mode_row[...], t_high) + dot(mode_row[...], t_low)).reshape(SP, 2, 16, 256)[:, 0]
-    cosine, sine = phase[:, :, 0:128], phase[:, :, 128:256]
-    cosine, sine = jnp.concatenate([cosine, cosine], axis=2), jnp.concatenate([sine, sine], axis=2)
-    first = (high[...].astype(F32) + low[...].astype(F32)).reshape(SP, 2, 16, 256)
-    re, im = first[:, 0], first[:, 1]
-    turned = jnp.concatenate([(re * cosine + im * sine)[:, None], (im * cosine - re * sine)[:, None]], axis=1)
-    h, w = split(turned.reshape(SP * 32, 256))
+    phase = dot(mode_row[...], t_high) + dot(mode_row[...], t_low)
+    cosine, sine = phase[:, 0:128], phase[:, 128:256]
+    cosine, sine = jnp.concatenate([cosine, cosine], axis=1), jnp.concatenate([sine, sine], axis=1)
+    first = high[...].astype(F32) + low[...].astype(F32)
+    turned = turned_high[...].astype(F32) + turned_low[...].astype(F32)
+    turned = first * cosine + turned * sine
+    h, w = split(turned)
     own_high[...], own_low[...] = h, w
     flat[...] = dot(field[...], table[...])
     cols[...] = jnp.zeros_like(cols)
@@ -217,7 +220,7 @@
     return ref[i : i + count].reshape(count * GR, NC)
 
 
-def kernel_b(place, rows, first, second, w_one, w_two, w_point, after, middle, slope, pre, taps, mid_taps):
+def kernel_b(place, rows, first, second, w_one, w_two, w_point, middle, slope, pre, taps, mid_taps):
     index = place[0]
     halo = halo_rows(index % 2 == 0, first, second)
     for i, x in enumerate(halo[0:2] + [rows[0, r].astype(F32) for r in range(RL)] + halo[2:4]):
@@ -249,7 +252,7 @@
 def by_channel(own, real, imag):
     rest = jnp.zeros((96, 128), F32)
     real[...] = jnp.transpose(jnp.concatenate([own, rest], axis=0))
-    imag[...] = jnp.transpose(jnp.concatenate([own[16:32], own[0:16], rest], axis=0))
+    imag[...] = jnp.transpose(jnp.concatenate([pltpu.roll(own, 32 - QN, 0), rest], axis=0))
 
 
 def weight_rows(weight, lines):
@@ -276,7 +279,7 @@
             re.append(jnp.sum(w_re * s_re - w_im * s_im, axis=0, keepdims=True))
             im.append(jnp.sum(w_im * s_re + w_re * s_im, axis=0, keepdims=True))
         mixed[q : q + 1] = re[0] + pltpu.roll(re[1], 64, 1)
-        mixed[16 + q : 17 + q] = im[0] + pltpu.roll(im[1], 64, 1)
+        mixed[QN + q : QN + q + 1] = im[0] + pltpu.roll(im[1], 64, 1)
     message[...] = jnp.broadcast_to(mixed[0:32].astype(BF)[None], (SP, 32, 128))
 
 
@@ -286,14 +289,14 @@
     for q in range(QN):
         w_re, w_im = mode_line(lines, q, 0), mode_line(lines, q, 1)
         for lev, z in enumerate((own, other)):
-            z_re, z_im = z[q : q + 1], z[16 + q : 17 + q]
+            z_re, z_im = z[q : q + 1], z[QN + q : QN + q + 1]
             at = lev * 64
             mixed[at : at + C, q : q + 1] = jnp.sum(w_re * z_re + w_im * z_im, axis=1, keepdims=True)
-            mixed[at : at + C, 16 + q : 17 + q] = jnp.sum(w_re * z_im - w_im * z_re, axis=1, keepdims=True)
+            mixed[at : at + C, QN + q : QN + q + 1] = jnp.sum(w_re * z_im - w_im * z_re, axis=1, keepdims=True)
     return jnp.transpose(mixed[...])[0:32].astype(BF)
 
 
-def kernel_spec_grad(p0, p1, p2, p3, after, grad, s_re, s_im, lines):
+def kernel_spec_grad(p0, p1, p2, p3, grad, s_re, s_im, lines):
     pairs = (p0, p1, p2, p3)
     co = []
     for i, pair in enumerate(pairs):
@@ -306,7 +309,7 @@
             for lev in range(LEV):
                 at = lev * 64
                 a, b = s_re[i, at : at + C, q : q + 1], s_im[i, at : at + C, q : q + 1]
-                x, y = co[i][lev][q : q + 1], co[i][lev][16 + q : 17 + q]
+                x, y = co[i][lev][q : q + 1], co[i][lev][QN + q : QN + q + 1]
                 re = re + (a * x + b * y)
                 im = im + (a * y - b * x)
             res.append(re)
@@ -356,10 +359,9 @@
             out[lev, :, n : n + 128] = wide[n // 128, lev * C * RL : (lev + 1) * C * RL].astype(BF)
 
 
-def kernel_own(received, kept, first, second, sums):
+def kernel_own(received, kept, sums):
     sums[0:32] = kept[...]
-    sums[32:64] = own_modes(received[:, 0:32])
-    sums[64:80] = own_modes(received[:, 32:48])
+    sums[32:64] = own_modes(received[...])
 
 
 def kernel_mix_back(sums, weight, cofield, mixed, lines):
@@ -368,9 +370,10 @@
 
 
 def kernel_send_back(cofield, p0, p1, p2, p3, message):
-    total = (p0[64:80] + p1[64:80]) + (p2[64:80] + p3[64:80])
-    high, low = split(total)
-    message[...] = jnp.broadcast_to(jnp.concatenate([cofield[...], high, low], axis=0)[None], (SP, 64, 128))
+    total = (p0[32:64] + p1[32:64]) + (p2[32:64] + p3[32:64])
+    row = lax.broadcasted_iota(jnp.int32, (32, 128), 0)
+    total = jnp.where(row < 2 * QN, cofield[...].astype(F32), total).astype(BF)
+    message[...] = jnp.broadcast_to(total[None], (SP, 32, 128))
 
 
 def kernel_e_zero(slopes, middle, rows, grad_two, taps):
@@ -390,7 +393,7 @@
         grad_two[...] += part
 
 
-def kernel_e(place, slopes, first, second, rows, f_first, f_second, slope, w_two, modes, grad_two, pre_slope, message, taps, pre_taps, grad_one, sums):
+def kernel_e(place, slopes, first, second, rows, f_first, f_second, slope, w_two, modes, grad_two, pre_slope, message, taps, pre_taps, grad_one, sums, packed):
     index = place[0]
     lev = pl.program_id(0)
     even = index % 2 == 0
@@ -423,11 +426,14 @@
         sums[...] = jnp.zeros_like(sums)
         two, one = grad_two[...], grad_one[...] + part_one
         for b in range(3):
-            sums[b * GR : (b + 1) * GR, 0:CP] = two[0:GR, b * CP : (b + 1) * CP]
-            sums[b * GR : (b + 1) * GR, 64 : 64 + CP] = one[:, b * CP : (b + 1) * CP]
-        sums[3 * GR : 3 * GR + CP, 0:CP] = two[GR : GR + CP, CP : 2 * CP]
-        message[:, 0:32] = modes[...]
-        message[:, 32:48] = sums[...].reshape(SP, 16, 128).astype(BF)
+            at = b * CP
+            sums[b * GR : (b + 1) * GR, 0:C] = two[0:GR, at : at + C]
+            sums[b * GR : (b + 1) * GR, C : 2 * C] = one[:, at : at + C]
+        sums[0:CP, 2 * C : 3 * C] = two[GR : GR + CP, CP : CP + C]
+        packed[...] = modes[...].astype(F32)
+        for owner in range(SP):
+            packed[owner, 2 * QN : 32] = sums[owner * SHARE : (owner + 1) * SHARE]
+        message[...] = packed[...].astype(BF)
 
 
 def kernel_e_two(pre_slope, slopes, w_one, w_point, after, back, taps, wide):
@@ -443,12 +449,12 @@
         back[0, :, n : n + 128] = wide[n // 128]
 
 
-def kernel_f(received, high, low, inverse, back, out, point, one, two, left):
+def kernel_f(received, high, low, inverse, back, out, point, one, two, left, packed, sums):
     lev = pl.program_id(0)
 
     @pl.when(lev == 0)
     def _():
-        modes = received[:, 0:32].reshape(SP * 32, 128)
+        modes = received[...].reshape(SP * 32, 128)
         r_high, r_low = split(row_expand(modes, high[...], low[...]))
         r_high, r_low = r_high.astype(F32), r_low.astype(F32)
         rest = jnp.zeros((C, 56), F32)
@@ -457,14 +463,16 @@
                 h = r_high[at * 64 : at * 64 + C, r * 24 : r * 24 + 24]
                 w = r_low[at * 64 : at * 64 + C, r * 24 : r * 24 + 24]
                 left[at, pl.ds(r, C, stride=RL), :] = jnp.concatenate([h, h, w, rest], axis=1)
-        total = (received[:, 32:48].astype(F32) + received[:, 48:64].astype(F32)).reshape(SP * 16, 128)
-        scaled = total * (1.0 / math.sqrt(NR * NC * LEV * 4))
+        packed[...] = received[...].astype(F32)
+        for owner in range(SP):
+            sums[owner * SHARE : (owner + 1) * SHARE] = packed[owner, 2 * QN : 32]
+        scaled = sums[...] * (1.0 / math.sqrt(NR * NC * LEV * 4))
         for a in range(3):
             for b in range(3):
                 at = (2 - b) * GR + a * CP
                 two[a, b] = scaled[at : at + C, 0:C]
-                one[a, b] = scaled[at : at + C, 64 : 64 + C]
-        point[...] = scaled[3 * GR : 3 * GR + C, 0:C]
+                one[a, b] = scaled[at : at + C, C : 2 * C]
+        point[...] = scaled[0:C, 2 * C : 3 * C]
 
     out[0] = (back[0] + dot(left[lev].astype(BF), inverse[...])).astype(BF)
 
@@ -531,7 +539,7 @@
     row_matrix = shape((SP * 32, 256), BF)
     message, high, low = plain_call(
         kernel_a,
-        (inputs, table, jnp.asarray(ROW_HIGH), jnp.asarray(ROW_LOW), jnp.asarray(MODE_ROW)),
+        (inputs, table, *map(jnp.asarray, ROWS + ROWS_TURNED), jnp.asarray(MODE_ROW)),
         (),
         [shape((SP * 32, 128), BF), row_matrix, row_matrix],
         [flat, cols],
@@ -590,7 +598,6 @@
             whole_spec(4 * CP, 6 * GR),
             whole_spec(4 * CP, 6 * GR),
             whole_spec(4 * CP, 4 * CP),
-            anywhere(),
         ],
         out_specs=[
             level_spec(RL + 2, CP, NC),
@@ -605,7 +612,7 @@
         scratch_shapes=[pltpu.VMEM((RL + 4, GR, NC), BF), pltpu.VMEM((RL + 2, GR, NC), BF)],
         compiler_params=params(56),
         name="two_convolutions",
-    )(place, rows, f_first, f_second, w_one, w_two, w_point, mixed)
+    )(place, rows, f_first, f_second, w_one, w_two, w_point)
 
     left, spec = pltpu.VMEM((LEV * RL * CO, 128), F32), pltpu.VMEM((LEV * RL * CO, NC), F32)
     values, slopes, s_first, s_second, message = pl.pallas_call(
@@ -661,13 +668,14 @@
             whole_spec(SP, 32, 128),
             whole_spec(GR + CP, GR),
         ],
-        out_specs=[level_spec(RL + 2, CP, NC), whole_spec(SP, 48, 128)],
-        out_shape=[shape((LEV, RL + 2, CP, NC), BF), shape((SP, 48, 128), BF)],
+        out_specs=[level_spec(RL + 2, CP, NC), whole_spec(SP, 32, 128)],
+        out_shape=[shape((LEV, RL + 2, CP, NC), BF), shape((SP, 32, 128), BF)],
         scratch_shapes=[
             pltpu.VMEM((RL + 4, GR, NC), BF),
             pltpu.VMEM((RL + 2, GR, NC), BF),
             pltpu.VMEM((GR, GR), F32),
-            pltpu.VMEM((SP * 16, 128), F32),
+            pltpu.VMEM((SP * SHARE, 128), F32),
+            pltpu.VMEM((SP, 32, 128), F32),
         ],
         compiler_params=params(56),
         name="slope_and_weight_gradients",
@@ -699,23 +707,23 @@
         "output_layout",
     )
     (sums,) = plain_call(
-        kernel_own, (arrived, kept), (back, out), [shape((80, 128), F32)], [], 56, "own_sums"
+        kernel_own, (arrived, kept), (), [shape((64, 128), F32)], [], 8, "own_sums"
     )
     others = [lax.ppermute(sums, "rep", [(i, i ^ k) for i in range(4)]) for k in (1, 2, 3)]
     (cofield,) = plain_call(
-        kernel_mix_back, (sums, weight), (), [shape((32, 128), BF)], [square, lines], 56, "mode_mix_back"
+        kernel_mix_back, (sums, weight), (), [shape((32, 128), BF)], [square, lines], 8, "mode_mix_back"
     )
     (message,) = plain_call(
-        kernel_send_back, (cofield, sums, *others), (), [shape((SP, 64, 128), BF)], [], 56, "gradient_modes"
+        kernel_send_back, (cofield, sums, *others), (), [shape((SP, 32, 128), BF)], [], 8, "gradient_modes"
     )
     gathered = exchange(message)
     (spec_grad,) = plain_call(
         kernel_spec_grad,
         (sums, *others),
-        (message,),
+        (),
         [shape(weight.shape, F32)],
         [pltpu.VMEM((4, 128, 128), F32)] * 2 + [lines],
-        56,
+        8,
         "spectral_gradient",
     )
     kernel_out_shape = shape((3, 3, C, C), F32)
@@ -723,7 +731,7 @@
         kernel_f,
         grid=(LEV,),
         in_specs=[
-            whole_spec(SP, 64, 128),
+            whole_spec(SP, 32, 128),
             whole_spec(SP * 32, 256),
             whole_spec(SP * 32, 256),
             whole_spec(128, NC),
@@ -731,7 +739,11 @@
         ],
         out_specs=[level_spec(C * RL, NC), whole_spec(C, C), whole_spec(3, 3, C, C), whole_spec(3, 3, C, C)],
         out_shape=[natural, shape((C, C), F32), kernel_out_shape, kernel_out_shape],
-        scratch_shapes=[pltpu.VMEM((LEV, C * RL, 128), F32)],
+        scratch_shapes=[
+            pltpu.VMEM((LEV, C * RL, 128), F32),
+            pltpu.VMEM((SP, 32, 128), F32),
+            pltpu.VMEM((SP * SHARE, 128), F32),
+        ],
         compiler_params=params(56),
         name="field_gradient",
     )(gathered, high, low, jnp.asarray(BACK), back)

time: 136 us -> 124 us (0.912); the launches traced: 134 us -> 124 us
  blocking collectives: 0 us -> 24.9 us
  starting transfers between devices: 53.7 us -> 35.2 us
  waiting for transfers between devices: 13.3 us -> 4.2 us
  Pallas kernels: 60.3 us -> 55.4 us
  local copies, waits for them, and re-layouts: 5.72 us -> 3.03 us
    all_to_all x0 -> x1, blocking collectives: none -> 24.9 us  [exchange(): return lax.all_to_all(x, 'sp', 0, 0, tiled=True)]
    all_to_all x4 -> x3, starting transfers between devices: 43.6 us -> 24.2 us  [exchange(): return lax.all_to_all(x, 'sp', 0, 0, tiled=True)]
    all_to_all x4 -> x3, waiting for transfers between devices: 12.6 us -> 2.5 us  [exchange(): return lax.all_to_all(x, 'sp', 0, 0, tiled=True)]
    pallas_call x7, Pallas kernels: 16.7 us -> 11.9 us  [plain_call(): pl.pallas_call(kernel, in_specs=[pl.BlockSpec(memory_space=pltpu.SMEM)] *...]
    unnamed x24 -> x14, local copies, waits for them, and re-layouts: 5.72 us -> 3.03 us
  transfers between devices with their start and end apart: 11 -> 10, of which waited for: 5 -> 4; matrix products, arithmetic and copies ran while one was open for 0% -> 0% of each run, Pallas kernels for 25% -> 25%
where the time goes in v5:
time: 124 us
  Pallas kernels  55.4 us (45%)
  starting transfers between devices  35.2 us (28%)
  blocking collectives  24.9 us (20%)
  waiting for transfers between devices  4.2 us (3%)
  local copies, waits for them, and re-layouts  3.03 us (2%)
    all_to_all x1, blocking collectives, exchange(): return lax.all_to_all(x, 'sp', 0, 0, tiled=True)  24.9 us
    all_to_all x3, starting transfers between devices, exchange(): return lax.all_to_all(x, 'sp', 0, 0, tiled=True)  24.2 us
    pallas_call x7, Pallas kernels, plain_call(): pl.pallas_call(kernel, in_specs=[pl.BlockSpec(memory_space=pltpu.SMEM)] *...  11.9 us
    pallas_call x1, Pallas kernels, local(): pl.pallas_call(kernel_e, grid=(LEV,), in_specs=[pl.BlockSpec(memory_space...  9.02 us
    pallas_call x1, Pallas kernels, local(): pl.pallas_call(kernel_b, grid=(LEV,), in_specs=[pl.BlockSpec(memory_space...  8.48 us
    ppermute x3, starting transfers between devices, local(): lax.ppermute(sums, 'rep', [(i, i ^ k) for i in range(4)])  7.23 us
    pallas_call x1, Pallas kernels, local(): pl.pallas_call(kernel_d, grid=(LEV,), in_specs=[pl.BlockSpec(memory_space...  6.97 us
    pallas_call x1, Pallas kernels, local(): pl.pallas_call(kernel_e_two, grid=(LEV,), in_specs=[level_spec(RL + 2, CP...  5.55 us
  transfers between devices with their start and end apart: 10, of which 4 were waited for; matrix products, arithmetic and copies ran while one was open for 0% of the time, Pallas kernels for 25%

profile of v5, /device:TPU:1, one launch (start us, length us, event | category | flops | bytes accessed | tf_op | source)
XLA Modules:
  0.0 123.6 jit_solution(9394365625625189742)
XLA Ops:
  0.6 4.1 %field_modes.1 = (bf16[1024,128]{1,0:T(8,128)(2,1)}, bf16[1024,256]{1,0:T(8,128)(2,1)}, bf16[1024,256]{1,0:T(8,128)(2,1)}) custom-call(s32[1]{0:T(128)} %bitcast.place, bf16[576,1024]{1,0:T(8,128)(2,1)} %bitcast.17, bf16[1024,128]{1,0:T(8,128)(2,1)} %constant.22.clone.table, bf16[1024,256]{1,0:T(8,128)(2,1)} %constant.23.clone.high, ...), custom_call_target="tpu_custom_call" | custom-call | tf_op jit(solution)/shard_map/field_modes/pallas_call | solution.py:518
  4.8 11.5 %all-to-all-start = ((bf16[32,32,128]{2,1,0:T(8,128)(2,1)}), bf16[32,32,128]{2,1,0:T(8,128)(2,1)S(1)}, u32[]{:S(2)}, u32[]{:S(2)}) async-start(bf16[32,32,128]{2,1,0:T(8,128)(2,1)} %bitcast.21), calls=%async_computation | async-start | bytes 524288 | tf_op jit(solution)/shard_map/all_to_all | solution.py:509
  16.2 5.4 %row_layout.1 = (bf16[2,8,48,1024]{3,2,1,0:T(8,128)(2,1)}, bf16[2,80,1024]{2,1,0:T(8,128)(2,1)}, bf16[2,80,1024]{2,1,0:T(8,128)(2,1)}, bf16[2,8,48,1024]{3,2,1,0...) custom-call(s32[1]{0:T(128)} %bitcast.place, ...), custom_call_target="tpu_custom_call" | custom-call | tf_op jit(solution)/shard_map/row_layout/pallas_call | solution.py:553
  21.6 1.3 %collective-permute-start = (bf16[2,80,1024]{2,1,0:T(8,128)(2,1)}, bf16[2,80,1024]{2,1,0:T(8,128)(2,1)S(1)}, u32[]{:S(2)}, u32[]{:S(2)}) collective-permute-start(bf16[2,80,1024]{2,1,0:T(8,128)(2,1)} %get-tuple-element.40), channel_id=1, source_target_pairs={{0,1},{1,0},{2,3},{3,2},{4,5},{5,4},{6,7},{7,6},{8,9},{9,8},{10,11... | collective-permute-start | bytes 983048 | tf_op jit(solution)/shard_map/ppermute | solution.py:505
  22.9 0.7 collective-permute-start.1
  23.6 2.2 %all-to-all-done.received = bf16[32,32,128]{2,1,0:T(8,128)(2,1)S(1)} async-done(((bf16[32,32,128]{2,1,0:T(8,128)(2,1)}), bf16[32,32,128]{2,1,0:T(8,128)(2,1)S(1)}, u32[]{:S(2)}, u32[]{:S(2)}) %all-to-all-start) | async-done | bytes 262176 | tf_op jit(solution)/shard_map/all_to_all | solution.py:509
  25.9 1.4 %mode_mix.1 = (bf16[32,32,128]{2,1,0:T(8,128)(2,1)}, f32[32,128]{1,0:T(8,128)S(1)}) custom-call(bf16[32,32,128]{2,1,0:T(8,128)(2,1)S(1)} %all-to-all-done.received, f32[648,36]{1,0:T(8,128)S(1)} %bitcast.15), custom_call_target="tpu_custom_call" | custom-call | tf_op jit(solution)/shard_map/mode_mix/pallas_call | solution.py:518
  27.3 8.8 %all-to-all-start.1 = ((bf16[32,32,128]{2,1,0:T(8,128)(2,1)}), bf16[32,32,128]{2,1,0:T(8,128)(2,1)S(1)}, u32[]{:S(2)}, u32[]{:S(2)}) async-start(bf16[32,32,128]{2,1,0:T(8,128)(2,1)} %get-tuple-element.36), calls=%async_computation.1 | async-start | bytes 524288 | tf_op jit(solution)/shard_map/all_to_all | solution.py:509
  36.1 0.7 copy-done.1
  36.9 8.5 %two_convolutions.1 = (bf16[2,10,48,1024]{3,2,1,0:T(8,128)(2,1)}, bf16[2,10,48,1024]{3,2,1,0:T(8,128)(2,1)}, f32[2,8,40,1024]{3,2,1,0:T(8,128)}) custom-call(s32[1]{0:T(128)} %bitcast.place, bf16[2,8,48,1024]{3,2,1,0:T(8,128)(2,1)} %get-tuple-element.39.rows, bf16[2,80,1024]{2,1,0:T(8,128)(2,1)} %copy-done.1, bf16[2,80,1024]{2,1,0:T(8,128)(2,1)} %copy-done.2, ...), custom_call_target="tpu_custom_call" | custom-call | tf_op jit(solution)/shard_map/two_convolutions/pallas_call | solution.py:590
  45.4 0.3 all-to-all-done.1
  45.7 0.7 copy-done.3
  46.4 7.0 %output_and_slope.1 = (bf16[2,8,48,1024]{3,2,1,0:T(8,128)(2,1)}, bf16[2,8,48,1024]{3,2,1,0:T(8,128)(2,1)}, bf16[2,80,1024]{2,1,0:T(8,128)(2,1)}, bf16[2,80,1024]{2,1,0:T(8,128)(2,1)}, bf16[1024,128]{1,0:T(8,128)(2,1)}) custom-call(s32[1]{0:T(128)} %bitcast.place, bf16[1024,128]{1,0:T(8,128)(2,1)} %bitcast.22, bf16[1024,256]{1,0:T(8,128)(2,1)} %get-tuple-element.37.high, ...), custom_call_target="tpu_custom_call" | custom-call | tf_op jit(solution)/shard_map/output_and_slope/pallas_call | solution.py:618
  53.4 1.0 collective-permute-start.2
  54.4 0.8 collective-permute-start.3
  55.3 4.5 %weight_gradients_two.1.grad_two = f32[192,144]{1,0:T(8,128)} custom-call(bf16[2,8,48,1024]{3,2,1,0:T(8,128)(2,1)} %get-tuple-element.48.slopes, bf16[2,10,48,1024]{3,2,1,0:T(8,128)(2,1)} %get-tuple-element.54.middle, bf16[2,8,48,1024]{3,2,1,0:T(8,128)(2,1)} %get-tuple-element.39.rows), custom_call_target="tpu_custom_call" | custom-call | tf_op jit(solution)/shard_map/weight_gradients_two/pallas_call | solution.py:645
  59.8 0.7 copy-done.5
  60.5 0.1 copy-done.6
  60.6 9.0 %slope_and_weight_gradients.1 = (bf16[2,10,48,1024]{3,2,1,0:T(8,128)(2,1)}, bf16[32,32,128]{2,1,0:T(8,128)(2,1)}) custom-call(s32[1]{0:T(128)} %bitcast.place, bf16[2,8,48,1024]{3,2,1,0:T(8,128)(2,1)} %get-tuple-element.48.slopes, bf16[2,80,1024]{2,1,0:T(8,128)(2,1)} %copy-done.5, bf16[2,80,1024]{2,1,0:T(8,128)(2,1)} %copy-done.6, ...), custom_call_target="tpu_custom_call" | custom-call | tf_op jit(solution)/shard_map/slope_and_weight_gradients/pallas_call | solution.py:655
  69.6 24.9 %all_to_all.20.received = bf16[32,32,128]{2,1,0:T(8,128)(2,1)S(1)} all-to-all(bf16[32,32,128]{2,1,0:T(8,128)(2,1)} %get-tuple-element.55.after), channel_id=1, replica_groups=mesh['rep'=4,'sp'=32] {'sp'}, dimensions={0} | all-to-all | bytes 524288 | tf_op jit(solution)/shard_map/all_to_all | solution.py:509
  94.6 6.2 %collective-permute-start.6 = (f32[64,128]{1,0:T(8,128)S(1)}, f32[64,128]{1,0:T(8,128)S(1)}, u32[]{:S(2)}, u32[]{:S(2)}) collective-permute-start(f32[64,128]{1,0:T(8,128)S(1)} %own_sums.1.sums.p0), channel_id=1, source_target_pairs={{0,96},{32,64},{64,32},{96,0},{1,97},{33,65},{65,33},{97,1},{2,98}... | collective-permute-start | bytes 98312 | tf_op jit(solution)/shard_map/ppermute | solution.py:712
  100.8 1.1 collective-permute-start.5
  101.9 0.4 mode_mix_back.1.cofield
  102.2 0.1 collective-permute-done.6.p3
  102.4 1.5 %collective-permute-done.5.p2 = f32[64,128]{1,0:T(8,128)S(1)} collective-permute-done((f32[64,128]{1,0:T(8,128)S(1)}, f32[64,128]{1,0:T(8,128)S(1)}, u32[]{:S(2)}, u32[]{:S(2)}) %collective-permute-start.5) | collective-permute-done | bytes 32800 | tf_op jit(solution)/shard_map/ppermute | solution.py:712
  103.9 0.7 gradient_modes.1
  104.7 3.9 %all-to-all-start.3 = ((bf16[32,32,128]{2,1,0:T(8,128)(2,1)}), bf16[32,32,128]{2,1,0:T(8,128)(2,1)S(1)}, u32[]{:S(2)}, u32[]{:S(2)}) async-start(bf16[32,32,128]{2,1,0:T(8,128)(2,1)} %gradient_modes.1), calls=%async_computation.3 | async-start | bytes 524288 | tf_op jit(solution)/shard_map/all_to_all | solution.py:509
  108.5 3.4 %output_layout.1 = bf16[2,288,1024]{2,1,0:T(8,128)(2,1)} custom-call(bf16[2,8,48,1024]{3,2,1,0:T(8,128)(2,1)} %get-tuple-element.47.values, bf16[32,32,128]{2,1,0:T(8,128)(2,1)} %get-tuple-element.55.after), custom_call_target="tpu_custom_call" | custom-call | tf_op jit(solution)/shard_map/output_layout/pallas_call | solution.py:518
  111.9 5.5 %backward_convolution.1.back = f32[2,288,1024]{2,1,0:T(8,128)} custom-call(bf16[2,10,48,1024]{3,2,1,0:T(8,128)(2,1)} %get-tuple-element.57.pre_slope, bf16[2,8,48,1024]{3,2,1,0:T(8,128)(2,1)} %get-tuple-element.48.slopes, bf16[192,864]{1,0:T(8,128)(2,1)} %get-tuple-element.58.w_one, bf16[192,192]{1,0:T(8,128)(2,1)} %get-tuple-element.59.w_point, ...), custom_call_target="tpu_custom_call" | custom-call | tf_op jit(solution)/shard_map/backward_convolution/pallas_call | solution.py:684
  117.4 1.8 %spectral_gradient.1 = f32[648,36]{1,0:T(8,128)} custom-call(f32[64,128]{1,0:T(8,128)S(1)} %own_sums.1.sums.p0, f32[64,128]{1,0:T(8,128)S(1)} %collective-permute-done.4.p1, f32[64,128]{1,0:T(8,128)S(1)} %collective-permute-done.5.p2, f32[64,128]{1,0:T(8,128)S(1)} %collective-permute-done.6.p3), custom_call_target="tpu_custom_call" | custom-call | tf_op jit(solution)/shard_map/spectral_gradient/pallas_call | solution.py:518
  119.3 0.7 copy-done.4
  120.0 3.6 %field_gradient.1 = (bf16[2,288,1024]{2,1,0:T(8,128)(2,1)}, f32[36,36]{1,0:T(8,128)}, f32[3,3,36,36]{3,2,1,0:T(8,128)}, f32[3,3,36,36]{3,2,1,0:T(8,128)}) custom-call(bf16[32,32,128]{2,1,0:T(8,128)(2,1)} %copy-done.4, bf16[1024,256]{1,0:T(8,128)(2,1)} %get-tuple-element.37.high, bf16[1024,256]{1,0:T(8,128)(2,1)} %get-tuple-element.38.low, ...), custom_call_target="tpu_custom_call" | custom-call | tf_op jit(solution)/shard_map/field_gradient/pallas_call | solution.py:730
  (17 shorter events, 0.2 us)
Async XLA Ops:
  4.8 21.1 %copy-start = (f32[2,36,36,9]{2,0,3,1:T(2,128)S(1)}, f32[2,36,36,9]{2,0,3,1:T(2,128)}, u32[]{:S(2)}) copy-start(f32[2,36,36,9]{2,0,3,1:T(2,128)} %param.17) | copy-start | bytes 279940
  4.8 21.1 %all-to-all-start = ((bf16[32,32,128]{2,1,0:T(8,128)(2,1)}), bf16[32,32,128]{2,1,0:T(8,128)(2,1)S(1)}, u32[]{:S(2)}, u32[]{:S(2)}) async-start(bf16[32,32,128]{2,1,0:T(8,128)(2,1)} %bitcast.21), calls=%async_computation | async-start | bytes 524288 | tf_op jit(solution)/shard_map/all_to_all | solution.py:509
  21.6 14.5 %collective-permute-start = (bf16[2,80,1024]{2,1,0:T(8,128)(2,1)}, bf16[2,80,1024]{2,1,0:T(8,128)(2,1)S(1)}, u32[]{:S(2)}, u32[]{:S(2)}) collective-permute-start(bf16[2,80,1024]{2,1,0:T(8,128)(2,1)} %get-tuple-element.40), channel_id=1, source_target_pairs={{0,1},{1,0},{2,3},{3,2},{4,5},{5,4},{6,7},{7,6},{8,9},{9,8},{10,11... | collective-permute-start | bytes 983048 | tf_op jit(solution)/shard_map/ppermute | solution.py:505
  22.9 13.2 %collective-permute-start.1 = (bf16[2,80,1024]{2,1,0:T(8,128)(2,1)}, bf16[2,80,1024]{2,1,0:T(8,128)(2,1)S(1)}, u32[]{:S(2)}, u32[]{:S(2)}) collective-permute-start(bf16[2,80,1024]{2,1,0:T(8,128)(2,1)} %get-tuple-element.41), channel_id=1, source_target_pairs={{1,2},{3,4},{5,6},{7,8},{9,10},{11,12},{13,14},{15,16},{17,18},{19... | collective-permute-start | bytes 983048 | tf_op jit(solution)/shard_map/ppermute | solution.py:505
  27.3 18.4 %all-to-all-start.1 = ((bf16[32,32,128]{2,1,0:T(8,128)(2,1)}), bf16[32,32,128]{2,1,0:T(8,128)(2,1)S(1)}, u32[]{:S(2)}, u32[]{:S(2)}) async-start(bf16[32,32,128]{2,1,0:T(8,128)(2,1)} %get-tuple-element.36), calls=%async_computation.1 | async-start | bytes 524288 | tf_op jit(solution)/shard_map/all_to_all | solution.py:509
  36.1 0.7 copy-start.1
  36.1 0.8 copy-start.2
  45.7 0.7 copy-start.3
  53.4 6.4 %collective-permute-start.2 = (bf16[2,80,1024]{2,1,0:T(8,128)(2,1)}, bf16[2,80,1024]{2,1,0:T(8,128)(2,1)S(1)}, u32[]{:S(2)}, u32[]{:S(2)}) collective-permute-start(bf16[2,80,1024]{2,1,0:T(8,128)(2,1)} %get-tuple-element.49), channel_id=1, source_target_pairs={{0,1},{1,0},{2,3},{3,2},{4,5},{5,4},{6,7},{7,6},{8,9},{9,8},{10,11... | collective-permute-start | bytes 983048 | tf_op jit(solution)/shard_map/ppermute | solution.py:505
  54.4 5.4 %collective-permute-start.3 = (bf16[2,80,1024]{2,1,0:T(8,128)(2,1)}, bf16[2,80,1024]{2,1,0:T(8,128)(2,1)S(1)}, u32[]{:S(2)}, u32[]{:S(2)}) collective-permute-start(bf16[2,80,1024]{2,1,0:T(8,128)(2,1)} %get-tuple-element.50), channel_id=1, source_target_pairs={{1,2},{3,4},{5,6},{7,8},{9,10},{11,12},{13,14},{15,16},{17,18},{19... | collective-permute-start | bytes 983048 | tf_op jit(solution)/shard_map/ppermute | solution.py:505
  59.8 0.7 copy-start.5
  59.8 0.8 copy-start.6
  94.6 7.8 %collective-permute-start.6 = (f32[64,128]{1,0:T(8,128)S(1)}, f32[64,128]{1,0:T(8,128)S(1)}, u32[]{:S(2)}, u32[]{:S(2)}) collective-permute-start(f32[64,128]{1,0:T(8,128)S(1)} %own_sums.1.sums.p0), channel_id=1, source_target_pairs={{0,96},{32,64},{64,32},{96,0},{1,97},{33,65},{65,33},{97,1},{2,98}... | collective-permute-start | bytes 98312 | tf_op jit(solution)/shard_map/ppermute | solution.py:712
  100.8 3.1 %collective-permute-start.5 = (f32[64,128]{1,0:T(8,128)S(1)}, f32[64,128]{1,0:T(8,128)S(1)}, u32[]{:S(2)}, u32[]{:S(2)}) collective-permute-start(f32[64,128]{1,0:T(8,128)S(1)} %own_sums.1.sums.p0), channel_id=1, source_target_pairs={{0,64},{32,96},{64,0},{96,32},{1,65},{33,97},{65,1},{97,33},{2,66}... | collective-permute-start | bytes 98312 | tf_op jit(solution)/shard_map/ppermute | solution.py:712
  101.9 2.1 %collective-permute-start.4 = (f32[64,128]{1,0:T(8,128)S(1)}, f32[64,128]{1,0:T(8,128)S(1)}, u32[]{:S(2)}, u32[]{:S(2)}) collective-permute-start(f32[64,128]{1,0:T(8,128)S(1)} %own_sums.1.sums.p0), channel_id=1, source_target_pairs={{0,32},{32,0},{64,96},{96,64},{1,33},{33,1},{65,97},{97,65},{2,34}... | collective-permute-start | bytes 98312 | tf_op jit(solution)/shard_map/ppermute | solution.py:712
  104.7 14.6 %all-to-all-start.3 = ((bf16[32,32,128]{2,1,0:T(8,128)(2,1)}), bf16[32,32,128]{2,1,0:T(8,128)(2,1)S(1)}, u32[]{:S(2)}, u32[]{:S(2)}) async-start(bf16[32,32,128]{2,1,0:T(8,128)(2,1)} %gradient_modes.1), calls=%async_computation.3 | async-start | bytes 524288 | tf_op jit(solution)/shard_map/all_to_all | solution.py:509
  119.3 0.7 copy-start.4

commit v6 on v5

--- a/solution.py
+++ b/solution.py
@@ -113,15 +113,13 @@
     taps[i, 2 * CP : 3 * CP] = jnp.where(col == NC - 1, 0.0, pltpu.roll(x, NC - 1, 1)).astype(BF)
 
 
-def row_transform(cols, high, low):
-    c_high, c_low = split(cols)
-    both = dot_nt(high, jnp.concatenate([c_high, c_low], axis=0))
-    return (both[:, 0:128] + both[:, 128:256] + dot_nt(low, c_high)).astype(BF)
-
-
-def row_expand(modes, high, low):
-    both = dot_tn(modes, jnp.concatenate([high, low], axis=1))
-    return both[:, 0:256] + both[:, 256:512]
+def row_transform(cols, matrix):
+    both = dot_nt(matrix, jnp.concatenate(split(cols), axis=0))
+    return (both[:, 0:128] + both[:, 128:256]).astype(BF)
+
+
+def row_expand(modes, matrix):
+    return dot_tn(modes, matrix)
 
 
 def strip_pair(even, top, bottom):
@@ -148,7 +146,7 @@
             left[at : at + CO, 0:72] = jnp.concatenate([h, h, w], axis=1)
 
 
-def kernel_a(place, field, table, high, low, turned_high, turned_low, mode_row, message, own_high, own_low, flat, cols):
+def kernel_a(place, field, table, high, low, turned_high, turned_low, mode_row, message, matrix, flat, cols):
     j = lax.broadcasted_iota(jnp.int32, (32, 128), 0)
     turn = ((j + jnp.where(j < M, 0, NR - 24)) * place[0]) % SP
     angle = turn.astype(F32) * (2.0 * math.pi / SP)
@@ -158,16 +156,15 @@
     cosine, sine = jnp.concatenate([cosine, cosine], axis=1), jnp.concatenate([sine, sine], axis=1)
     first = high[...].astype(F32) + low[...].astype(F32)
     turned = turned_high[...].astype(F32) + turned_low[...].astype(F32)
-    turned = first * cosine + turned * sine
-    h, w = split(turned)
-    own_high[...], own_low[...] = h, w
+    turned = (first * cosine + turned * sine).astype(BF)
+    matrix[...] = turned
     flat[...] = dot(field[...], table[...])
     cols[...] = jnp.zeros_like(cols)
     for lev in range(LEV):
         for r in range(RL):
             part = flat[pl.ds(lev * C * RL + r, C, stride=RL), :]
             cols[lev * 64 : lev * 64 + C, r * 24 : r * 24 + 24] = part[:, 0:24]
-    message[...] = row_transform(cols[...], h, w)
+    message[...] = row_transform(cols[...], turned)
 
 
 def prepare(one, two, point, w_one, w_two, w_two_back, w_one_back, w_point, w_point_back, base, wide):
@@ -319,12 +316,12 @@
     grad[...] = lines[:, 0:C]
 
 
-def kernel_d(place, received, high, low, inverse, pre, cot, table, scale, values, slopes, strip_one, strip_two, message, left, spec, kept, cols):
+def kernel_d(place, received, matrix, inverse, pre, cot, table, scale, values, slopes, strip_one, strip_two, message, left, spec, kept, cols):
     lev = pl.program_id(0)
 
     @pl.when(lev == 0)
     def _():
-        place_rows(row_expand(received[...], high[...], low[...]), left)
+        place_rows(row_expand(received[...], matrix[...]), left)
         spec[...] = dot(left[...].astype(BF), inverse[...]).reshape(LEV * RL, CO, NC)
         cols[...] = jnp.zeros_like(cols)
 
@@ -345,7 +342,7 @@
         for at in range(LEV):
             for r in range(RL):
                 cols[at * 64 : at * 64 + CO, r * 24 : r * 24 + 24] = kept[at, r * CP : r * CP + CO, 0:24]
-        message[...] = row_transform(cols[...] * scale[...], high[...], low[...])
+        message[...] = row_transform(cols[...] * scale[...], matrix[...])
 
 
 def kernel_out(values, after, out, wide):
@@ -376,12 +373,17 @@
     message[...] = jnp.broadcast_to(total[None], (SP, 32, 128))
 
 
-def kernel_e_zero(slopes, middle, rows, grad_two, taps):
+def kernel_e_zero(slopes, middle, rows, slope, w_two, grad_two, inner, taps):
     left, right = [], []
     for r in range(RL):
         store_taps(taps, r, slopes[0, r].astype(F32))
         left.append(jnp.concatenate([middle[0, r], middle[0, r + 1], middle[0, r + 2], rows[0, r]], axis=0))
         right.append(taps[r])
+    for start in (0, 3):
+        d = dot(w_two[0 : 3 * CP, 0 : 5 * GR], window(taps, start, 5))
+        for t in range(3):
+            value = d[t * CP : (t + 1) * CP] * slope[0, start + t + 2].astype(F32)
+            inner[0, start + t] = value.astype(BF)
     part = dot_nt(jnp.concatenate(left, axis=1), jnp.concatenate(right, axis=1))
 
     @pl.when(pl.program_id(0) == 0)
@@ -393,28 +395,30 @@
         grad_two[...] += part
 
 
-def kernel_e(place, slopes, first, second, rows, f_first, f_second, slope, w_two, modes, grad_two, pre_slope, message, taps, pre_taps, grad_one, sums, packed):
+def kernel_e(place, slopes, first, second, rows, f_first, f_second, slope, w_two, modes, grad_two, inner, outer, message, taps, pre_taps, grad_one, sums, packed):
     index = place[0]
     lev = pl.program_id(0)
     even = index % 2 == 0
     halo = halo_rows(even, first, second)
-    for i, x in enumerate(halo[0:2] + [slopes[0, r].astype(F32) for r in range(RL)] + halo[2:4]):
+    near = [slopes[0, r].astype(F32) for r in (0, 1, RL - 2, RL - 1)]
+    for i, x in enumerate(halo[0:2] + near + halo[2:4]):
         store_taps(taps, i, x)
-    rest = jnp.zeros((CP - CO, NC), F32)
-    for start, count in ((0, 4), (4, 3), (7, 3)):
-        d = dot(w_two[0 : CP * count, 0 : GR * (count + 2)], window(taps, start, count + 2))
-        for t in range(count):
-            i = start + t
-            value = d[t * CP : t * CP + CO] * slope[0, i].astype(F32)[0:CO]
+    for i in range(6):
+        store_taps(pre_taps, i + 1, inner[0, i].astype(F32))
+    for k in range(2):
+        d = dot(w_two[0 : 2 * CP, 0 : 4 * GR], window(taps, 4 * k, 4))
+        for t in range(2):
+            i = RL * k + t
+            value = d[t * CP : (t + 1) * CP] * slope[0, i].astype(F32)
             if i in (0, RL + 1):
                 value = value * jnp.where(index == (0 if i == 0 else SP - 1), 0.0, 1.0).astype(F32)
-            value = jnp.concatenate([value, rest], axis=0)
-            pre_slope[0, i] = value.astype(BF)
-            store_taps(pre_taps, i, value)
+            else:
+                store_taps(pre_taps, i - 1, value)
+            outer[0, 2 * k + t] = value.astype(BF)
     halo = halo_rows(even, f_first, f_second)
     field = [halo[1].astype(BF)] + [rows[0, r] for r in range(RL)] + [halo[2].astype(BF)]
     left = jnp.concatenate([jnp.concatenate(field[r : r + 3], axis=0) for r in range(RL)], axis=1)
-    right = jnp.concatenate([pre_taps[r + 1] for r in range(RL)], axis=1)
+    right = jnp.concatenate([pre_taps[r] for r in range(RL)], axis=1)
     part_one = dot_nt(left, right)
 
     @pl.when(lev == 0)
@@ -436,9 +440,10 @@
         message[...] = packed[...].astype(BF)
 
 
-def kernel_e_two(pre_slope, slopes, w_one, w_point, after, back, taps, wide):
-    for i in range(RL + 2):
-        store_taps(taps, i, pre_slope[0, i].astype(F32))
+def kernel_e_two(inner, outer, slopes, w_one, w_point, after, back, taps, wide):
+    lines = [outer[0, 0], outer[0, 1]] + [inner[0, i] for i in range(6)] + [outer[0, 2], outer[0, 3]]
+    for i, x in enumerate(lines):
+        store_taps(taps, i, x.astype(F32))
     for r in (0, 4):
         d = dot(w_one[...], window(taps, r, 6))
         d = d + dot(w_point[...], slopes[0, r : r + 4].reshape(4 * CP, NC))
@@ -449,13 +454,13 @@
         back[0, :, n : n + 128] = wide[n // 128]
 
 
-def kernel_f(received, high, low, inverse, back, out, point, one, two, left, packed, sums):
+def kernel_f(received, matrix, inverse, back, out, point, one, two, left, packed, sums):
     lev = pl.program_id(0)
 
     @pl.when(lev == 0)
     def _():
         modes = received[...].reshape(SP * 32, 128)
-        r_high, r_low = split(row_expand(modes, high[...], low[...]))
+        r_high, r_low = split(row_expand(modes, matrix[...]))
         r_high, r_low = r_high.astype(F32), r_low.astype(F32)
         rest = jnp.zeros((C, 56), F32)
         for at in range(LEV):
@@ -537,11 +542,11 @@
     natural = shape((LEV, C * RL, NC), BF)
     flat, cols = pltpu.VMEM((LEV * C * RL, 128), F32), pltpu.VMEM((128, 256), F32)
     row_matrix = shape((SP * 32, 256), BF)
-    message, high, low = plain_call(
+    message, matrix = plain_call(
         kernel_a,
         (inputs, table, *map(jnp.asarray, ROWS + ROWS_TURNED), jnp.asarray(MODE_ROW)),
         (),
-        [shape((SP * 32, 128), BF), row_matrix, row_matrix],
+        [shape((SP * 32, 128), BF), row_matrix],
         [flat, cols],
         56,
         "field_modes",
@@ -622,7 +627,6 @@
             pl.BlockSpec(memory_space=pltpu.SMEM),
             whole_spec(SP * 32, 128),
             whole_spec(SP * 32, 256),
-            whole_spec(SP * 32, 256),
             whole_spec(128, NC),
             level_spec(RL, CO, NC),
             level_spec(RL, CP, NC),
@@ -639,20 +643,26 @@
         ],
         compiler_params=params(56),
         name="output_and_slope",
-    )(place, gathered, high, low, jnp.asarray(INVERSE), pre, cot_rows, table, jnp.asarray(SCALE))
+    )(place, gathered, matrix, jnp.asarray(INVERSE), pre, cot_rows, table, jnp.asarray(SCALE))
     s_first, s_second = partners(s_first, s_second)
 
-    grad_two = pl.pallas_call(
+    grad_two, inner = pl.pallas_call(
         kernel_e_zero,
         grid=(LEV,),
-        in_specs=[level_spec(RL, CP, NC), level_spec(RL + 2, CP, NC), level_spec(RL, CP, NC)],
+        in_specs=[
+            level_spec(RL, CP, NC),
+            level_spec(RL + 2, CP, NC),
+            level_spec(RL, CP, NC),
+            level_spec(RL + 2, CP, NC),
+            whole_spec(4 * CP, 6 * GR),
+        ],
+        out_specs=[whole_spec(GR + CP, GR), level_spec(6, CP, NC)],
+        out_shape=[shape((GR + CP, GR), F32), shape((LEV, 6, CP, NC), BF)],
         scratch_shapes=[pltpu.VMEM((RL, GR, NC), BF)],
-        out_specs=whole_spec(GR + CP, GR),
-        out_shape=shape((GR + CP, GR), F32),
         compiler_params=params(56),
-        name="weight_gradients_two",
-    )(slopes, middle, rows)
-    pre_slope, message = pl.pallas_call(
+        name="inner_slopes_and_gradients",
+    )(slopes, middle, rows, slope, w_two_back)
+    outer, message = pl.pallas_call(
         kernel_e,
         grid=(LEV,),
         in_specs=[
@@ -667,25 +677,27 @@
             whole_spec(4 * CP, 6 * GR),
             whole_spec(SP, 32, 128),
             whole_spec(GR + CP, GR),
-        ],
-        out_specs=[level_spec(RL + 2, CP, NC), whole_spec(SP, 32, 128)],
-        out_shape=[shape((LEV, RL + 2, CP, NC), BF), shape((SP, 32, 128), BF)],
+            level_spec(6, CP, NC),
+        ],
+        out_specs=[level_spec(4, CP, NC), whole_spec(SP, 32, 128)],
+        out_shape=[shape((LEV, 4, CP, NC), BF), shape((SP, 32, 128), BF)],
         scratch_shapes=[
-            pltpu.VMEM((RL + 4, GR, NC), BF),
-            pltpu.VMEM((RL + 2, GR, NC), BF),
+            pltpu.VMEM((RL, GR, NC), BF),
+            pltpu.VMEM((RL, GR, NC), BF),
             pltpu.VMEM((GR, GR), F32),
             pltpu.VMEM((SP * SHARE, 128), F32),
             pltpu.VMEM((SP, 32, 128), F32),
         ],
         compiler_params=params(56),
-        name="slope_and_weight_gradients",
-    )(place, slopes, s_first, s_second, rows, f_first, f_second, slope, w_two_back, message.reshape(SP, 32, 128), grad_two)
+        name="outer_slopes_and_gradients",
+    )(place, slopes, s_first, s_second, rows, f_first, f_second, slope, w_two_back, message.reshape(SP, 32, 128), grad_two, inner)
     arrived = exchange(message)
     back = pl.pallas_call(
         kernel_e_two,
         grid=(LEV,),
         in_specs=[
-            level_spec(RL + 2, CP, NC),
+            level_spec(6, CP, NC),
+            level_spec(4, CP, NC),
             level_spec(RL, CP, NC),
             whole_spec(4 * CP, 6 * GR),
             whole_spec(4 * CP, 4 * CP),
@@ -696,7 +708,7 @@
         scratch_shapes=[pltpu.VMEM((RL + 2, GR, NC), BF), pltpu.VMEM((NC // 128, C * RL, 128), F32)],
         compiler_params=params(56),
         name="backward_convolution",
-    )(pre_slope, slopes, w_one_back, w_point_back, message)
+    )(inner, outer, slopes, w_one_back, w_point_back, message)
     (out,) = plain_call(
         kernel_out,
         (values,),
@@ -733,7 +745,6 @@
         in_specs=[
             whole_spec(SP, 32, 128),
             whole_spec(SP * 32, 256),
-            whole_spec(SP * 32, 256),
             whole_spec(128, NC),
             level_spec(C * RL, NC),
         ],
@@ -746,7 +757,7 @@
         ],
         compiler_params=params(56),
         name="field_gradient",
-    )(gathered, high, low, jnp.asarray(BACK), back)
+    )(gathered, matrix, jnp.asarray(BACK), back)
     spec_total = jnp.transpose(spec_grad.reshape(C, QN, 2, C), (2, 0, 3, 1))
     return (
         out.reshape(field.shape),

time: 124 us -> 122 us (0.984)
  blocking collectives: 24.9 us -> 22.9 us
    all_to_all x1, blocking collectives: 24.9 us -> 22.9 us  [exchange(): return lax.all_to_all(x, 'sp', 0, 0, tiled=True)]
    pallas_call x1, Pallas kernels: 4.52 us -> 6.52 us  [local(): pl.pallas_call(kernel_e_zero, grid=(LEV,), in_specs=[level_spec(RL, CP, N...]
    pallas_call x1, Pallas kernels: 9.02 us -> 7.16 us  [local(): pl.pallas_call(kernel_e, grid=(LEV,), in_specs=[pl.BlockSpec(memory_space...]
  transfers between devices with their start and end apart: 10 -> 10, of which waited for: 4 -> 4; matrix products, arithmetic and copies ran while one was open for 0% -> 0% of each run, Pallas kernels for 25% -> 27%
where the time goes in v6:
time: 122 us; the launch traced here: 121 us
  Pallas kernels  55.3 us (45%)
  starting transfers between devices  35.3 us (29%)
  blocking collectives  22.9 us (19%)
  waiting for transfers between devices  4.22 us (3%)
  local copies, waits for them, and re-layouts  3.01 us (2%)
    all_to_all x3, starting transfers between devices, exchange(): return lax.all_to_all(x, 'sp', 0, 0, tiled=True)  24.1 us
    all_to_all x1, blocking collectives, exchange(): return lax.all_to_all(x, 'sp', 0, 0, tiled=True)  22.9 us
    pallas_call x7, Pallas kernels, plain_call(): pl.pallas_call(kernel, in_specs=[pl.BlockSpec(memory_space=pltpu.SMEM)] *...  12.1 us
    pallas_call x1, Pallas kernels, local(): pl.pallas_call(kernel_b, grid=(LEV,), in_specs=[pl.BlockSpec(memory_space...  8.49 us
    ppermute x3, starting transfers between devices, local(): lax.ppermute(sums, 'rep', [(i, i ^ k) for i in range(4)])  7.24 us
    pallas_call x1, Pallas kernels, local(): pl.pallas_call(kernel_e, grid=(LEV,), in_specs=[pl.BlockSpec(memory_space...  7.16 us
    pallas_call x1, Pallas kernels, local(): pl.pallas_call(kernel_d, grid=(LEV,), in_specs=[pl.BlockSpec(memory_space...  6.54 us
    pallas_call x1, Pallas kernels, local(): pl.pallas_call(kernel_e_zero, grid=(LEV,), in_specs=[level_spec(RL, CP, N...  6.52 us
  transfers between devices with their start and end apart: 10, of which 4 were waited for; matrix products, arithmetic and copies ran while one was open for 0% of the time, Pallas kernels for 27%

profile of v6, /device:TPU:1, one launch (start us, length us, event | category | flops | bytes accessed | tf_op | source)
XLA Modules:
  0.0 121.4 jit_solution(5960720178688670624)
XLA Ops:
  0.6 4.3 %field_modes.1 = (bf16[1024,128]{1,0:T(8,128)(2,1)}, bf16[1024,256]{1,0:T(8,128)(2,1)}) custom-call(s32[1]{0:T(128)} %bitcast.place, bf16[576,1024]{1,0:T(8,128)(2,1)} %bitcast.17, bf16[1024,128]{1,0:T(8,128)(2,1)} %constant.22.clone.table, bf16[1024,256]{1,0:T(8,128)(2,1)} %constant.23.clone.high, bf16[1024,256]{1,0:T(8,128)(2,1)} %constant.24.clone.low, ...), custom_call_target="tpu_custom_call" | custom-call | tf_op jit(solution)/shard_map/field_modes/pallas_call | solution.py:523
  5.0 11.5 %all-to-all-start = ((bf16[32,32,128]{2,1,0:T(8,128)(2,1)}), bf16[32,32,128]{2,1,0:T(8,128)(2,1)S(1)}, u32[]{:S(2)}, u32[]{:S(2)}) async-start(bf16[32,32,128]{2,1,0:T(8,128)(2,1)} %bitcast.22), calls=%async_computation | async-start | bytes 524288 | tf_op jit(solution)/shard_map/all_to_all | solution.py:514
  16.4 5.4 %row_layout.1 = (bf16[2,8,48,1024]{3,2,1,0:T(8,128)(2,1)}, bf16[2,80,1024]{2,1,0:T(8,128)(2,1)}, bf16[2,80,1024]{2,1,0:T(8,128)(2,1)}, bf16[2,8,48,1024]{3,2,1,0...) custom-call(s32[1]{0:T(128)} %bitcast.place, ...), custom_call_target="tpu_custom_call" | custom-call | tf_op jit(solution)/shard_map/row_layout/pallas_call | solution.py:558
  21.8 1.3 %collective-permute-start = (bf16[2,80,1024]{2,1,0:T(8,128)(2,1)}, bf16[2,80,1024]{2,1,0:T(8,128)(2,1)S(1)}, u32[]{:S(2)}, u32[]{:S(2)}) collective-permute-start(bf16[2,80,1024]{2,1,0:T(8,128)(2,1)} %get-tuple-element.40), channel_id=1, source_target_pairs={{0,1},{1,0},{2,3},{3,2},{4,5},{5,4},{6,7},{7,6},{8,9},{9,8},{10,11... | collective-permute-start | bytes 983048 | tf_op jit(solution)/shard_map/ppermute | solution.py:510
  23.1 0.7 collective-permute-start.1
  23.8 2.3 %all-to-all-done.received = bf16[32,32,128]{2,1,0:T(8,128)(2,1)S(1)} async-done(((bf16[32,32,128]{2,1,0:T(8,128)(2,1)}), bf16[32,32,128]{2,1,0:T(8,128)(2,1)S(1)}, u32[]{:S(2)}, u32[]{:S(2)}) %all-to-all-start) | async-done | bytes 262176 | tf_op jit(solution)/shard_map/all_to_all | solution.py:514
  26.1 1.4 %mode_mix.1 = (bf16[32,32,128]{2,1,0:T(8,128)(2,1)}, f32[32,128]{1,0:T(8,128)S(1)}) custom-call(bf16[32,32,128]{2,1,0:T(8,128)(2,1)S(1)} %all-to-all-done.received, f32[648,36]{1,0:T(8,128)S(1)} %bitcast.15), custom_call_target="tpu_custom_call" | custom-call | tf_op jit(solution)/shard_map/mode_mix/pallas_call | solution.py:523
  27.5 8.8 %all-to-all-start.1 = ((bf16[32,32,128]{2,1,0:T(8,128)(2,1)}), bf16[32,32,128]{2,1,0:T(8,128)(2,1)S(1)}, u32[]{:S(2)}, u32[]{:S(2)}) async-start(bf16[32,32,128]{2,1,0:T(8,128)(2,1)} %get-tuple-element.37), calls=%async_computation.1 | async-start | bytes 524288 | tf_op jit(solution)/shard_map/all_to_all | solution.py:514
  36.3 0.7 copy-done.1
  37.1 8.5 %two_convolutions.1 = (bf16[2,10,48,1024]{3,2,1,0:T(8,128)(2,1)}, bf16[2,10,48,1024]{3,2,1,0:T(8,128)(2,1)}, f32[2,8,40,1024]{3,2,1,0:T(8,128)}) custom-call(s32[1]{0:T(128)} %bitcast.place, bf16[2,8,48,1024]{3,2,1,0:T(8,128)(2,1)} %get-tuple-element.39.rows, bf16[2,80,1024]{2,1,0:T(8,128)(2,1)} %copy-done.1, bf16[2,80,1024]{2,1,0:T(8,128)(2,1)} %copy-done.2, ...), custom_call_target="tpu_custom_call" | custom-call | tf_op jit(solution)/shard_map/two_convolutions/pallas_call | solution.py:595
  45.6 0.3 all-to-all-done.1
  45.9 0.7 copy-done.3
  46.6 6.5 %output_and_slope.1 = (bf16[2,8,48,1024]{3,2,1,0:T(8,128)(2,1)}, bf16[2,8,48,1024]{3,2,1,0:T(8,128)(2,1)}, bf16[2,80,1024]{2,1,0:T(8,128)(2,1)}, bf16[2,80,1024]{2,1,0:T(8,128)(2,1)}, bf16[1024,128]{1,0:T(8,128)(2,1)}) custom-call(s32[1]{0:T(128)} %bitcast.place, bf16[1024,128]{1,0:T(8,128)(2,1)} %bitcast.21, bf16[1024,256]{1,0:T(8,128)(2,1)} %get-tuple-element.38.matrix, ...), custom_call_target="tpu_custom_call" | custom-call | tf_op jit(solution)/shard_map/output_and_slope/pallas_call | solution.py:623
  53.1 1.0 collective-permute-start.2
  54.2 0.8 collective-permute-start.3
  55.0 6.5 %inner_slopes_and_gradients.1 = (f32[192,144]{1,0:T(8,128)}, bf16[2,6,48,1024]{3,2,1,0:T(8,128)(2,1)}) custom-call(bf16[2,8,48,1024]{3,2,1,0:T(8,128)(2,1)} %get-tuple-element.48.slopes, bf16[2,10,48,1024]{3,2,1,0:T(8,128)(2,1)} %get-tuple-element.54.middle, bf16[2,8,48,1024]{3,2,1,0:T(8,128)(2,1)} %get-tuple-element.39.rows, ...), custom_call_target="tpu_custom_call" | custom-call | tf_op jit(solution)/shard_map/inner_slopes_and_gradients/pallas_call | solution.py:649
  61.6 0.7 copy-done.5
  62.3 0.1 copy-done.6
  62.4 7.2 %outer_slopes_and_gradients.1 = (bf16[2,4,48,1024]{3,2,1,0:T(8,128)(2,1)}, bf16[32,32,128]{2,1,0:T(8,128)(2,1)}) custom-call(s32[1]{0:T(128)} %bitcast.place, bf16[2,8,48,1024]{3,2,1,0:T(8,128)(2,1)} %get-tuple-element.48.slopes, bf16[2,80,1024]{2,1,0:T(8,128)(2,1)} %copy-done.5, bf16[2,80,1024]{2,1,0:T(8,128)(2,1)} %copy-done.6, ...), custom_call_target="tpu_custom_call" | custom-call | tf_op jit(solution)/shard_map/outer_slopes_and_gradients/pallas_call | solution.py:665
  69.5 22.9 %all_to_all.20.received = bf16[32,32,128]{2,1,0:T(8,128)(2,1)S(1)} all-to-all(bf16[32,32,128]{2,1,0:T(8,128)(2,1)} %get-tuple-element.57.after), channel_id=1, replica_groups=mesh['rep'=4,'sp'=32] {'sp'}, dimensions={0} | all-to-all | bytes 524288 | tf_op jit(solution)/shard_map/all_to_all | solution.py:514
  92.5 6.2 %collective-permute-start.6 = (f32[64,128]{1,0:T(8,128)S(1)}, f32[64,128]{1,0:T(8,128)S(1)}, u32[]{:S(2)}, u32[]{:S(2)}) collective-permute-start(f32[64,128]{1,0:T(8,128)S(1)} %own_sums.1.sums.p0), channel_id=1, source_target_pairs={{0,96},{32,64},{64,32},{96,0},{1,97},{33,65},{65,33},{97,1},{2,98}... | collective-permute-start | bytes 98312 | tf_op jit(solution)/shard_map/ppermute | solution.py:724
  98.7 1.1 collective-permute-start.5
  99.8 0.4 mode_mix_back.1.cofield
  100.1 0.1 collective-permute-done.6.p3
  100.3 1.5 %collective-permute-done.5.p2 = f32[64,128]{1,0:T(8,128)S(1)} collective-permute-done((f32[64,128]{1,0:T(8,128)S(1)}, f32[64,128]{1,0:T(8,128)S(1)}, u32[]{:S(2)}, u32[]{:S(2)}) %collective-permute-start.5) | collective-permute-done | bytes 32800 | tf_op jit(solution)/shard_map/ppermute | solution.py:724
  101.8 0.7 gradient_modes.1
  102.6 3.9 %all-to-all-start.3 = ((bf16[32,32,128]{2,1,0:T(8,128)(2,1)}), bf16[32,32,128]{2,1,0:T(8,128)(2,1)S(1)}, u32[]{:S(2)}, u32[]{:S(2)}) async-start(bf16[32,32,128]{2,1,0:T(8,128)(2,1)} %gradient_modes.1), calls=%async_computation.3 | async-start | bytes 524288 | tf_op jit(solution)/shard_map/all_to_all | solution.py:514
  106.4 3.4 %output_layout.1 = bf16[2,288,1024]{2,1,0:T(8,128)(2,1)} custom-call(bf16[2,8,48,1024]{3,2,1,0:T(8,128)(2,1)} %get-tuple-element.47.values, bf16[32,32,128]{2,1,0:T(8,128)(2,1)} %get-tuple-element.57.after), custom_call_target="tpu_custom_call" | custom-call | tf_op jit(solution)/shard_map/output_layout/pallas_call | solution.py:523
  109.8 5.7 %backward_convolution.1.back = f32[2,288,1024]{2,1,0:T(8,128)} custom-call(bf16[2,6,48,1024]{3,2,1,0:T(8,128)(2,1)} %get-tuple-element.56.inner, bf16[2,4,48,1024]{3,2,1,0:T(8,128)(2,1)} %get-tuple-element.59.outer, bf16[2,8,48,1024]{3,2,1,0:T(8,128)(2,1)} %get-tuple-element.48.slopes, bf16[192,864]{1,0:T(8,128)(2,1)} %get-tuple-element.60.w_one, ...), custom_call_target="tpu_custom_call" | custom-call | tf_op jit(solution)/shard_map/backward_convolution/pallas_call | solution.py:695
  115.5 1.8 %spectral_gradient.1 = f32[648,36]{1,0:T(8,128)} custom-call(f32[64,128]{1,0:T(8,128)S(1)} %own_sums.1.sums.p0, f32[64,128]{1,0:T(8,128)S(1)} %collective-permute-done.4.p1, f32[64,128]{1,0:T(8,128)S(1)} %collective-permute-done.5.p2, f32[64,128]{1,0:T(8,128)S(1)} %collective-permute-done.6.p3), custom_call_target="tpu_custom_call" | custom-call | tf_op jit(solution)/shard_map/spectral_gradient/pallas_call | solution.py:523
  117.3 0.7 copy-done.4
  118.0 3.4 %field_gradient.1 = (bf16[2,288,1024]{2,1,0:T(8,128)(2,1)}, f32[36,36]{1,0:T(8,128)}, f32[3,3,36,36]{3,2,1,0:T(8,128)}, f32[3,3,36,36]{3,2,1,0:T(8,128)}) custom-call(bf16[32,32,128]{2,1,0:T(8,128)(2,1)} %copy-done.4, bf16[1024,256]{1,0:T(8,128)(2,1)} %get-tuple-element.38.matrix, bf16[128,1024]{1,0:T(8,128)(2,1)} %constant.30.clone.inverse, ...), custom_call_target="tpu_custom_call" | custom-call | tf_op jit(solution)/shard_map/field_gradient/pallas_call | solution.py:742
  (17 shorter events, 0.2 us)
Async XLA Ops:
  5.0 21.1 %copy-start = (f32[2,36,36,9]{2,0,3,1:T(2,128)S(1)}, f32[2,36,36,9]{2,0,3,1:T(2,128)}, u32[]{:S(2)}) copy-start(f32[2,36,36,9]{2,0,3,1:T(2,128)} %param.17) | copy-start | bytes 279940
  5.0 21.1 %all-to-all-start = ((bf16[32,32,128]{2,1,0:T(8,128)(2,1)}), bf16[32,32,128]{2,1,0:T(8,128)(2,1)S(1)}, u32[]{:S(2)}, u32[]{:S(2)}) async-start(bf16[32,32,128]{2,1,0:T(8,128)(2,1)} %bitcast.22), calls=%async_computation | async-start | bytes 524288 | tf_op jit(solution)/shard_map/all_to_all | solution.py:514
  21.8 14.5 %collective-permute-start = (bf16[2,80,1024]{2,1,0:T(8,128)(2,1)}, bf16[2,80,1024]{2,1,0:T(8,128)(2,1)S(1)}, u32[]{:S(2)}, u32[]{:S(2)}) collective-permute-start(bf16[2,80,1024]{2,1,0:T(8,128)(2,1)} %get-tuple-element.40), channel_id=1, source_target_pairs={{0,1},{1,0},{2,3},{3,2},{4,5},{5,4},{6,7},{7,6},{8,9},{9,8},{10,11... | collective-permute-start | bytes 983048 | tf_op jit(solution)/shard_map/ppermute | solution.py:510
  23.1 13.2 %collective-permute-start.1 = (bf16[2,80,1024]{2,1,0:T(8,128)(2,1)}, bf16[2,80,1024]{2,1,0:T(8,128)(2,1)S(1)}, u32[]{:S(2)}, u32[]{:S(2)}) collective-permute-start(bf16[2,80,1024]{2,1,0:T(8,128)(2,1)} %get-tuple-element.41), channel_id=1, source_target_pairs={{1,2},{3,4},{5,6},{7,8},{9,10},{11,12},{13,14},{15,16},{17,18},{19... | collective-permute-start | bytes 983048 | tf_op jit(solution)/shard_map/ppermute | solution.py:510
  27.5 18.4 %all-to-all-start.1 = ((bf16[32,32,128]{2,1,0:T(8,128)(2,1)}), bf16[32,32,128]{2,1,0:T(8,128)(2,1)S(1)}, u32[]{:S(2)}, u32[]{:S(2)}) async-start(bf16[32,32,128]{2,1,0:T(8,128)(2,1)} %get-tuple-element.37), calls=%async_computation.1 | async-start | bytes 524288 | tf_op jit(solution)/shard_map/all_to_all | solution.py:514
  36.3 0.7 copy-start.1
  36.3 0.8 copy-start.2
  45.9 0.7 copy-start.3
  53.1 8.4 %collective-permute-start.2 = (bf16[2,80,1024]{2,1,0:T(8,128)(2,1)}, bf16[2,80,1024]{2,1,0:T(8,128)(2,1)S(1)}, u32[]{:S(2)}, u32[]{:S(2)}) collective-permute-start(bf16[2,80,1024]{2,1,0:T(8,128)(2,1)} %get-tuple-element.49), channel_id=1, source_target_pairs={{0,1},{1,0},{2,3},{3,2},{4,5},{5,4},{6,7},{7,6},{8,9},{9,8},{10,11... | collective-permute-start | bytes 983048 | tf_op jit(solution)/shard_map/ppermute | solution.py:510
  54.2 7.4 %collective-permute-start.3 = (bf16[2,80,1024]{2,1,0:T(8,128)(2,1)}, bf16[2,80,1024]{2,1,0:T(8,128)(2,1)S(1)}, u32[]{:S(2)}, u32[]{:S(2)}) collective-permute-start(bf16[2,80,1024]{2,1,0:T(8,128)(2,1)} %get-tuple-element.50), channel_id=1, source_target_pairs={{1,2},{3,4},{5,6},{7,8},{9,10},{11,12},{13,14},{15,16},{17,18},{19... | collective-permute-start | bytes 983048 | tf_op jit(solution)/shard_map/ppermute | solution.py:510
  61.6 0.7 copy-start.5
  61.6 0.8 copy-start.6
  92.5 7.8 %collective-permute-start.6 = (f32[64,128]{1,0:T(8,128)S(1)}, f32[64,128]{1,0:T(8,128)S(1)}, u32[]{:S(2)}, u32[]{:S(2)}) collective-permute-start(f32[64,128]{1,0:T(8,128)S(1)} %own_sums.1.sums.p0), channel_id=1, source_target_pairs={{0,96},{32,64},{64,32},{96,0},{1,97},{33,65},{65,33},{97,1},{2,98}... | collective-permute-start | bytes 98312 | tf_op jit(solution)/shard_map/ppermute | solution.py:724
  98.7 3.1 %collective-permute-start.5 = (f32[64,128]{1,0:T(8,128)S(1)}, f32[64,128]{1,0:T(8,128)S(1)}, u32[]{:S(2)}, u32[]{:S(2)}) collective-permute-start(f32[64,128]{1,0:T(8,128)S(1)} %own_sums.1.sums.p0), channel_id=1, source_target_pairs={{0,64},{32,96},{64,0},{96,32},{1,65},{33,97},{65,1},{97,33},{2,66}... | collective-permute-start | bytes 98312 | tf_op jit(solution)/shard_map/ppermute | solution.py:724
  99.8 2.1 %collective-permute-start.4 = (f32[64,128]{1,0:T(8,128)S(1)}, f32[64,128]{1,0:T(8,128)S(1)}, u32[]{:S(2)}, u32[]{:S(2)}) collective-permute-start(f32[64,128]{1,0:T(8,128)S(1)} %own_sums.1.sums.p0), channel_id=1, source_target_pairs={{0,32},{32,0},{64,96},{96,64},{1,33},{33,1},{65,97},{97,65},{2,34}... | collective-permute-start | bytes 98312 | tf_op jit(solution)/shard_map/ppermute | solution.py:724
  102.6 14.7 %all-to-all-start.3 = ((bf16[32,32,128]{2,1,0:T(8,128)(2,1)}), bf16[32,32,128]{2,1,0:T(8,128)(2,1)S(1)}, u32[]{:S(2)}, u32[]{:S(2)}) async-start(bf16[32,32,128]{2,1,0:T(8,128)(2,1)} %gradient_modes.1), calls=%async_computation.3 | async-start | bytes 524288 | tf_op jit(solution)/shard_map/all_to_all | solution.py:514
  117.3 0.7 copy-start.4

commit v7 on v6

--- a/solution.py
+++ b/solution.py
@@ -641,7 +641,7 @@
             pltpu.VMEM((LEV, RL * CP, 128), F32),
             cols,
         ],
-        compiler_params=params(56),
+        compiler_params=params(52),
         name="output_and_slope",
     )(place, gathered, matrix, jnp.asarray(INVERSE), pre, cot_rows, table, jnp.asarray(SCALE))
     s_first, s_second = partners(s_first, s_second)
@@ -755,7 +755,7 @@
             pltpu.VMEM((SP, 32, 128), F32),
             pltpu.VMEM((SP * SHARE, 128), F32),
         ],
-        compiler_params=params(56),
+        compiler_params=params(52),
         name="field_gradient",
     )(gathered, matrix, jnp.asarray(BACK), back)
     spec_total = jnp.transpose(spec_grad.reshape(C, QN, 2, C), (2, 0, 3, 1))

time: 122 us -> 120 us (0.984)
    unnamed x14 -> x22, local copies, waits for them, and re-layouts: 3.01 us -> 2.34 us
  transfers between devices with their start and end apart: 10 -> 10, of which waited for: 4 -> 4; matrix products, arithmetic and copies ran while one was open for 0% -> 0% of each run, Pallas kernels for 27% -> 28%
where the time goes in v7:
time: 120 us
  Pallas kernels  54.6 us (46%)
  starting transfers between devices  35.2 us (29%)
  blocking collectives  22.7 us (19%)
  waiting for transfers between devices  4.19 us (3%)
  local copies, waits for them, and re-layouts  2.34 us (2%)
    all_to_all x3, starting transfers between devices, exchange(): return lax.all_to_all(x, 'sp', 0, 0, tiled=True)  24.1 us
    all_to_all x1, blocking collectives, exchange(): return lax.all_to_all(x, 'sp', 0, 0, tiled=True)  22.7 us
    pallas_call x7, Pallas kernels, plain_call(): pl.pallas_call(kernel, in_specs=[pl.BlockSpec(memory_space=pltpu.SMEM)] *...  12.1 us
    pallas_call x1, Pallas kernels, local(): pl.pallas_call(kernel_b, grid=(LEV,), in_specs=[pl.BlockSpec(memory_space...  8.47 us
    ppermute x3, starting transfers between devices, local(): lax.ppermute(sums, 'rep', [(i, i ^ k) for i in range(4)])  7.19 us
    pallas_call x1, Pallas kernels, local(): pl.pallas_call(kernel_e, grid=(LEV,), in_specs=[pl.BlockSpec(memory_space...  7.13 us
    pallas_call x1, Pallas kernels, local(): pl.pallas_call(kernel_e_zero, grid=(LEV,), in_specs=[level_spec(RL, CP, N...  6.52 us
    pallas_call x1, Pallas kernels, local(): pl.pallas_call(kernel_d, grid=(LEV,), in_specs=[pl.BlockSpec(memory_space...  6.08 us
  transfers between devices with their start and end apart: 10, of which 4 were waited for; matrix products, arithmetic and copies ran while one was open for 0% of the time, Pallas kernels for 28%

profile of v7, /device:TPU:1, one launch (start us, length us, event | category | flops | bytes accessed | tf_op | source)
XLA Modules:
  0.0 119.8 jit_solution(12488406321598177237)
XLA Ops:
  0.6 4.3 %field_modes.1 = (bf16[1024,128]{1,0:T(8,128)(2,1)}, bf16[1024,256]{1,0:T(8,128)(2,1)}) custom-call(s32[1]{0:T(128)} %bitcast.place, bf16[576,1024]{1,0:T(8,128)(2,1)} %bitcast.19, bf16[1024,128]{1,0:T(8,128)(2,1)} %constant.22.clone.table, bf16[1024,256]{1,0:T(8,128)(2,1)} %constant.23.clone.high, bf16[1024,256]{1,0:T(8,128)(2,1)} %constant.24.clone.low, ...), custom_call_target="tpu_custom_call" | custom-call | tf_op jit(solution)/shard_map/field_modes/pallas_call | solution.py:523
  5.0 11.5 %all-to-all-start = ((bf16[32,32,128]{2,1,0:T(8,128)(2,1)}), bf16[32,32,128]{2,1,0:T(8,128)(2,1)S(1)}, u32[]{:S(2)}, u32[]{:S(2)}) async-start(bf16[32,32,128]{2,1,0:T(8,128)(2,1)} %bitcast.23), calls=%async_computation | async-start | bytes 524288 | tf_op jit(solution)/shard_map/all_to_all | solution.py:514
  16.4 5.4 %row_layout.1 = (bf16[2,8,48,1024]{3,2,1,0:T(8,128)(2,1)}, bf16[2,80,1024]{2,1,0:T(8,128)(2,1)}, bf16[2,80,1024]{2,1,0:T(8,128)(2,1)}, bf16[2,8,48,1024]{3,2,1,0...) custom-call(s32[1]{0:T(128)} %bitcast.place, ...), custom_call_target="tpu_custom_call" | custom-call | tf_op jit(solution)/shard_map/row_layout/pallas_call | solution.py:558
  21.8 1.3 %collective-permute-start = (bf16[2,80,1024]{2,1,0:T(8,128)(2,1)}, bf16[2,80,1024]{2,1,0:T(8,128)(2,1)S(1)}, u32[]{:S(2)}, u32[]{:S(2)}) collective-permute-start(bf16[2,80,1024]{2,1,0:T(8,128)(2,1)} %get-tuple-element.40), channel_id=1, source_target_pairs={{0,1},{1,0},{2,3},{3,2},{4,5},{5,4},{6,7},{7,6},{8,9},{9,8},{10,11... | collective-permute-start | bytes 983048 | tf_op jit(solution)/shard_map/ppermute | solution.py:510
  23.1 0.7 collective-permute-start.1
  23.8 2.3 %all-to-all-done.received = bf16[32,32,128]{2,1,0:T(8,128)(2,1)S(1)} async-done(((bf16[32,32,128]{2,1,0:T(8,128)(2,1)}), bf16[32,32,128]{2,1,0:T(8,128)(2,1)S(1)}, u32[]{:S(2)}, u32[]{:S(2)}) %all-to-all-start) | async-done | bytes 262176 | tf_op jit(solution)/shard_map/all_to_all | solution.py:514
  26.1 1.4 %mode_mix.1 = (bf16[32,32,128]{2,1,0:T(8,128)(2,1)}, f32[32,128]{1,0:T(8,128)S(1)}) custom-call(bf16[32,32,128]{2,1,0:T(8,128)(2,1)S(1)} %all-to-all-done.received, f32[648,36]{1,0:T(8,128)S(1)} %bitcast.15), custom_call_target="tpu_custom_call" | custom-call | tf_op jit(solution)/shard_map/mode_mix/pallas_call | solution.py:523
  27.5 8.8 %all-to-all-start.1 = ((bf16[32,32,128]{2,1,0:T(8,128)(2,1)}), bf16[32,32,128]{2,1,0:T(8,128)(2,1)S(1)}, u32[]{:S(2)}, u32[]{:S(2)}) async-start(bf16[32,32,128]{2,1,0:T(8,128)(2,1)} %get-tuple-element.37), calls=%async_computation.1 | async-start | bytes 524288 | tf_op jit(solution)/shard_map/all_to_all | solution.py:514
  36.4 0.7 copy-done.7
  37.1 0.1 copy-done.8
  37.2 8.5 %two_convolutions.1 = (bf16[2,10,48,1024]{3,2,1,0:T(8,128)(2,1)}, bf16[2,10,48,1024]{3,2,1,0:T(8,128)(2,1)}, f32[2,8,40,1024]{3,2,1,0:T(8,128)}) custom-call(s32[1]{0:T(128)} %bitcast.place, bf16[2,8,48,1024]{3,2,1,0:T(8,128)(2,1)} %get-tuple-element.39.rows, bf16[2,80,1024]{2,1,0:T(8,128)(2,1)} %copy-done.7, bf16[2,80,1024]{2,1,0:T(8,128)(2,1)} %copy-done.8, ...), custom_call_target="tpu_custom_call" | custom-call | tf_op jit(solution)/shard_map/two_convolutions/pallas_call | solution.py:595
  45.6 0.2 all-to-all-done.1
  45.9 6.1 %output_and_slope.1 = (bf16[2,8,48,1024]{3,2,1,0:T(8,128)(2,1)}, bf16[2,8,48,1024]{3,2,1,0:T(8,128)(2,1)}, bf16[2,80,1024]{2,1,0:T(8,128)(2,1)S(1)}, bf16[2,80,1...) custom-call(s32[1]{0:T(128)} %bitcast.place, bf16[1024,128]{1,0:T(8,128)(2,1)S(1)} %bitcast.17, ...), custom_call_target="tpu_custom_call" | custom-call | tf_op jit(solution)/shard_map/output_and_slope/pallas_call | solution.py:623
  52.0 0.7 copy-done.4
  52.6 1.0 collective-permute-start.2
  53.7 0.8 collective-permute-start.3
  54.5 6.5 %inner_slopes_and_gradients.1 = (f32[192,144]{1,0:T(8,128)}, bf16[2,6,48,1024]{3,2,1,0:T(8,128)(2,1)}) custom-call(bf16[2,8,48,1024]{3,2,1,0:T(8,128)(2,1)} %get-tuple-element.48.slopes, bf16[2,10,48,1024]{3,2,1,0:T(8,128)(2,1)} %get-tuple-element.54.middle, bf16[2,8,48,1024]{3,2,1,0:T(8,128)(2,1)} %get-tuple-element.39.rows, ...), custom_call_target="tpu_custom_call" | custom-call | tf_op jit(solution)/shard_map/inner_slopes_and_gradients/pallas_call | solution.py:649
  61.1 0.7 copy-done.9
  61.8 0.1 copy-done.10
  61.9 7.1 %outer_slopes_and_gradients.1 = (bf16[2,4,48,1024]{3,2,1,0:T(8,128)(2,1)}, bf16[32,32,128]{2,1,0:T(8,128)(2,1)}) custom-call(s32[1]{0:T(128)} %bitcast.place, bf16[2,8,48,1024]{3,2,1,0:T(8,128)(2,1)} %get-tuple-element.48.slopes, bf16[2,80,1024]{2,1,0:T(8,128)(2,1)} %copy-done.9, bf16[2,80,1024]{2,1,0:T(8,128)(2,1)} %copy-done.10, ...), custom_call_target="tpu_custom_call" | custom-call | tf_op jit(solution)/shard_map/outer_slopes_and_gradients/pallas_call | solution.py:665
  69.0 22.7 %all_to_all.20.received = bf16[32,32,128]{2,1,0:T(8,128)(2,1)S(1)} all-to-all(bf16[32,32,128]{2,1,0:T(8,128)(2,1)} %get-tuple-element.57.after), channel_id=1, replica_groups=mesh['rep'=4,'sp'=32] {'sp'}, dimensions={0} | all-to-all | bytes 524288 | tf_op jit(solution)/shard_map/all_to_all | solution.py:514
  91.8 6.1 %collective-permute-start.6 = (f32[64,128]{1,0:T(8,128)S(1)}, f32[64,128]{1,0:T(8,128)S(1)}, u32[]{:S(2)}, u32[]{:S(2)}) collective-permute-start(f32[64,128]{1,0:T(8,128)S(1)} %own_sums.1.sums.p0), channel_id=1, source_target_pairs={{0,96},{32,64},{64,32},{96,0},{1,97},{33,65},{65,33},{97,1},{2,98}... | collective-permute-start | bytes 98312 | tf_op jit(solution)/shard_map/ppermute | solution.py:724
  97.9 1.1 collective-permute-start.5
  99.0 0.4 mode_mix_back.1.cofield
  99.4 0.1 collective-permute-done.6.p3
  99.5 1.5 %collective-permute-done.5.p2 = f32[64,128]{1,0:T(8,128)S(1)} collective-permute-done((f32[64,128]{1,0:T(8,128)S(1)}, f32[64,128]{1,0:T(8,128)S(1)}, u32[]{:S(2)}, u32[]{:S(2)}) %collective-permute-start.5) | collective-permute-done | bytes 32800 | tf_op jit(solution)/shard_map/ppermute | solution.py:724
  101.1 0.7 gradient_modes.1
  101.8 3.9 %all-to-all-start.3 = ((bf16[32,32,128]{2,1,0:T(8,128)(2,1)}), bf16[32,32,128]{2,1,0:T(8,128)(2,1)S(1)}, u32[]{:S(2)}, u32[]{:S(2)}) async-start(bf16[32,32,128]{2,1,0:T(8,128)(2,1)} %gradient_modes.1), calls=%async_computation.3 | async-start | bytes 524288 | tf_op jit(solution)/shard_map/all_to_all | solution.py:514
  105.7 3.4 %output_layout.1 = bf16[2,288,1024]{2,1,0:T(8,128)(2,1)} custom-call(bf16[2,8,48,1024]{3,2,1,0:T(8,128)(2,1)} %get-tuple-element.47.values, bf16[32,32,128]{2,1,0:T(8,128)(2,1)} %get-tuple-element.57.after), custom_call_target="tpu_custom_call" | custom-call | tf_op jit(solution)/shard_map/output_layout/pallas_call | solution.py:523
  109.0 5.8 %backward_convolution.1.back = f32[2,288,1024]{2,1,0:T(8,128)} custom-call(bf16[2,6,48,1024]{3,2,1,0:T(8,128)(2,1)} %get-tuple-element.56.inner, bf16[2,4,48,1024]{3,2,1,0:T(8,128)(2,1)} %get-tuple-element.59.outer, bf16[2,8,48,1024]{3,2,1,0:T(8,128)(2,1)} %get-tuple-element.48.slopes, bf16[192,864]{1,0:T(8,128)(2,1)} %get-tuple-element.60.w_one, ...), custom_call_target="tpu_custom_call" | custom-call | tf_op jit(solution)/shard_map/backward_convolution/pallas_call | solution.py:695
  114.8 1.8 %spectral_gradient.1 = f32[648,36]{1,0:T(8,128)} custom-call(f32[64,128]{1,0:T(8,128)S(1)} %own_sums.1.sums.p0, f32[64,128]{1,0:T(8,128)S(1)} %collective-permute-done.4.p1, f32[64,128]{1,0:T(8,128)S(1)} %collective-permute-done.5.p2, f32[64,128]{1,0:T(8,128)S(1)} %collective-permute-done.6.p3), custom_call_target="tpu_custom_call" | custom-call | tf_op jit(solution)/shard_map/spectral_gradient/pallas_call | solution.py:523
  116.6 3.2 %field_gradient.1 = (bf16[2,288,1024]{2,1,0:T(8,128)(2,1)}, f32[36,36]{1,0:T(8,128)}, f32[3,3,36,36]{3,2,1,0:T(8,128)}, f32[3,3,36,36]{3,2,1,0:T(8,128)}) custom-call(bf16[32,32,128]{2,1,0:T(8,128)(2,1)S(1)} %all-to-all-done.3.received, bf16[1024,256]{1,0:T(8,128)(2,1)S(1)} %copy-done, bf16[128,1024]{1,0:T(8,128)(2,1)S(1)} %copy-done.5, ...), custom_call_target="tpu_custom_call" | custom-call | tf_op jit(solution)/shard_map/field_gradient/pallas_call | solution.py:742
  (25 shorter events, 0.1 us)
Async XLA Ops:
  5.0 21.1 %copy-start.1 = (f32[2,36,36,9]{2,0,3,1:T(2,128)S(1)}, f32[2,36,36,9]{2,0,3,1:T(2,128)}, u32[]{:S(2)}) copy-start(f32[2,36,36,9]{2,0,3,1:T(2,128)} %param.17) | copy-start | bytes 279940
  5.0 21.1 %all-to-all-start = ((bf16[32,32,128]{2,1,0:T(8,128)(2,1)}), bf16[32,32,128]{2,1,0:T(8,128)(2,1)S(1)}, u32[]{:S(2)}, u32[]{:S(2)}) async-start(bf16[32,32,128]{2,1,0:T(8,128)(2,1)} %bitcast.23), calls=%async_computation | async-start | bytes 524288 | tf_op jit(solution)/shard_map/all_to_all | solution.py:514
  21.8 14.5 %collective-permute-start = (bf16[2,80,1024]{2,1,0:T(8,128)(2,1)}, bf16[2,80,1024]{2,1,0:T(8,128)(2,1)S(1)}, u32[]{:S(2)}, u32[]{:S(2)}) collective-permute-start(bf16[2,80,1024]{2,1,0:T(8,128)(2,1)} %get-tuple-element.40), channel_id=1, source_target_pairs={{0,1},{1,0},{2,3},{3,2},{4,5},{5,4},{6,7},{7,6},{8,9},{9,8},{10,11... | collective-permute-start | bytes 983048 | tf_op jit(solution)/shard_map/ppermute | solution.py:510
  23.1 13.2 %collective-permute-start.1 = (bf16[2,80,1024]{2,1,0:T(8,128)(2,1)}, bf16[2,80,1024]{2,1,0:T(8,128)(2,1)S(1)}, u32[]{:S(2)}, u32[]{:S(2)}) collective-permute-start(bf16[2,80,1024]{2,1,0:T(8,128)(2,1)} %get-tuple-element.41), channel_id=1, source_target_pairs={{1,2},{3,4},{5,6},{7,8},{9,10},{11,12},{13,14},{15,16},{17,18},{19... | collective-permute-start | bytes 983048 | tf_op jit(solution)/shard_map/ppermute | solution.py:510
  27.5 18.4 %all-to-all-start.1 = ((bf16[32,32,128]{2,1,0:T(8,128)(2,1)}), bf16[32,32,128]{2,1,0:T(8,128)(2,1)S(1)}, u32[]{:S(2)}, u32[]{:S(2)}) async-start(bf16[32,32,128]{2,1,0:T(8,128)(2,1)} %get-tuple-element.37), calls=%async_computation.1 | async-start | bytes 524288 | tf_op jit(solution)/shard_map/all_to_all | solution.py:514
  36.3 9.6 %copy-start.2 = (bf16[1024,128]{1,0:T(8,128)(2,1)S(1)}, bf16[1024,128]{1,0:T(8,128)(2,1)}, u32[]{:S(2)}) copy-start(bf16[1024,128]{1,0:T(8,128)(2,1)} %constant.22.clone.table) | copy-start | bytes 786436
  36.3 9.6 %copy-start.3 = (bf16[128,1024]{1,0:T(8,128)(2,1)S(1)}, bf16[128,1024]{1,0:T(8,128)(2,1)}, u32[]{:S(2)}) copy-start(bf16[128,1024]{1,0:T(8,128)(2,1)} %constant.28.clone.inverse) | copy-start | bytes 786436
  36.3 9.6 %copy-start.6 = (f32[1,256]{1,0:T(1,128)S(1)}, f32[1,256]{1,0:T(1,128)}, u32[]{:S(2)}) copy-start(f32[1,256]{1,0:T(1,128)} %constant.29.clone.scale) | copy-start | bytes 3076
  36.3 0.7 copy-start.7
  36.3 0.8 copy-start.8
  52.0 0.7 copy-start.4
  52.6 8.4 %collective-permute-start.2 = (bf16[2,80,1024]{2,1,0:T(8,128)(2,1)S(1)}, bf16[2,80,1024]{2,1,0:T(8,128)(2,1)S(1)}, u32[]{:S(2)}, u32[]{:S(2)}) collective-permute-start(bf16[2,80,1024]{2,1,0:T(8,128)(2,1)S(1)} %get-tuple-element.49), channel_id=1, source_target_pairs={{0,1},{1,0},{2,3},{3,2},{4,5},{5,4},{6,7},{7,6},{8,9},{9,8},{10,11... | collective-permute-start | bytes 983048 | tf_op jit(solution)/shard_map/ppermute | solution.py:510
  53.7 7.4 %collective-permute-start.3 = (bf16[2,80,1024]{2,1,0:T(8,128)(2,1)S(1)}, bf16[2,80,1024]{2,1,0:T(8,128)(2,1)S(1)}, u32[]{:S(2)}, u32[]{:S(2)}) collective-permute-start(bf16[2,80,1024]{2,1,0:T(8,128)(2,1)S(1)} %get-tuple-element.50), channel_id=1, source_target_pairs={{1,2},{3,4},{5,6},{7,8},{9,10},{11,12},{13,14},{15,16},{17,18},{19... | collective-permute-start | bytes 983048 | tf_op jit(solution)/shard_map/ppermute | solution.py:510
  61.1 0.7 copy-start.9
  61.1 0.8 copy-start.10
  91.8 7.7 %collective-permute-start.6 = (f32[64,128]{1,0:T(8,128)S(1)}, f32[64,128]{1,0:T(8,128)S(1)}, u32[]{:S(2)}, u32[]{:S(2)}) collective-permute-start(f32[64,128]{1,0:T(8,128)S(1)} %own_sums.1.sums.p0), channel_id=1, source_target_pairs={{0,96},{32,64},{64,32},{96,0},{1,97},{33,65},{65,33},{97,1},{2,98}... | collective-permute-start | bytes 98312 | tf_op jit(solution)/shard_map/ppermute | solution.py:724
  97.9 3.1 %collective-permute-start.5 = (f32[64,128]{1,0:T(8,128)S(1)}, f32[64,128]{1,0:T(8,128)S(1)}, u32[]{:S(2)}, u32[]{:S(2)}) collective-permute-start(f32[64,128]{1,0:T(8,128)S(1)} %own_sums.1.sums.p0), channel_id=1, source_target_pairs={{0,64},{32,96},{64,0},{96,32},{1,65},{33,97},{65,1},{97,33},{2,66}... | collective-permute-start | bytes 98312 | tf_op jit(solution)/shard_map/ppermute | solution.py:724
  99.0 2.1 %collective-permute-start.4 = (f32[64,128]{1,0:T(8,128)S(1)}, f32[64,128]{1,0:T(8,128)S(1)}, u32[]{:S(2)}, u32[]{:S(2)}) collective-permute-start(f32[64,128]{1,0:T(8,128)S(1)} %own_sums.1.sums.p0), channel_id=1, source_target_pairs={{0,32},{32,0},{64,96},{96,64},{1,33},{33,1},{65,97},{97,65},{2,34}... | collective-permute-start | bytes 98312 | tf_op jit(solution)/shard_map/ppermute | solution.py:724
  101.8 14.8 %all-to-all-start.3 = ((bf16[32,32,128]{2,1,0:T(8,128)(2,1)}), bf16[32,32,128]{2,1,0:T(8,128)(2,1)S(1)}, u32[]{:S(2)}, u32[]{:S(2)}) async-start(bf16[32,32,128]{2,1,0:T(8,128)(2,1)} %gradient_modes.1), calls=%async_computation.3 | async-start | bytes 524288 | tf_op jit(solution)/shard_map/all_to_all | solution.py:514
  109.0 7.6 %copy-start = (bf16[1024,256]{1,0:T(8,128)(2,1)S(1)}, bf16[1024,256]{1,0:T(8,128)(2,1)}, u32[]{:S(2)}) copy-start(bf16[1024,256]{1,0:T(8,128)(2,1)} %get-tuple-element.38.matrix) | copy-start | bytes 1572868
  109.0 7.6 %copy-start.5 = (bf16[128,1024]{1,0:T(8,128)(2,1)S(1)}, bf16[128,1024]{1,0:T(8,128)(2,1)}, u32[]{:S(2)}) copy-start(bf16[128,1024]{1,0:T(8,128)(2,1)} %constant.30.clone.inverse) | copy-start | bytes 786436

commit v8 on v7

--- a/solution.py
+++ b/solution.py
@@ -688,7 +688,7 @@
             pltpu.VMEM((SP * SHARE, 128), F32),
             pltpu.VMEM((SP, 32, 128), F32),
         ],
-        compiler_params=params(56),
+        compiler_params=params(52),
         name="outer_slopes_and_gradients",
     )(place, slopes, s_first, s_second, rows, f_first, f_second, slope, w_two_back, message.reshape(SP, 32, 128), grad_two, inner)
     arrived = exchange(message)

time: 120 us -> 119 us (level)
  no operation moved by 1% of the time
where the time goes in v8:
time: 119 us
  Pallas kernels  54.4 us (46%)
  starting transfers between devices  35.2 us (30%)
  blocking collectives  22.5 us (19%)
  waiting for transfers between devices  4.19 us (4%)
  local copies, waits for them, and re-layouts  1.77 us (1%)
    all_to_all x3, starting transfers between devices, exchange(): return lax.all_to_all(x, 'sp', 0, 0, tiled=True)  24.1 us
    all_to_all x1, blocking collectives, exchange(): return lax.all_to_all(x, 'sp', 0, 0, tiled=True)  22.5 us
    pallas_call x7, Pallas kernels, plain_call(): pl.pallas_call(kernel, in_specs=[pl.BlockSpec(memory_space=pltpu.SMEM)] *...  12 us
    pallas_call x1, Pallas kernels, local(): pl.pallas_call(kernel_b, grid=(LEV,), in_specs=[pl.BlockSpec(memory_space...  8.47 us
    ppermute x3, starting transfers between devices, local(): lax.ppermute(sums, 'rep', [(i, i ^ k) for i in range(4)])  7.18 us
    pallas_call x1, Pallas kernels, local(): pl.pallas_call(kernel_e, grid=(LEV,), in_specs=[pl.BlockSpec(memory_space...  6.89 us
    pallas_call x1, Pallas kernels, local(): pl.pallas_call(kernel_e_zero, grid=(LEV,), in_specs=[level_spec(RL, CP, N...  6.56 us
    pallas_call x1, Pallas kernels, local(): pl.pallas_call(kernel_d, grid=(LEV,), in_specs=[pl.BlockSpec(memory_space...  6.11 us
  transfers between devices with their start and end apart: 10, of which 4 were waited for; matrix products, arithmetic and copies ran while one was open for 0% of the time, Pallas kernels for 28%

profile of v8, /device:TPU:1, one launch (start us, length us, event | category | flops | bytes accessed | tf_op | source)
XLA Modules:
  0.0 118.9 jit_solution(3442180312497707511)
XLA Ops:
  0.6 4.3 %field_modes.1 = (bf16[1024,128]{1,0:T(8,128)(2,1)}, bf16[1024,256]{1,0:T(8,128)(2,1)}) custom-call(s32[1]{0:T(128)} %bitcast.place, bf16[576,1024]{1,0:T(8,128)(2,1)} %bitcast.19, bf16[1024,128]{1,0:T(8,128)(2,1)} %constant.22.clone.table, bf16[1024,256]{1,0:T(8,128)(2,1)} %constant.23.clone.high, bf16[1024,256]{1,0:T(8,128)(2,1)} %constant.24.clone.low, ...), custom_call_target="tpu_custom_call" | custom-call | tf_op jit(solution)/shard_map/field_modes/pallas_call | solution.py:523
  4.9 11.5 %all-to-all-start = ((bf16[32,32,128]{2,1,0:T(8,128)(2,1)}), bf16[32,32,128]{2,1,0:T(8,128)(2,1)S(1)}, u32[]{:S(2)}, u32[]{:S(2)}) async-start(bf16[32,32,128]{2,1,0:T(8,128)(2,1)} %bitcast.23), calls=%async_computation | async-start | bytes 524288 | tf_op jit(solution)/shard_map/all_to_all | solution.py:514
  16.4 5.4 %row_layout.1 = (bf16[2,8,48,1024]{3,2,1,0:T(8,128)(2,1)}, bf16[2,80,1024]{2,1,0:T(8,128)(2,1)}, bf16[2,80,1024]{2,1,0:T(8,128)(2,1)}, bf16[2,8,48,1024]{3,2,1,0...) custom-call(s32[1]{0:T(128)} %bitcast.place, ...), custom_call_target="tpu_custom_call" | custom-call | tf_op jit(solution)/shard_map/row_layout/pallas_call | solution.py:558
  21.8 1.3 %collective-permute-start = (bf16[2,80,1024]{2,1,0:T(8,128)(2,1)}, bf16[2,80,1024]{2,1,0:T(8,128)(2,1)S(1)}, u32[]{:S(2)}, u32[]{:S(2)}) collective-permute-start(bf16[2,80,1024]{2,1,0:T(8,128)(2,1)} %get-tuple-element.40), channel_id=1, source_target_pairs={{0,1},{1,0},{2,3},{3,2},{4,5},{5,4},{6,7},{7,6},{8,9},{9,8},{10,11... | collective-permute-start | bytes 983048 | tf_op jit(solution)/shard_map/ppermute | solution.py:510
  23.1 0.7 collective-permute-start.1
  23.8 2.3 %all-to-all-done.received = bf16[32,32,128]{2,1,0:T(8,128)(2,1)S(1)} async-done(((bf16[32,32,128]{2,1,0:T(8,128)(2,1)}), bf16[32,32,128]{2,1,0:T(8,128)(2,1)S(1)}, u32[]{:S(2)}, u32[]{:S(2)}) %all-to-all-start) | async-done | bytes 262176 | tf_op jit(solution)/shard_map/all_to_all | solution.py:514
  26.0 1.4 %mode_mix.1 = (bf16[32,32,128]{2,1,0:T(8,128)(2,1)}, f32[32,128]{1,0:T(8,128)S(1)}) custom-call(bf16[32,32,128]{2,1,0:T(8,128)(2,1)S(1)} %all-to-all-done.received, f32[648,36]{1,0:T(8,128)S(1)} %bitcast.15), custom_call_target="tpu_custom_call" | custom-call | tf_op jit(solution)/shard_map/mode_mix/pallas_call | solution.py:523
  27.4 8.8 %all-to-all-start.1 = ((bf16[32,32,128]{2,1,0:T(8,128)(2,1)}), bf16[32,32,128]{2,1,0:T(8,128)(2,1)S(1)}, u32[]{:S(2)}, u32[]{:S(2)}) async-start(bf16[32,32,128]{2,1,0:T(8,128)(2,1)} %get-tuple-element.37), calls=%async_computation.1 | async-start | bytes 524288 | tf_op jit(solution)/shard_map/all_to_all | solution.py:514
  36.3 0.0 copy-start.5
  36.3 0.7 copy-done.3
  37.0 0.1 copy-done.10
  37.1 8.5 %two_convolutions.1 = (bf16[2,10,48,1024]{3,2,1,0:T(8,128)(2,1)}, bf16[2,10,48,1024]{3,2,1,0:T(8,128)(2,1)}, f32[2,8,40,1024]{3,2,1,0:T(8,128)}) custom-call(s32[1]{0:T(128)} %bitcast.place, bf16[2,8,48,1024]{3,2,1,0:T(8,128)(2,1)} %get-tuple-element.39.rows, bf16[2,80,1024]{2,1,0:T(8,128)(2,1)} %copy-done.3, bf16[2,80,1024]{2,1,0:T(8,128)(2,1)} %copy-done.10, ...), custom_call_target="tpu_custom_call" | custom-call | tf_op jit(solution)/shard_map/two_convolutions/pallas_call | solution.py:595
  45.6 0.2 all-to-all-done.1
  45.9 6.1 %output_and_slope.1 = (bf16[2,8,48,1024]{3,2,1,0:T(8,128)(2,1)}, bf16[2,8,48,1024]{3,2,1,0:T(8,128)(2,1)}, bf16[2,80,1024]{2,1,0:T(8,128)(2,1)S(1)}, bf16[2,80,1...) custom-call(s32[1]{0:T(128)} %bitcast.place, bf16[1024,128]{1,0:T(8,128)(2,1)S(1)} %bitcast.17, ...), custom_call_target="tpu_custom_call" | custom-call | tf_op jit(solution)/shard_map/output_and_slope/pallas_call | solution.py:623
  52.0 1.0 collective-permute-start.2
  53.0 0.8 collective-permute-start.3
  53.9 6.6 %inner_slopes_and_gradients.1 = (f32[192,144]{1,0:T(8,128)}, bf16[2,6,48,1024]{3,2,1,0:T(8,128)(2,1)}) custom-call(bf16[2,8,48,1024]{3,2,1,0:T(8,128)(2,1)} %get-tuple-element.48.slopes, bf16[2,10,48,1024]{3,2,1,0:T(8,128)(2,1)} %get-tuple-element.54.middle, bf16[2,8,48,1024]{3,2,1,0:T(8,128)(2,1)} %get-tuple-element.39.rows, ...), custom_call_target="tpu_custom_call" | custom-call | tf_op jit(solution)/shard_map/inner_slopes_and_gradients/pallas_call | solution.py:649
  60.5 0.9 copy-done.8
  61.4 6.9 %outer_slopes_and_gradients.1 = (bf16[2,4,48,1024]{3,2,1,0:T(8,128)(2,1)}, bf16[32,32,128]{2,1,0:T(8,128)(2,1)S(1)}) custom-call(s32[1]{0:T(128)} %bitcast.place, bf16[2,8,48,1024]{3,2,1,0:T(8,128)(2,1)} %get-tuple-element.48.slopes, bf16[2,80,1024]{2,1,0:T(8,128)(2,1)S(1)} %collective-permute-done.2.first, ...), custom_call_target="tpu_custom_call" | custom-call | tf_op jit(solution)/shard_map/outer_slopes_and_gradients/pallas_call | solution.py:665
  68.3 22.5 %all_to_all.20.received = bf16[32,32,128]{2,1,0:T(8,128)(2,1)S(1)} all-to-all(bf16[32,32,128]{2,1,0:T(8,128)(2,1)S(1)} %get-tuple-element.57.after), channel_id=1, replica_groups=mesh['rep'=4,'sp'=32] {'sp'}, dimensions={0} | all-to-all | bytes 524288 | tf_op jit(solution)/shard_map/all_to_all | solution.py:514
  90.8 0.1 own_sums.1.sums.p0
  90.9 6.1 %collective-permute-start.6 = (f32[64,128]{1,0:T(8,128)S(1)}, f32[64,128]{1,0:T(8,128)S(1)}, u32[]{:S(2)}, u32[]{:S(2)}) collective-permute-start(f32[64,128]{1,0:T(8,128)S(1)} %own_sums.1.sums.p0), channel_id=1, source_target_pairs={{0,96},{32,64},{64,32},{96,0},{1,97},{33,65},{65,33},{97,1},{2,98}... | collective-permute-start | bytes 98312 | tf_op jit(solution)/shard_map/ppermute | solution.py:724
  97.0 1.1 collective-permute-start.5
  98.0 0.4 mode_mix_back.1.cofield
  98.4 0.1 collective-permute-done.6.p3
  98.6 1.5 %collective-permute-done.5.p2 = f32[64,128]{1,0:T(8,128)S(1)} collective-permute-done((f32[64,128]{1,0:T(8,128)S(1)}, f32[64,128]{1,0:T(8,128)S(1)}, u32[]{:S(2)}, u32[]{:S(2)}) %collective-permute-start.5) | collective-permute-done | bytes 32800 | tf_op jit(solution)/shard_map/ppermute | solution.py:724
  100.1 0.7 gradient_modes.1
  100.9 3.9 %all-to-all-start.3 = ((bf16[32,32,128]{2,1,0:T(8,128)(2,1)}), bf16[32,32,128]{2,1,0:T(8,128)(2,1)S(1)}, u32[]{:S(2)}, u32[]{:S(2)}) async-start(bf16[32,32,128]{2,1,0:T(8,128)(2,1)} %gradient_modes.1), calls=%async_computation.3 | async-start | bytes 524288 | tf_op jit(solution)/shard_map/all_to_all | solution.py:514
  104.7 3.4 %output_layout.1 = bf16[2,288,1024]{2,1,0:T(8,128)(2,1)} custom-call(bf16[2,8,48,1024]{3,2,1,0:T(8,128)(2,1)} %get-tuple-element.47.values, bf16[32,32,128]{2,1,0:T(8,128)(2,1)} %copy-done), custom_call_target="tpu_custom_call" | custom-call | tf_op jit(solution)/shard_map/output_layout/pallas_call | solution.py:523
  108.1 5.8 %backward_convolution.1.back = f32[2,288,1024]{2,1,0:T(8,128)} custom-call(bf16[2,6,48,1024]{3,2,1,0:T(8,128)(2,1)} %get-tuple-element.56.inner, bf16[2,4,48,1024]{3,2,1,0:T(8,128)(2,1)} %get-tuple-element.59.outer, bf16[2,8,48,1024]{3,2,1,0:T(8,128)(2,1)} %get-tuple-element.48.slopes, bf16[192,864]{1,0:T(8,128)(2,1)} %get-tuple-element.60.w_one, ...), custom_call_target="tpu_custom_call" | custom-call | tf_op jit(solution)/shard_map/backward_convolution/pallas_call | solution.py:695
  113.9 1.8 %spectral_gradient.1 = f32[648,36]{1,0:T(8,128)} custom-call(f32[64,128]{1,0:T(8,128)S(1)} %own_sums.1.sums.p0, f32[64,128]{1,0:T(8,128)S(1)} %collective-permute-done.4.p1, f32[64,128]{1,0:T(8,128)S(1)} %collective-permute-done.5.p2, f32[64,128]{1,0:T(8,128)S(1)} %collective-permute-done.6.p3), custom_call_target="tpu_custom_call" | custom-call | tf_op jit(solution)/shard_map/spectral_gradient/pallas_call | solution.py:523
  115.7 3.2 %field_gradient.1 = (bf16[2,288,1024]{2,1,0:T(8,128)(2,1)}, f32[36,36]{1,0:T(8,128)}, f32[3,3,36,36]{3,2,1,0:T(8,128)}, f32[3,3,36,36]{3,2,1,0:T(8,128)}) custom-call(bf16[32,32,128]{2,1,0:T(8,128)(2,1)S(1)} %all-to-all-done.3.received, bf16[1024,256]{1,0:T(8,128)(2,1)S(1)} %copy-done.1, bf16[128,1024]{1,0:T(8,128)(2,1)S(1)} %copy-done.7, ...), custom_call_target="tpu_custom_call" | custom-call | tf_op jit(solution)/shard_map/field_gradient/pallas_call | solution.py:742
  (25 shorter events, 0.1 us)
Async XLA Ops:
  4.9 21.1 %copy-start.2 = (f32[2,36,36,9]{2,0,3,1:T(2,128)S(1)}, f32[2,36,36,9]{2,0,3,1:T(2,128)}, u32[]{:S(2)}) copy-start(f32[2,36,36,9]{2,0,3,1:T(2,128)} %param.17) | copy-start | bytes 279940
  4.9 21.1 %all-to-all-start = ((bf16[32,32,128]{2,1,0:T(8,128)(2,1)}), bf16[32,32,128]{2,1,0:T(8,128)(2,1)S(1)}, u32[]{:S(2)}, u32[]{:S(2)}) async-start(bf16[32,32,128]{2,1,0:T(8,128)(2,1)} %bitcast.23), calls=%async_computation | async-start | bytes 524288 | tf_op jit(solution)/shard_map/all_to_all | solution.py:514
  21.8 14.5 %collective-permute-start = (bf16[2,80,1024]{2,1,0:T(8,128)(2,1)}, bf16[2,80,1024]{2,1,0:T(8,128)(2,1)S(1)}, u32[]{:S(2)}, u32[]{:S(2)}) collective-permute-start(bf16[2,80,1024]{2,1,0:T(8,128)(2,1)} %get-tuple-element.40), channel_id=1, source_target_pairs={{0,1},{1,0},{2,3},{3,2},{4,5},{5,4},{6,7},{7,6},{8,9},{9,8},{10,11... | collective-permute-start | bytes 983048 | tf_op jit(solution)/shard_map/ppermute | solution.py:510
  23.1 13.2 %collective-permute-start.1 = (bf16[2,80,1024]{2,1,0:T(8,128)(2,1)}, bf16[2,80,1024]{2,1,0:T(8,128)(2,1)S(1)}, u32[]{:S(2)}, u32[]{:S(2)}) collective-permute-start(bf16[2,80,1024]{2,1,0:T(8,128)(2,1)} %get-tuple-element.41), channel_id=1, source_target_pairs={{1,2},{3,4},{5,6},{7,8},{9,10},{11,12},{13,14},{15,16},{17,18},{19... | collective-permute-start | bytes 983048 | tf_op jit(solution)/shard_map/ppermute | solution.py:510
  27.4 18.4 %all-to-all-start.1 = ((bf16[32,32,128]{2,1,0:T(8,128)(2,1)}), bf16[32,32,128]{2,1,0:T(8,128)(2,1)S(1)}, u32[]{:S(2)}, u32[]{:S(2)}) async-start(bf16[32,32,128]{2,1,0:T(8,128)(2,1)} %get-tuple-element.37), calls=%async_computation.1 | async-start | bytes 524288 | tf_op jit(solution)/shard_map/all_to_all | solution.py:514
  36.3 9.6 %copy-start.5 = (bf16[1024,128]{1,0:T(8,128)(2,1)S(1)}, bf16[1024,128]{1,0:T(8,128)(2,1)}, u32[]{:S(2)}) copy-start(bf16[1024,128]{1,0:T(8,128)(2,1)} %constant.22.clone.table) | copy-start | bytes 786436
  36.3 9.6 %copy-start.6 = (bf16[128,1024]{1,0:T(8,128)(2,1)S(1)}, bf16[128,1024]{1,0:T(8,128)(2,1)}, u32[]{:S(2)}) copy-start(bf16[128,1024]{1,0:T(8,128)(2,1)} %constant.28.clone.inverse) | copy-start | bytes 786436
  36.3 9.6 %copy-start.9 = (f32[1,256]{1,0:T(1,128)S(1)}, f32[1,256]{1,0:T(1,128)}, u32[]{:S(2)}) copy-start(f32[1,256]{1,0:T(1,128)} %constant.29.clone.scale) | copy-start | bytes 3076
  36.3 0.7 copy-start.3
  36.3 0.8 copy-start.10
  52.0 8.5 %collective-permute-start.2 = (bf16[2,80,1024]{2,1,0:T(8,128)(2,1)S(1)}, bf16[2,80,1024]{2,1,0:T(8,128)(2,1)S(1)}, u32[]{:S(2)}, u32[]{:S(2)}) collective-permute-start(bf16[2,80,1024]{2,1,0:T(8,128)(2,1)S(1)} %get-tuple-element.49), channel_id=1, source_target_pairs={{0,1},{1,0},{2,3},{3,2},{4,5},{5,4},{6,7},{7,6},{8,9},{9,8},{10,11... | collective-permute-start | bytes 983048 | tf_op jit(solution)/shard_map/ppermute | solution.py:510
  53.0 7.4 %collective-permute-start.3 = (bf16[2,80,1024]{2,1,0:T(8,128)(2,1)S(1)}, bf16[2,80,1024]{2,1,0:T(8,128)(2,1)S(1)}, u32[]{:S(2)}, u32[]{:S(2)}) collective-permute-start(bf16[2,80,1024]{2,1,0:T(8,128)(2,1)S(1)} %get-tuple-element.50), channel_id=1, source_target_pairs={{1,2},{3,4},{5,6},{7,8},{9,10},{11,12},{13,14},{15,16},{17,18},{19... | collective-permute-start | bytes 983048 | tf_op jit(solution)/shard_map/ppermute | solution.py:510
  53.9 6.6 %copy-start.4 = (bf16[2,80,1024]{2,1,0:T(8,128)(2,1)S(1)}, bf16[2,80,1024]{2,1,0:T(8,128)(2,1)}, u32[]{:S(2)}) copy-start(bf16[2,80,1024]{2,1,0:T(8,128)(2,1)} %copy-done.3) | copy-start | bytes 983044
  60.4 0.9 copy-start.8
  68.3 36.5 %copy-start = (bf16[32,32,128]{2,1,0:T(8,128)(2,1)}, bf16[32,32,128]{2,1,0:T(8,128)(2,1)S(1)}, u32[]{:S(2)}) copy-start(bf16[32,32,128]{2,1,0:T(8,128)(2,1)S(1)} %get-tuple-element.57.after) | copy-start | bytes 786436
  90.9 7.7 %collective-permute-start.6 = (f32[64,128]{1,0:T(8,128)S(1)}, f32[64,128]{1,0:T(8,128)S(1)}, u32[]{:S(2)}, u32[]{:S(2)}) collective-permute-start(f32[64,128]{1,0:T(8,128)S(1)} %own_sums.1.sums.p0), channel_id=1, source_target_pairs={{0,96},{32,64},{64,32},{96,0},{1,97},{33,65},{65,33},{97,1},{2,98}... | collective-permute-start | bytes 98312 | tf_op jit(solution)/shard_map/ppermute | solution.py:724
  97.0 3.1 %collective-permute-start.5 = (f32[64,128]{1,0:T(8,128)S(1)}, f32[64,128]{1,0:T(8,128)S(1)}, u32[]{:S(2)}, u32[]{:S(2)}) collective-permute-start(f32[64,128]{1,0:T(8,128)S(1)} %own_sums.1.sums.p0), channel_id=1, source_target_pairs={{0,64},{32,96},{64,0},{96,32},{1,65},{33,97},{65,1},{97,33},{2,66}... | collective-permute-start | bytes 98312 | tf_op jit(solution)/shard_map/ppermute | solution.py:724
  98.0 2.1 %collective-permute-start.4 = (f32[64,128]{1,0:T(8,128)S(1)}, f32[64,128]{1,0:T(8,128)S(1)}, u32[]{:S(2)}, u32[]{:S(2)}) collective-permute-start(f32[64,128]{1,0:T(8,128)S(1)} %own_sums.1.sums.p0), channel_id=1, source_target_pairs={{0,32},{32,0},{64,96},{96,64},{1,33},{33,1},{65,97},{97,65},{2,34}... | collective-permute-start | bytes 98312 | tf_op jit(solution)/shard_map/ppermute | solution.py:724
  100.9 14.8 %all-to-all-start.3 = ((bf16[32,32,128]{2,1,0:T(8,128)(2,1)}), bf16[32,32,128]{2,1,0:T(8,128)(2,1)S(1)}, u32[]{:S(2)}, u32[]{:S(2)}) async-start(bf16[32,32,128]{2,1,0:T(8,128)(2,1)} %gradient_modes.1), calls=%async_computation.3 | async-start | bytes 524288 | tf_op jit(solution)/shard_map/all_to_all | solution.py:514
  108.1 7.6 %copy-start.1 = (bf16[1024,256]{1,0:T(8,128)(2,1)S(1)}, bf16[1024,256]{1,0:T(8,128)(2,1)}, u32[]{:S(2)}) copy-start(bf16[1024,256]{1,0:T(8,128)(2,1)} %get-tuple-element.38.matrix) | copy-start | bytes 1572868
  108.1 7.6 %copy-start.7 = (bf16[128,1024]{1,0:T(8,128)(2,1)S(1)}, bf16[128,1024]{1,0:T(8,128)(2,1)}, u32[]{:S(2)}) copy-start(bf16[128,1024]{1,0:T(8,128)(2,1)} %constant.30.clone.inverse) | copy-start | bytes 786436
